TPU v7x, 32 devices: a whole 2x2x4 slice. The times are simulated.
32 devices in a mesh: section: 2 (over core), tm: 4 (over z), item: 4 (over y, x).
Axes of the slice: x: 2, y: 2, z: 4, core: 2. Of those that a mesh axis runs over, the one named last changes fastest.
Arguments:
- sources: bfloat16 [3, 32, 128, 4096], P(None, 'item', 'section', 'tm'), may hold values from -40 to 40
- source_counts: int32 [32], P('item'), may hold values from 2 to 3
- valid_lengths: int32 [32], P('item'), may hold values from 2048 to 4096, as said below
- w_in: bfloat16 [2, 512, 128], P('section'), may hold values from -0.5 to 0.5
- chan: float32 [2, 11, 512], P('section'), may hold values from -3 to 3
- w_out: bfloat16 [2, 256, 512], P('section'), may hold values from -0.25 to 0.25
- b_out: float32 [2, 256], P('section'), may hold values from -2 to 2
- grad_out: bfloat16 [32, 128, 4096], P('item', None, 'tm'), may hold values from -6 to 6
- grad_skip: bfloat16 [32, 128, 4096], P('item', None, 'tm'), may hold values from -6 to 6
Outputs:
- block_out: bfloat16 [2, 32, 128, 4096], P('section', 'item', None, 'tm')
- skip_out: bfloat16 [2, 32, 128, 4096], P('section', 'item', None, 'tm')
- grad_sources: float32 [3, 32, 128, 4096], P(None, 'item', 'section', 'tm')
- grad_w_in: float32 [2, 512, 128], P('section')
- grad_chan: float32 [2, 11, 512], P('section')
- grad_w_out: float32 [2, 256, 512], P('section')
- grad_b_out: float32 [2, 256], P('section')
Inputs may be any that keep to these rules, and one draw needn't show every extreme that they name: `valid_lengths`: in each aligned block of 8 items one item has all 4096 frames valid.
All inputs are finite; a program needn't handle non-finite values.
Results may differ from a plain program's by a relative error of at most 0.0095.
Values may be sent and summed in bfloat16 or wider, within the bound.
A program may use at most 256 MiB of HBM per device.

v0:
```python
import jax
import jax.numpy as jnp
from jax import lax
from jax.sharding import PartitionSpec as P

FIRST_DILATION = 128
MICRO = 4


EPSILON = 1e-05


def padded(cells, sides, width):
    for axis, dim in sides:
        count = lax.axis_size(axis)
        ends = count - 1
        head = lax.slice_in_dim(cells, 0, width, axis=dim)
        tail = lax.slice_in_dim(cells, cells.shape[dim] - width, cells.shape[dim], axis=dim)
        cells = jnp.concatenate(
            [
                lax.ppermute(tail, axis, [(i, (i + 1) % count) for i in range(ends)]),
                cells,
                lax.ppermute(head, axis, [((i + 1) % count, i) for i in range(ends)]),
            ],
            axis=dim,
        )
    return cells


def passed_along(block, axis, distance):
    devices = range(lax.axis_size(axis))
    route = [(i - distance, i) for i in devices if i - distance in devices]
    return lax.ppermute(block, axis, route)


def soft_prelu(values_in, slope_row):
    return jax.nn.softplus(values_in) - slope_row * jax.nn.softplus(-values_in)


def soft_prelu_back(values_in, slope_row, upstream):
    slope_grad = jnp.sum(-upstream * jax.nn.softplus(-values_in), axis=(0, 2))
    return (
        upstream * (jax.nn.sigmoid(values_in) + slope_row * jax.nn.sigmoid(-values_in)),
        slope_grad,
    )


def norm_stats(hidden_act, frame_valid_mask, normalizer_count):
    totals = lax.psum(jnp.sum(hidden_act * frame_valid_mask, axis=(1, 2)), "tm")
    mean_val = totals / normalizer_count
    centered = (hidden_act - mean_val[:, None, None]) * frame_valid_mask
    spread = lax.psum(jnp.sum(centered * centered, axis=(1, 2)), "tm") / normalizer_count
    return (mean_val[:, None, None], lax.rsqrt(spread + EPSILON)[:, None, None])


def norm_forward(hidden_act, frame_valid_mask, normalizer_count, gain_row, offset_row):
    mean_val, inv_scale = norm_stats(hidden_act, frame_valid_mask, normalizer_count)
    normed = (hidden_act - mean_val) * inv_scale
    return (
        (normed * gain_row[None, :, None] + offset_row[None, :, None]) * frame_valid_mask,
        normed,
        inv_scale,
    )


def norm_backward(upstream, normed, inv_scale, frame_valid_mask, normalizer_count, gain_row):
    masked_up = upstream * frame_valid_mask
    gain_grad = jnp.sum(masked_up * normed, axis=(0, 2))
    offset_grad = jnp.sum(masked_up, axis=(0, 2))
    d_normed = masked_up * gain_row[None, :, None]
    first_sum, second_sum = lax.psum(
        (jnp.sum(d_normed, axis=(1, 2)), jnp.sum(d_normed * normed, axis=(1, 2))), "tm"
    )
    d_act = (
        frame_valid_mask
        * inv_scale
        * (
            d_normed
            - (first_sum / normalizer_count)[:, None, None]
            - normed * (second_sum / normalizer_count)[:, None, None]
        )
    )
    return (d_act, gain_grad, offset_grad)


def dilated_parts(padded_input, dilation_rate, frame_count):
    left_kernel_tap = lax.dynamic_slice_in_dim(
        padded_input, FIRST_DILATION - dilation_rate, frame_count, 2
    ).astype(jnp.float32)
    middle_frames = padded_input[:, :, FIRST_DILATION : FIRST_DILATION + frame_count].astype(
        jnp.float32
    )
    right_kernel_tap = lax.dynamic_slice_in_dim(
        padded_input, FIRST_DILATION + dilation_rate, frame_count, 2
    ).astype(jnp.float32)
    return (left_kernel_tap, middle_frames, right_kernel_tap)


def block_forward(
    block_in, frame_valid_mask, normalizer_count, w_first, params, w_last, bias_last, dilation_rate
):
    frame_count = block_in.shape[2]
    bottleneck = block_in.shape[1]
    pre_act = (
        jnp.einsum("hb,ibf->ihf", w_first, block_in, preferred_element_type=jnp.float32)
        + params[0][None, :, None]
    )
    hidden_act = soft_prelu(pre_act, params[1][None, :, None])
    first_block_output, first_normed, first_scale = norm_forward(
        hidden_act, frame_valid_mask, normalizer_count, params[2], params[3]
    )
    padded_input = padded(first_block_output.astype(jnp.bfloat16), (("tm", 2),), FIRST_DILATION)
    left_kernel_tap, middle_frames, right_kernel_tap = dilated_parts(
        padded_input, dilation_rate, frame_count
    )
    conv_out = (
        params[4][None, :, None] * left_kernel_tap
        + params[5][None, :, None] * middle_frames
        + params[6][None, :, None] * right_kernel_tap
        + params[7][None, :, None]
    )
    second_act = soft_prelu(conv_out, params[8][None, :, None])
    second_out, second_normed, second_scale = norm_forward(
        second_act, frame_valid_mask, normalizer_count, params[9], params[10]
    )
    second_low = second_out.astype(jnp.bfloat16)
    projected = (
        jnp.einsum("oh,ihf->iof", w_last, second_low, preferred_element_type=jnp.float32)
        + bias_last[None, :, None]
    )
    kept_vals = (
        pre_act,
        first_normed,
        first_scale,
        left_kernel_tap,
        middle_frames,
        right_kernel_tap,
        conv_out,
        second_normed,
        second_scale,
        second_low,
    )
    return (
        projected[:, :bottleneck] * frame_valid_mask,
        projected[:, bottleneck:] * frame_valid_mask,
        kept_vals,
    )


def block_backward(
    block_in,
    frame_valid_mask,
    normalizer_count,
    w_first,
    params,
    w_last,
    dilation_rate,
    d_next,
    d_skip,
    kept_vals,
):
    (
        pre_act,
        first_normed,
        first_scale,
        left_kernel_tap,
        middle_frames,
        right_kernel_tap,
        conv_out,
        second_normed,
        second_scale,
        second_low,
    ) = kept_vals
    frame_count = block_in.shape[2]
    d_proj = (jnp.concatenate([d_next, d_skip], axis=1) * frame_valid_mask).astype(jnp.bfloat16)
    grad_last = jnp.einsum("iof,ihf->oh", d_proj, second_low, preferred_element_type=jnp.float32)
    grad_bias = jnp.sum(d_proj.astype(jnp.float32), axis=(0, 2))
    d_second = jnp.einsum("oh,iof->ihf", w_last, d_proj, preferred_element_type=jnp.float32)
    d_act_two, gain_two, offset_two = norm_backward(
        d_second, second_normed, second_scale, frame_valid_mask, normalizer_count, params[9]
    )
    d_conv, slope_two = soft_prelu_back(conv_out, params[8][None, :, None], d_act_two)
    grad_conv_lower = d_conv.astype(jnp.bfloat16)
    d_conv_wide = grad_conv_lower.astype(jnp.float32)
    tap_left = jnp.sum(d_conv_wide * left_kernel_tap, axis=(0, 2))
    tap_middle = jnp.sum(d_conv_wide * middle_frames, axis=(0, 2))
    tap_right = jnp.sum(d_conv_wide * right_kernel_tap, axis=(0, 2))
    conv_bias = jnp.sum(d_conv_wide, axis=(0, 2))
    padded_input = padded(grad_conv_lower, (("tm", 2),), FIRST_DILATION)
    grad_left, grad_middle, grad_right = dilated_parts(padded_input, dilation_rate, frame_count)
    d_first = (
        params[4][None, :, None] * grad_right
        + params[5][None, :, None] * grad_middle
        + params[6][None, :, None] * grad_left
    )
    d_act, gain_one, offset_one = norm_backward(
        d_first, first_normed, first_scale, frame_valid_mask, normalizer_count, params[2]
    )
    d_pre, slope_one = soft_prelu_back(pre_act, params[1][None, :, None], d_act)
    d_pre_low = d_pre.astype(jnp.bfloat16)
    grad_first = jnp.einsum("ihf,ibf->hb", d_pre_low, block_in, preferred_element_type=jnp.float32)
    first_bias = jnp.sum(d_pre_low.astype(jnp.float32), axis=(0, 2))
    d_input = d_next + jnp.einsum(
        "hb,ihf->ibf", w_first, d_pre_low, preferred_element_type=jnp.float32
    )
    chan_grad = jnp.stack(
        [
            first_bias,
            slope_one,
            gain_one,
            offset_one,
            tap_left,
            tap_middle,
            tap_right,
            conv_bias,
            slope_two,
            gain_two,
            offset_two,
        ]
    )
    return (d_input, grad_first, chan_grad, grad_last, grad_bias)


def local(sources, source_counts, valid_lengths, w_in, chan, w_out, b_out, grad_out, grad_skip):
    n_sources, per_device, half_width, frame_count = sources.shape
    hidden = w_in.shape[1]
    bottleneck = w_in.shape[2]
    per_micro = per_device // MICRO
    section_num = lax.axis_index("section")
    leading_frames = section_num == 0
    dilation_rate = jnp.where(leading_frames, FIRST_DILATION, 1)
    offset_frames = lax.axis_index("tm") * frame_count
    positions = offset_frames + jnp.arange(frame_count, dtype=jnp.int32)
    masks = (positions[None, :] < valid_lengths[:, None]).astype(jnp.float32)
    chosen = (jnp.arange(n_sources, dtype=jnp.int32)[:, None] < source_counts[None, :]).astype(
        jnp.float32
    )
    mix_half = (
        jnp.sum(sources.astype(jnp.float32) * chosen[:, :, None, None], axis=0) * masks[:, None, :]
    )
    source_mixture = lax.all_gather(mix_half.astype(jnp.bfloat16), "section", axis=1, tiled=True)
    norm_counts = valid_lengths.astype(jnp.float32) * hidden
    w_first = w_in[0]
    params = chan[0]
    w_last = w_out[0]
    bias_last = b_out[0]
    stored_in = jnp.zeros((per_device, bottleneck, frame_count), jnp.bfloat16)
    out_store = jnp.zeros_like(stored_in)
    skip_store = jnp.zeros_like(stored_in)
    carry_out = jnp.zeros((per_micro, bottleneck, frame_count), jnp.bfloat16)
    carry_skip = jnp.zeros_like(carry_out)
    for tick_num in range(MICRO + 1):
        slot_raw = tick_num - section_num
        is_live = (slot_raw >= 0) & (slot_raw < MICRO)
        slot_start = jnp.clip(slot_raw, 0, MICRO - 1) * per_micro
        block_in = jnp.where(
            leading_frames,
            lax.dynamic_slice_in_dim(source_mixture, slot_start, per_micro, 0),
            carry_out,
        )
        frame_valid_mask = lax.dynamic_slice_in_dim(masks, slot_start, per_micro, 0)[:, None, :]
        normalizer_count = lax.dynamic_slice_in_dim(norm_counts, slot_start, per_micro, 0)
        residual, skip_part, unused_kept = block_forward(
            block_in,
            frame_valid_mask,
            normalizer_count,
            w_first,
            params,
            w_last,
            bias_last,
            dilation_rate,
        )
        next_out = (block_in.astype(jnp.float32) + residual).astype(jnp.bfloat16)
        skip_before = jnp.where(leading_frames, 0.0, carry_skip.astype(jnp.float32))
        next_skip = (skip_before + skip_part).astype(jnp.bfloat16)
        stored_in = jnp.where(
            is_live, lax.dynamic_update_slice_in_dim(stored_in, block_in, slot_start, 0), stored_in
        )
        out_store = jnp.where(
            is_live, lax.dynamic_update_slice_in_dim(out_store, next_out, slot_start, 0), out_store
        )
        skip_store = jnp.where(
            is_live,
            lax.dynamic_update_slice_in_dim(skip_store, next_skip, slot_start, 0),
            skip_store,
        )
        if tick_num < MICRO:
            carry_out, carry_skip = passed_along((next_out, next_skip), "section", 1)
    grad_first = jnp.zeros((hidden, bottleneck), jnp.float32)
    grad_chan = jnp.zeros(params.shape, jnp.float32)
    grad_last = jnp.zeros(w_last.shape, jnp.float32)
    grad_bias = jnp.zeros(bias_last.shape, jnp.float32)
    grad_mix = jnp.zeros((per_device, bottleneck, frame_count), jnp.float32)
    carry_grad = jnp.zeros((per_micro, bottleneck, frame_count), jnp.bfloat16)
    for tick_num in range(MICRO + 1):
        slot_raw = MICRO - tick_num - section_num
        is_live = (slot_raw >= 0) & (slot_raw < MICRO)
        live_factor = is_live.astype(jnp.float32)
        slot_start = jnp.clip(slot_raw, 0, MICRO - 1) * per_micro
        block_in = lax.dynamic_slice_in_dim(stored_in, slot_start, per_micro, 0)
        frame_valid_mask = lax.dynamic_slice_in_dim(masks, slot_start, per_micro, 0)[:, None, :]
        normalizer_count = lax.dynamic_slice_in_dim(norm_counts, slot_start, per_micro, 0)
        cot_out = lax.dynamic_slice_in_dim(grad_out, slot_start, per_micro, 0).astype(jnp.float32)
        d_next = jnp.where(leading_frames, carry_grad.astype(jnp.float32), cot_out)
        d_skip = lax.dynamic_slice_in_dim(grad_skip, slot_start, per_micro, 0).astype(jnp.float32)
        unused_res, unused_skip, kept_vals = block_forward(
            block_in,
            frame_valid_mask,
            normalizer_count,
            w_first,
            params,
            w_last,
            bias_last,
            dilation_rate,
        )
        d_input, step_first, step_chan, step_last, step_bias = block_backward(
            block_in,
            frame_valid_mask,
            normalizer_count,
            w_first,
            params,
            w_last,
            dilation_rate,
            d_next,
            d_skip,
            kept_vals,
        )
        step_grads = (
            step_first * live_factor,
            step_chan * live_factor,
            step_last * live_factor,
            step_bias * live_factor,
        )
        summed = lax.psum(
            (step_grads[0], step_grads[1], step_grads[2], step_grads[3]), ("tm", "item")
        )
        grad_first = grad_first + summed[0]
        grad_chan = grad_chan + summed[1]
        grad_last = grad_last + summed[2]
        grad_bias = grad_bias + summed[3]
        grad_mix = jnp.where(
            is_live & leading_frames,
            lax.dynamic_update_slice_in_dim(grad_mix, d_input, slot_start, 0),
            grad_mix,
        )
        if tick_num < MICRO:
            carry_grad = passed_along(d_input.astype(jnp.bfloat16), "section", -1)
    upper_half = passed_along(grad_mix[:, half_width:].astype(jnp.bfloat16), "section", 1).astype(
        jnp.float32
    )
    own_half = jnp.where(leading_frames, grad_mix[:, :half_width], upper_half)
    grad_sources = chosen[:, :, None, None] * (own_half * masks[:, None, :])[None]
    return (
        out_store[None],
        skip_store[None],
        grad_sources,
        grad_first[None],
        grad_chan[None],
        grad_last[None],
        grad_bias[None],
    )


def solution(mesh):
    in_specs = (
        P(None, "item", "section", "tm"),
        P("item"),
        P("item"),
        P("section", None, None),
        P("section", None, None),
        P("section", None, None),
        P("section", None),
        P("item", None, "tm"),
        P("item", None, "tm"),
    )
    out_specs = (
        P("section", "item", None, "tm"),
        P("section", "item", None, "tm"),
        P(None, "item", "section", "tm"),
        P("section", None, None),
        P("section", None, None),
        P("section", None, None),
        P("section", None),
    )
    return jax.shard_map(local, mesh=mesh, in_specs=in_specs, out_specs=out_specs, check_vma=False)
```

profile of v0, /device:TPU:0, one launch (start us, length us, event | category | flops | bytes accessed | tf_op | source)
XLA Modules:
  0.0 1191.2 jit_solution(377082892270332029)
XLA Ops:
  14.9 12.1 %all-gather.2.cloned.1.call-done = bf16[8,128,1024]{2,0,1:T(8,128)(2,1)} async-done(((bf16[8,64,1024]{2,0,1:T(8,128)(2,1)}), bf16[8,128,1024]{2,0,1:T(8,128)(2,1)}) %all-gather.2.cloned.1.call-update) | async-done | bytes 2097168 | tf_op jit(solution)/shard_map/all_gather | solution.py:241
  27.0 8.2 constant_dynamic-slice_fusion.1
  35.2 7.0 multiply_reduce_fusion.65
  42.2 11.9 %psum.560 = f32[2]{0:T(128)S(1)} all-reduce(f32[2]{0:T(128)S(1)} %get-tuple-element.355), channel_id=1, replica_groups=mesh['section'=2,'tm'=4,'item'=4] {'tm'}, use_global_device_ids=true, to_apply=%region_2.3 | all-reduce | flops 2 | bytes 16 | tf_op jit(solution)/shard_map/psum | solution.py:49
  57.5 8.3 psum.561
  84.8 9.8 multiply_reduce_fusion.63
  94.6 8.4 psum.562
  106.3 10.3 psum.563
  128.1 8.3 multiply_reduce_fusion.61
  136.4 8.5 psum.564
  149.0 10.8 psum.565
  173.4 9.8 multiply_reduce_fusion.59
  183.2 8.6 psum.566
  197.2 10.1 psum.567
  217.8 7.9 multiply_reduce_fusion.57
  225.6 8.7 psum.568
  237.8 10.2 psum.569
  262.0 9.8 multiply_reduce_fusion.55
  271.8 8.4 psum.570
  286.7 11.0 psum.571
  309.3 7.6 multiply_reduce_fusion.53
  316.9 8.6 psum.572
  328.9 10.3 psum.573
  353.1 9.8 multiply_reduce_fusion.51
  362.9 8.5 psum.574
  377.0 10.2 psum.575
  402.3 29.3 %multiply_reduce_fusion.21 = (f32[2]{0:T(128)}, f32[2,512,1024]{1,2,0:T(8,128)}, f32[2]{0:T(128)S(1)}, f32[2,512,1024]{1,2,0:T(8,128)}, f32[2]{0:T(128)}, /*inde...) fusion(f32[2,1024]{1,0:T(2,128)S(1)} %get-tuple-element.299, ...), kind=kOutput, calls=%fused_computation.336 | convolution fusion | flops 362807296 | bytes 42643500 | tf_op jit(solution)/shard_map/hb,ibf->ihf/dot_general | solution.py:105
  431.7 8.5 psum.580
  447.7 10.2 psum.581
  480.3 10.3 multiply_reduce_fusion.43
  490.6 12.4 %all-reduce.13 = (f32[2]{0:T(128)}, f32[2]{0:T(128)}) all-reduce(f32[2]{0:T(128)} %get-tuple-element.199, f32[2]{0:T(128)} %get-tuple-element.323), channel_id=1, replica_groups=mesh['section'=2,'tm'=4,'item'=4] {'tm'}, use_global_device_ids=true, to_apply=%region_46.47 | all-reduce | flops 4 | bytes 32 | tf_op jit(solution)/shard_map/psum | solution.py:49
  508.8 8.2 multiply_reduce_fusion.42
  517.0 8.5 all-reduce.12
  545.6 9.9 multiply_reduce_fusion.37
  555.5 11.0 all-reduce.11
  566.7 12.4 %fusion.20 = (f32[512]{0:T(512)S(1)}, f32[512]{0:T(512)S(1)}, f32[512]{0:T(512)S(1)}, f32[512]{0:T(512)S(1)}, f32[512]{0:T(512)S(1)}, /*index=5*/bf16[2,512,1024]{1,2,0:T(8,128)(2,1)S(1)}) fusion(bf16[2,512,1280]{1,2,0:T(8,128)(2,1)S(1)} %pad_maximum_fusion.5, s32[]{:T(128)S(6)} %select_n.498, s32[]{:T(128)S(6)} %select_n.497, f32[512]{0:T(512)S(1)} %bitcast.858, ...), kind=kLoop, calls=%fused_computation.101 | loop fusion | flops 51377664 | bytes 18928648 | tf_op jit(solution)/shard_map/reduce_sum | solution.py:187
  594.3 9.5 all-reduce.10
  604.0 7.7 convert_reduce_fusion.9
  624.7 8.9 multiply_reduce_fusion.31
  642.3 11.2 all-reduce.9
  653.6 12.7 %fusion.26 = (f32[512]{0:T(512)S(1)}, f32[512]{0:T(512)S(1)}, f32[512]{0:T(512)S(1)}, f32[512]{0:T(512)S(1)}, f32[512]{0:T(512)S(1)}, /*index=5*/bf16[2,512,1024]{1,2,0:T(8,128)(2,1)S(1)}) fusion(bf16[2,512,1280]{1,2,0:T(8,128)(2,1)} %copy-done.16, s32[]{:T(128)S(6)} %select_n.498, s32[]{:T(128)S(6)} %select_n.497, f32[512]{0:T(512)S(1)} %bitcast.860, ...), kind=kLoop, calls=%fused_computation.107 | loop fusion | flops 51377664 | bytes 18928648 | tf_op jit(solution)/shard_map/reduce_sum | solution.py:187
  677.5 9.0 multiply_reduce_fusion.14
  686.5 9.1 all-reduce.8
  695.7 7.8 convert_reduce_fusion.8
  719.5 9.0 multiply_reduce_fusion.25
  738.0 11.0 all-reduce.7
  749.1 10.9 fusion.32
  771.8 9.0 multiply_reduce_fusion.11
  780.9 8.8 all-reduce.6
  789.8 7.8 convert_reduce_fusion.7
  814.7 9.0 multiply_reduce_fusion.19
  833.1 11.7 all-reduce.5
  844.9 11.5 fusion.38
  868.3 9.0 multiply_reduce_fusion.8
  877.3 8.9 all-reduce.4
  886.3 7.8 convert_reduce_fusion.6
  910.9 9.0 multiply_reduce_fusion.47
  928.3 11.0 all-reduce.3
  939.4 10.6 fusion.44
  962.0 9.0 multiply_reduce_fusion.5
  971.0 9.9 all-reduce.2
  980.9 8.7 multiply_reduce_fusion.2
  998.8 74.4 %all-reduce = (f32[11,512]{1,0:T(8,128)S(1)}, f32[256]{0:T(256)}) all-reduce(f32[11,512]{1,0:T(8,128)S(1)} %multiply_add_fusion, f32[256]{0:T(256)S(1)} %multiply_add_fusion.1), channel_id=1, replica_groups=mesh['section'=2,'tm'=4,'item'=4] {'tm','item'}, use_global_device_ids=true, to_apply=%region_137.138 | all-reduce | flops 5888 | bytes 47104 | tf_op jit(solution)/shard_map/psum | solution.py:334
  1086.5 94.0 %all-reduce.16.cloned.1.call-done = (f32[512,128]{1,0:T(8,128)}, f32[256,512]{1,0:T(8,128)}) async-done(((f32[512,128]{1,0:T(8,128)}, f32[256,512]{1,0:T(8,128)}), (f32[512,128]{1,0:T(8,128)}, f32[256,512]{1,0:T(8,128)})) %all-reduce.16.cloned.1.call-update) | async-done | bytes 786448 | tf_op jit(solution)/shard_map/psum | solution.py:334
  (768 shorter events, 392.6 us)
Async XLA Ops:
  7.2 109.5 %copy-start = (bf16[1,256,512]{2,1,0:T(8,128)(2,1)S(1)}, bf16[1,256,512]{2,1,0:T(8,128)(2,1)}, u32[]{:S(2)}) copy-start(bf16[1,256,512]{2,1,0:T(8,128)(2,1)} %param.14) | copy-start | bytes 786436
  7.2 19.8 %all-gather.2.cloned.1.call-start = ((), (), s32[]{:S(2)}) async-start(), calls=%async_computation | async-start | bytes 3145728 | tf_op jit(solution)/shard_map/all_gather | solution.py:241
  13.5 1166.9 %all-reduce.16.cloned.1.call-start = ((), (), s32[]{:S(2)}) async-start(), calls=%async_computation.1 | async-start | bytes 1572864 | tf_op jit(solution)/shard_map/psum | solution.py:334
  14.3 39.8 %copy-start.174 = (f32[8]{0:T(128)}, f32[8]{0:T(128)S(1)}, u32[]{:S(2)}) copy-start(f32[8]{0:T(128)S(1)} %convert_multiply_fusion.35) | copy-start | bytes 100
  14.9 27.3 %copy-start.151 = (f32[1,1,512]{2,0,1:T(1,128)}, f32[1,1,512]{2,0,1:T(1,128)S(1)}, u32[]{:S(2)}) copy-start(f32[1,1,512]{2,0,1:T(1,128)S(1)} %get-tuple-element.308) | copy-start | bytes 6148
  14.9 27.3 %copy-start.155 = (f32[1,1,512]{2,0,1:T(1,128)}, f32[1,1,512]{2,0,1:T(1,128)S(1)}, u32[]{:S(2)}) copy-start(f32[1,1,512]{2,0,1:T(1,128)S(1)} %get-tuple-element.307) | copy-start | bytes 6148
  70.3 8.1 collective-permute-start
  74.9 8.6 collective-permute-start.1
  123.5 3.1 collective-permute-start.2
  145.7 61.7 %copy-start.189 = (f32[2]{0:T(128)}, f32[2]{0:T(128)S(1)}, u32[]{:S(2)}) copy-start(f32[2]{0:T(128)S(1)} %get-tuple-element.230) | copy-start | bytes 28
  163.0 6.0 collective-permute-start.3
  164.9 8.3 collective-permute-start.4
  195.1 15.8 %collective-permute-start.14 = (bf16[2,128,1024]{2,1,0:T(8,128)(2,1)}, bf16[2,128,1024]{2,1,0:T(8,128)(2,1)}, u32[]{:S(2)}, u32[]{:S(2)}) collective-permute-start(bf16[2,128,1024]{2,1,0:T(8,128)(2,1)} %get-tuple-element.175), channel_id=1, source_target_pairs={{0,16},{1,17},{2,18},{3,19},{4,20},{5,21},{6,22},{7,23},{8,24},{9,... | collective-permute-start | bytes 1572872 | tf_op jit(solution)/shard_map/ppermute | solution.py:33
  214.3 3.1 collective-permute-start.5
  234.5 45.7 %copy-start.192 = (f32[2]{0:T(128)}, f32[2]{0:T(128)S(1)}, u32[]{:S(2)}) copy-start(f32[2]{0:T(128)S(1)} %get-tuple-element.224) | copy-start | bytes 28
  251.1 6.2 collective-permute-start.6
  253.5 8.3 collective-permute-start.7
  284.5 17.4 %collective-permute-start.15 = (bf16[2,128,1024]{2,1,0:T(8,128)(2,1)}, bf16[2,128,1024]{2,1,0:T(8,128)(2,1)}, u32[]{:S(2)}, u32[]{:S(2)}) collective-permute-start(bf16[2,128,1024]{2,1,0:T(8,128)(2,1)} %get-tuple-element.173), channel_id=1, source_target_pairs={{0,16},{1,17},{2,18},{3,19},{4,20},{5,21},{6,22},{7,23},{8,24},{9,... | collective-permute-start | bytes 1572872 | tf_op jit(solution)/shard_map/ppermute | solution.py:33
  305.1 3.0 collective-permute-start.8
  325.6 45.9 %copy-start.195 = (f32[2]{0:T(128)}, f32[2]{0:T(128)S(1)}, u32[]{:S(2)}) copy-start(f32[2]{0:T(128)S(1)} %get-tuple-element.218) | copy-start | bytes 28
  342.4 6.0 collective-permute-start.9
  344.6 8.3 collective-permute-start.10
  362.9 24.3 %copy-start.161 = (f32[1,1,512]{2,0,1:T(1,128)S(1)}, f32[1,1,512]{2,0,1:T(1,128)}, u32[]{:S(2)}) copy-start(f32[1,1,512]{2,0,1:T(1,128)} %get-tuple-element.300) | copy-start | bytes 6148
  362.9 24.3 %copy-start.219 = (f32[1,1,512]{2,0,1:T(1,128)S(1)}, f32[1,1,512]{2,0,1:T(1,128)}, u32[]{:S(2)}) copy-start(f32[1,1,512]{2,0,1:T(1,128)} %get-tuple-element.310) | copy-start | bytes 6148
  362.9 24.3 %copy-start.237 = (f32[1,256]{1,0:T(1,128)S(1)}, f32[1,256]{1,0:T(1,128)}, u32[]{:S(2)}) copy-start(f32[1,256]{1,0:T(1,128)} %param.15) | copy-start | bytes 3076
  374.8 15.9 %collective-permute-start.16 = (bf16[2,128,1024]{2,1,0:T(8,128)(2,1)}, bf16[2,128,1024]{2,1,0:T(8,128)(2,1)}, u32[]{:S(2)}, u32[]{:S(2)}) collective-permute-start(bf16[2,128,1024]{2,1,0:T(8,128)(2,1)} %get-tuple-element.171), channel_id=1, source_target_pairs={{0,16},{1,17},{2,18},{3,19},{4,20},{5,21},{6,22},{7,23},{8,24},{9,... | collective-permute-start | bytes 1572872 | tf_op jit(solution)/shard_map/ppermute | solution.py:33
  394.0 3.0 collective-permute-start.11
  398.1 110.6 %copy-start.77 = (bf16[2,128,1024]{2,1,0:T(8,128)(2,1)}, bf16[2,128,1024]{2,1,0:T(8,128)(2,1)S(1)}, u32[]{:S(2)}) copy-start(bf16[2,128,1024]{2,1,0:T(8,128)(2,1)S(1)} %get-tuple-element.206) | copy-start | bytes 1572868
  400.5 31.2 %copy-start.38 = (f32[2,1024,512]{2,1,0:T(8,128)}, f32[2,1024,512]{2,1,0:T(8,128)S(1)}, u32[]{:S(2)}) copy-start(f32[2,1024,512]{2,1,0:T(8,128)S(1)} %fusion.296) | copy-start | bytes 12582916
  401.2 30.4 %copy-start.40 = (f32[2,1024,512]{2,1,0:T(8,128)}, f32[2,1024,512]{2,1,0:T(8,128)S(1)}, u32[]{:S(2)}) copy-start(f32[2,1024,512]{2,1,0:T(8,128)S(1)} %fusion.299) | copy-start | bytes 12582916
  402.3 37.9 %copy-start.177 = (f32[8]{0:T(128)S(1)}, f32[8]{0:T(128)}, u32[]{:S(2)}) copy-start(f32[8]{0:T(128)} %copy-done.174) | copy-start | bytes 100
  463.1 15.1 %collective-permute-start.18 = (bf16[2,512,128]{1,2,0:T(8,128)(2,1)}, bf16[2,512,128]{1,2,0:T(8,128)(2,1)S(1)}, u32[]{:S(2)}, u32[]{:S(2)}) collective-permute-start(bf16[2,512,128]{1,2,0:T(8,128)(2,1)} %get-tuple-element.272), channel_id=1, source_target_pairs={{0,4},{4,8},{8,12},{1,5},{5,9},{9,13},{2,6},{6,10},{10,14},{3,7},{... | collective-permute-start | bytes 786440 | tf_op jit(solution)/shard_map/ppermute | solution.py:21
  465.2 13.8 %collective-permute-start.19 = (bf16[2,512,128]{1,2,0:T(8,128)(2,1)}, bf16[2,512,128]{1,2,0:T(8,128)(2,1)}, u32[]{:S(2)}, u32[]{:S(2)}) collective-permute-start(bf16[2,512,128]{1,2,0:T(8,128)(2,1)} %get-tuple-element.273), channel_id=1, source_target_pairs={{4,0},{8,4},{12,8},{5,1},{9,5},{13,9},{6,2},{10,6},{14,10},{7,3},{... | collective-permute-start | bytes 786440 | tf_op jit(solution)/shard_map/ppermute | solution.py:23
  469.4 608.2 %collective-permute-start.17 = (bf16[2,128,1024]{2,1,0:T(8,128)(2,1)}, bf16[2,128,1024]{2,1,0:T(8,128)(2,1)}, u32[]{:S(2)}, u32[]{:S(2)}) collective-permute-start(bf16[2,128,1024]{2,1,0:T(8,128)(2,1)} %get-tuple-element.169), channel_id=1, source_target_pairs={{0,16},{1,17},{2,18},{3,19},{4,20},{5,21},{6,22},{7,23},{8,24},{9,... | collective-permute-start | bytes 1572872 | tf_op jit(solution)/shard_map/ppermute | solution.py:33
  527.3 39.4 %copy-start.182 = (f32[2]{0:T(128)}, f32[2]{0:T(128)S(1)}, u32[]{:S(2)}) copy-start(f32[2]{0:T(128)S(1)} %get-tuple-element.354) | copy-start | bytes 28
  531.1 11.1 collective-permute-start.23
  535.0 8.9 collective-permute-start.24
  579.1 5.5 collective-permute-start.20
  580.7 8.3 collective-permute-start.21
  611.8 12.7 %collective-permute-start.28 = (bf16[2,512,128]{1,2,0:T(8,128)(2,1)S(1)}, bf16[2,512,128]{1,2,0:T(8,128)(2,1)S(1)}, u32[]{:S(2)}, u32[]{:S(2)}) collective-permute-start(bf16[2,512,128]{1,2,0:T(8,128)(2,1)S(1)} %get-tuple-element.266), channel_id=1, source_target_pairs={{0,4},{4,8},{8,12},{1,5},{5,9},{9,13},{2,6},{6,10},{10,14},{3,7},{... | collective-permute-start | bytes 786440 | tf_op jit(solution)/shard_map/ppermute | solution.py:21
  615.1 9.4 collective-permute-start.29
  620.7 13.0 %collective-permute-start.22 = (bf16[2,128,1024]{2,1,0:T(8,128)(2,1)S(1)}, bf16[2,128,1024]{2,1,0:T(8,128)(2,1)S(1)}, u32[]{:S(2)}, u32[]{:S(2)}) collective-permute-start(bf16[2,128,1024]{2,1,0:T(8,128)(2,1)S(1)} %get-tuple-element.294), channel_id=1, source_target_pairs={{16,0},{17,1},{18,2},{19,3},{20,4},{21,5},{22,6},{23,7},{24,8},{25... | collective-permute-start | bytes 1572872 | tf_op jit(solution)/shard_map/ppermute | solution.py:33
  653.6 82.4 %copy-start.208 = (f32[2]{0:T(128)}, f32[2]{0:T(128)S(1)}, u32[]{:S(2)}) copy-start(f32[2]{0:T(128)S(1)} %div.286) | copy-start | bytes 28
  666.4 6.8 collective-permute-start.25
  668.0 9.3 collective-permute-start.26
  705.7 12.5 %collective-permute-start.33 = (bf16[2,512,128]{1,2,0:T(8,128)(2,1)}, bf16[2,512,128]{1,2,0:T(8,128)(2,1)}, u32[]{:S(2)}, u32[]{:S(2)}) collective-permute-start(bf16[2,512,128]{1,2,0:T(8,128)(2,1)} %get-tuple-element.262), channel_id=1, source_target_pairs={{0,4},{4,8},{8,12},{1,5},{5,9},{9,13},{2,6},{6,10},{10,14},{3,7},{... | collective-permute-start | bytes 786440 | tf_op jit(solution)/shard_map/ppermute | solution.py:21
  709.5 8.7 collective-permute-start.34
  714.1 14.5 %collective-permute-start.27 = (bf16[2,128,1024]{2,1,0:T(8,128)(2,1)}, bf16[2,128,1024]{2,1,0:T(8,128)(2,1)}, u32[]{:S(2)}, u32[]{:S(2)}) collective-permute-start(bf16[2,128,1024]{2,1,0:T(8,128)(2,1)} %get-tuple-element.292), channel_id=1, source_target_pairs={{16,0},{17,1},{18,2},{19,3},{20,4},{21,5},{22,6},{23,7},{24,8},{25... | collective-permute-start | bytes 1572872 | tf_op jit(solution)/shard_map/ppermute | solution.py:33
  760.1 7.4 collective-permute-start.30
  761.4 10.2 collective-permute-start.31
  789.7 41.3 %copy-start.216 = (f32[2]{0:T(128)}, f32[2]{0:T(128)S(1)}, u32[]{:S(2)}) copy-start(f32[2]{0:T(128)S(1)} %add_rsqrt_fusion.2) | copy-start | bytes 28
  799.7 12.4 %collective-permute-start.38 = (bf16[2,512,128]{1,2,0:T(8,128)(2,1)}, bf16[2,512,128]{1,2,0:T(8,128)(2,1)S(1)}, u32[]{:S(2)}, u32[]{:S(2)}) collective-permute-start(bf16[2,512,128]{1,2,0:T(8,128)(2,1)} %get-tuple-element.258), channel_id=1, source_target_pairs={{0,4},{4,8},{8,12},{1,5},{5,9},{9,13},{2,6},{6,10},{10,14},{3,7},{... | collective-permute-start | bytes 786440 | tf_op jit(solution)/shard_map/ppermute | solution.py:21
  803.1 9.7 collective-permute-start.39
  807.6 16.1 %collective-permute-start.32 = (bf16[2,128,1024]{2,1,0:T(8,128)(2,1)}, bf16[2,128,1024]{2,1,0:T(8,128)(2,1)}, u32[]{:S(2)}, u32[]{:S(2)}) collective-permute-start(bf16[2,128,1024]{2,1,0:T(8,128)(2,1)} %get-tuple-element.290), channel_id=1, source_target_pairs={{16,0},{17,1},{18,2},{19,3},{20,4},{21,5},{22,6},{23,7},{24,8},{25... | collective-permute-start | bytes 1572872 | tf_op jit(solution)/shard_map/ppermute | solution.py:33
  856.5 7.4 collective-permute-start.35
  857.8 10.2 collective-permute-start.36
  896.2 13.5 %collective-permute-start.12 = (bf16[2,512,128]{1,2,0:T(8,128)(2,1)}, bf16[2,512,128]{1,2,0:T(8,128)(2,1)}, u32[]{:S(2)}, u32[]{:S(2)}) collective-permute-start(bf16[2,512,128]{1,2,0:T(8,128)(2,1)} %get-tuple-element.254), channel_id=1, source_target_pairs={{0,4},{4,8},{8,12},{1,5},{5,9},{9,13},{2,6},{6,10},{10,14},{3,7},{... | collective-permute-start | bytes 786440 | tf_op jit(solution)/shard_map/ppermute | solution.py:21
  900.3 9.4 collective-permute-start.13
  904.8 15.1 %collective-permute-start.37 = (bf16[2,128,1024]{2,1,0:T(8,128)(2,1)}, bf16[2,128,1024]{2,1,0:T(8,128)(2,1)}, u32[]{:S(2)}, u32[]{:S(2)}) collective-permute-start(bf16[2,128,1024]{2,1,0:T(8,128)(2,1)} %get-tuple-element.288), channel_id=1, source_target_pairs={{16,0},{17,1},{18,2},{19,3},{20,4},{21,5},{22,6},{23,7},{24,8},{25... | collective-permute-start | bytes 1572872 | tf_op jit(solution)/shard_map/ppermute | solution.py:33
  950.1 7.5 collective-permute-start.40
  951.6 10.2 collective-permute-start.41
  992.1 81.7 %copy-start.229 = (f32[2]{0:T(128)S(1)}, f32[2]{0:T(128)}, u32[]{:S(2)}) copy-start(f32[2]{0:T(128)} %copy-done.228) | copy-start | bytes 28
  992.1 81.8 %copy-start.238 = (f32[1,256]{1,0:T(1,128)S(1)}, f32[1,256]{1,0:T(1,128)}, u32[]{:S(2)}) copy-start(f32[1,256]{1,0:T(1,128)} %param.15) | copy-start | bytes 3076
  997.2 83.3 %collective-permute-start.42 = (bf16[8,64,1024]{2,1,0:T(8,128)(2,1)S(1)}, bf16[8,64,1024]{2,1,0:T(8,128)(2,1)S(1)}, u32[]{:S(2)}, u32[]{:S(2)}) collective-permute-start(bf16[8,64,1024]{2,1,0:T(8,128)(2,1)S(1)} %slice.464), channel_id=1, source_target_pairs={{0,16},{1,17},{2,18},{3,19},{4,20},{5,21},{6,22},{7,23},{8,24},{9,... | collective-permute-start | bytes 3145736 | tf_op jit(solution)/shard_map/ppermute | solution.py:33
  (224 other events, 2101.2 us)
Sparse Core Ops, SparseCore 0:
  13.7 13.2 all-gather.1
  1074.0 106.4 all-reduce.15
where the time goes:
time: 1200 us; the launch traced here: 1190 us
  blocking collectives  369 us (31%)
  other arithmetic  356 us (30%)
  waiting for transfers between devices  164 us (14%)
  matrix products  148 us (12%)
  starting transfers between devices  82.6 us (7%)
  local copies, waits for them, and re-layouts  53.4 us (4%)
  between operations  18 us (2%)
    psum x12, blocking collectives, norm_stats(): lax.psum(jnp.sum(centered * centered, axis=(1, 2)), 'tm') / normalizer_count  119 us
    psum x11, blocking collectives, norm_stats(): totals = lax.psum(jnp.sum(hidden_act * frame_valid_mask, axis=(1, 2)), 'tm')  104 us
    reduce_sum x10, other arithmetic, norm_stats(): totals = lax.psum(jnp.sum(hidden_act * frame_valid_mask, axis=(1, 2)), 'tm')  95.3 us
    psum x1, waiting for transfers between devices, local(): lax.psum((step_grads[0], step_grads[1], step_grads[2], step_grads[3]), ('...  94 us
    psum x1, blocking collectives, local(): lax.psum((step_grads[0], step_grads[1], step_grads[2], step_grads[3]), ('...  74.4 us
    psum x7, blocking collectives, norm_backward(): lax.psum((jnp.sum(d_normed, axis=(1, 2)), jnp.sum(d_normed * normed, axis...  72.5 us
    dot_general x10, matrix products, block_forward(): jnp.einsum('hb,ibf->ihf', w_first, block_in, preferred_element_type=jnp.f...  71.2 us
    reduce_sum x5, other arithmetic, block_backward(): tap_right = jnp.sum(d_conv_wide * right_kernel_tap, axis=(0, 2))  58.1 us
  transfers between devices with their start and end apart: 45, of which 23 were waited for; matrix products, arithmetic and copies ran while one was open for 29% of the time, Pallas kernels for 0%

commit v1 on v0

v1 whole, which is shorter than its diff:
```python
import functools
import math

import jax
import jax.numpy as jnp
from jax import lax
from jax.experimental import pallas as pl
from jax.experimental.pallas import tpu as pltpu
from jax.sharding import PartitionSpec as P

DILATION = 128
LANES = 128
ROWS = 16
EPSILON = 1e-05
LN2 = math.log(2.0)
LOG2E = 1.0 / LN2
F32 = jnp.float32
BF16 = jnp.bfloat16
MESH = pl.DeviceIdType.MESH
NT = (((1,), (1,)), ((), ()))
NN = (((1,), (0,)), ((), ()))


def dot(a, b, dims=NN, precision=None):
    return lax.dot_general(a, b, dims, precision=precision, preferred_element_type=F32)


def remote(src, dst, send, recv, device):
    return pltpu.make_async_remote_copy(
        src_ref=src, dst_ref=dst, send_sem=send, recv_sem=recv, device_id=device, device_id_type=MESH
    )


def wide(v, width):
    return jnp.concatenate([v] * (width // LANES), axis=1)


def tall(v, rows):
    return jnp.concatenate([v] * (rows // v.shape[0]), axis=0)


def fold(v):
    parts = [v[:, at : at + LANES] for at in range(0, v.shape[1], LANES)]
    while len(parts) > 1:
        parts = [a + b for a, b in zip(parts[::2], parts[1::2])] + parts[len(parts) & ~1 :]
    return parts[0]


def fold_rows(v):
    parts = [v[at : at + 8] for at in range(0, v.shape[0], 8)]
    while len(parts) > 1:
        parts = [a + b for a, b in zip(parts[::2], parts[1::2])] + parts[len(parts) & ~1 :]
    return parts[0]


def column(table, j):
    return jnp.broadcast_to(table[:, j : j + 1], (table.shape[0], LANES))


def rows_at(t, count):
    return pl.ds(pl.multiple_of(t * count, count), count)


def kernel(
    dims,
    mix_h, gout_h, gskip_h, mask_ref, edge_mask_ref, invn_ref,
    wpre_h, wout_h, wg_h, win_h, chan_h, col_h,
    block_h, skip_h, gmix_h, gwi_h, gwo_h, gch_h, gb_h,
    x0, x1, skip0, out1, skip1, act1_0, act1_1, soft1, act2, soft2, buf, wide_s, dpre, dp, gacc,
    wpre, wout, wg, win, chan, col,
    gwi, gwo, gch, gb, rwi, rwo, rch, rb,
    stat, back, st_src, st_buf,
    edge_src, edge_in, x_edge, dp_edge, first_edge, act_edge, soft_edge, conv_edge,
    sem_w, sem_x, sem_xr, sem_g, sem_es, sem_er, sem_ss, sem_sr, sem_hs, sem_hr, sem_o, sem_or, sem_m, sem_mr,
    sem_k, sem_kr, sem_f,
):
    n_tm, NI, H, B, F = dims
    R = ROWS
    W = F + 2 * DILATION
    MID = slice(DILATION, DILATION + F)
    half = B // 2
    s = lax.axis_index("section")
    t = lax.axis_index("tm")
    o = 1 - s
    left = t - 1
    right = t + 1
    last = n_tm - 1
    first_item = s * NI
    lane = lax.broadcasted_iota(jnp.int32, (R, LANES), 1)
    lane8 = lax.broadcasted_iota(jnp.int32, (8, LANES), 1)

    edge_in[...] = jnp.zeros(edge_in.shape, BF16)

    barrier = pltpu.get_barrier_semaphore()
    pl.semaphore_signal(barrier, inc=1, device_id={"section": o}, device_id_type=MESH)

    def greet(d, c):
        to = lax.rem(t + d, n_tm)
        pl.semaphore_signal(barrier, inc=1, device_id={"tm": to}, device_id_type=MESH)
        pl.semaphore_signal(barrier, inc=1, device_id={"section": o, "tm": to}, device_id_type=MESH)
        return c

    lax.fori_loop(1, n_tm, greet, 0)
    pl.semaphore_wait(barrier, 2 * n_tm - 1)

    own_rows = pl.ds(pl.multiple_of(s * half, half), half)
    other_rows = pl.ds(pl.multiple_of(o * half, half), half)
    items_of = lambda core: pl.ds(core * NI, NI)
    centre = pl.ds(DILATION, F)
    head, tail = pl.ds(0, DILATION), pl.ds(F + DILATION, DILATION)

    main_local = pltpu.make_async_copy(mix_h.at[items_of(s)], x0.at[:, own_rows, centre], sem_x.at[0])
    main_send = remote(
        mix_h.at[items_of(o)], x0.at[:, own_rows, centre], sem_x.at[1], sem_xr.at[0], {"section": o}
    )
    main_recv = remote(
        mix_h.at[items_of(o)], x0.at[:, other_rows, centre], sem_x.at[1], sem_xr.at[0], {"section": o}
    )

    def halo_send(side, core):
        edge = pl.ds(0, DILATION) if side == 0 else pl.ds(F - DILATION, DILATION)
        place = tail if side == 0 else head
        return remote(
            mix_h.at[items_of(core), :, edge],
            x0.at[:, own_rows, place],
            sem_x.at[2 + 2 * side + core],
            sem_xr.at[1 + 2 * side + s],
            {"section": core, "tm": left if side == 0 else right},
        )

    def halo_recv(side, core):
        place = tail if side == 0 else head
        rows = pl.ds(core * half, half)
        return remote(
            x0.at[:, rows, place], x0.at[:, rows, place], sem_x.at[0], sem_xr.at[1 + 2 * side + core], {"section": o}
        )

    main_send.start()
    main_local.start()

    @pl.when(t > 0)
    def _():
        for core in (0, 1):
            halo_send(0, core).start()

    @pl.when(t < last)
    def _():
        for core in (0, 1):
            halo_send(1, core).start()

    weights = ((wpre_h, wpre), (wout_h, wout), (wg_h, wg), (win_h, win), (chan_h, chan), (col_h, col))

    def weight_copies(j):
        src, dst = weights[j]
        return (
            pltpu.make_async_copy(src, dst.at[s], sem_w.at[j, 0]),
            remote(src, dst.at[s], sem_w.at[j, 1], sem_w.at[j, 2], {"section": o}),
            remote(src, dst.at[o], sem_w.at[j, 1], sem_w.at[j, 2], {"section": o}),
        )

    for j in range(len(weights)):
        local, send, _ = weight_copies(j)
        send.start()
        local.start()
    load_out = pltpu.make_async_copy(gout_h.at[items_of(s)], dp.at[:, pl.ds(0, B)], sem_g.at[0])
    load_skip = pltpu.make_async_copy(gskip_h.at[items_of(s)], dp.at[:, pl.ds(B, B)], sem_g.at[1])
    load_out.start()
    load_skip.start()

    @pl.when(t == 0)
    def _():
        x0[:, :, 0:DILATION] = jnp.zeros((NI, B, DILATION), BF16)

    @pl.when(t == last)
    def _():
        x0[:, :, F + DILATION : W] = jnp.zeros((NI, B, DILATION), BF16)

    for j in range(2):
        gwi[j] = jnp.zeros((H, B), F32)
        gwo[j] = jnp.zeros((H, 2 * B), F32)
        gb[j] = jnp.zeros((8, 2 * B), F32)

    def stat_copy(ph, i, d, to):
        p = ph % 2
        return remote(
            st_src.at[p, i], st_buf.at[p, i, d - 1], sem_ss.at[p, i, d - 1], sem_sr.at[p, i, d - 1], {"tm": to}
        )

    def send_stats(ph, i, a, b):
        rows = [jnp.sum(a, axis=0, keepdims=True), jnp.sum(b, axis=0, keepdims=True)]
        st_src[ph % 2, i] = jnp.concatenate(rows + [jnp.zeros((6, LANES), F32)], axis=0)

        def one(d, c):
            stat_copy(ph, i, d, lax.rem(t + d, n_tm)).start()
            return c

        lax.fori_loop(1, n_tm, one, 0)

    def recv_stats(ph, i):
        def one(d, total):
            copy = stat_copy(ph, i, d, lax.rem(t + d, n_tm))
            copy.wait_send()
            copy.wait_recv()
            return total + st_buf[ph % 2, i, d - 1]

        total = lax.fori_loop(1, n_tm, one, st_src[ph % 2, i])
        sums = jnp.sum(total, axis=1, keepdims=True)
        return (
            jnp.broadcast_to(sums[0:1], (8, LANES)),
            jnp.broadcast_to(sums[1:2], (8, LANES)),
        )

    def finish_norm(ph, slot, i):
        a, b = recv_stats(ph, i)
        inv_n = invn_ref[i]
        mean = a * inv_n
        spread = jnp.maximum(b * inv_n - mean * mean, 0.0)
        stat[slot, i, 0] = mean
        stat[slot, i, 1] = lax.rsqrt(spread + EPSILON / (LN2 * LN2))

    def finish_back(ph, slot, i):
        a, b = recv_stats(ph, i)
        inv_n = invn_ref[i]
        mean, inv = stat[slot, i, 0], stat[slot, i, 1]
        q = b * inv_n * inv
        back[i, 0] = (mean * q - a * inv_n) * (inv * LOG2E)
        back[i, 1] = -q * (inv * LOG2E)

    def lanes_of(ref, j):
        out = ref[0, j]
        for i in range(1, NI):
            out = jnp.where(lane8 >= 32 * i, ref[i, j], out)
        return out

    def per_item(body):
        lax.fori_loop(0, NI, lambda i, c: (body(i), c)[1], 0)

    def per_tile(body, count=H, rows=R, init=0):
        return lax.fori_loop(0, count // rows, lambda j, c: body(rows_at(j, rows), c), init)

    def mask_row(i, rows, at=DILATION, width=F):
        return tall(mask_ref[i, :, at : at + width], rows)

    zero8 = jnp.zeros((8, LANES), F32)

    def pack_edges(src, channels, slot):
        def tile(r, c):
            to_left = to_right = own = jnp.zeros((R, LANES), F32)
            for i in range(NI):
                a = src[i, r, 0:LANES].astype(F32)
                z = src[i, r, F - LANES : F].astype(F32)
                base = 32 * i
                to_left += jnp.where(
                    (lane == base + 17) | (lane == base + 18), pltpu.roll(a, base + 17, 1), 0.0
                )
                to_right += jnp.where(
                    (lane == base) | (lane == base + 1), pltpu.roll(z, base + 2, 1), 0.0
                )
                own += jnp.where(lane == base + 2, pltpu.roll(a, base + 2, 1), 0.0)
                own += jnp.where(lane == base + 16, pltpu.roll(z, base + 17, 1), 0.0)
            edge_src[slot, 0, r, :] = to_left.astype(BF16)
            edge_src[slot, 1, r, :] = to_right.astype(BF16)
            edge_src[slot, 2, r, :] = own.astype(BF16)
            return c

        per_tile(tile, channels)

    def edge_copy(slot, side, channels):
        rows = pl.ds(0, channels)
        return remote(
            edge_src.at[slot, side, rows],
            edge_in.at[slot, side, rows],
            sem_es.at[slot, side],
            sem_er.at[slot, side],
            {"tm": left if side == 0 else right},
        )

    def send_edges(slot, channels):
        @pl.when(t > 0)
        def _():
            edge_copy(slot, 0, channels).start()

        @pl.when(t < last)
        def _():
            edge_copy(slot, 1, channels).start()

    def recv_edges(slot, channels, dst):
        @pl.when(t > 0)
        def _():
            edge_copy(slot, 0, channels).wait_send()
            edge_copy(slot, 1, channels).wait_recv()

        @pl.when(t < last)
        def _():
            edge_copy(slot, 1, channels).wait_send()
            edge_copy(slot, 0, channels).wait_recv()

        def tile(r, c):
            total = edge_src[slot, 2, r, :].astype(F32)
            for side in (0, 1):
                total += edge_in[slot, side, r, :].astype(F32)
            dst[r, :] = total.astype(BF16)
            return c

        per_tile(tile, channels)

    def rectify(neg, rest):
        soft = jnp.maximum(neg, jnp.log2(1.0 + jnp.exp2(jnp.minimum(neg, 100.0))))
        return rest * soft - neg, soft

    def masked_sums(a, m, sums):
        am = a * m
        return (sums[0] + fold_rows(fold(am)), sums[1] + fold_rows(fold(am * a)))

    def phase1(k):
        width = W if k == 0 else F
        x = x0 if k == 0 else x1
        act = act1_0 if k == 0 else act1_1
        mid = MID if k == 0 else slice(0, F)

        def item(i):
            wide_s[:, 0:width] = dot(wpre[k], x[i])
            m = mask_row(i, R)

            def tile(r, sums):
                table = chan[k, r, :]
                bias = column(table, 0) * -LOG2E
                rest = 1.0 - column(table, 1)
                neg = wide_s[r, 0:width] * -LOG2E + wide(bias, width)
                a, soft = rectify(neg, wide(rest, width))
                act[i, r, :] = a.astype(BF16)
                soft1[k, i, r, :] = soft[:, mid].astype(BF16)
                return masked_sums(a[:, mid], m, sums)

            a, b = per_tile(tile, init=(zero8, zero8))
            send_stats(4 * k, i, a, b)

        per_item(item)
        if k == 1:
            recv_edges(1, B, x_edge)
            wide_s[:, 0:LANES] = dot(wpre[1], x_edge[...])

            def tile(r, c):
                table = chan[1, r, :]
                neg = wide_s[r, 0:LANES] * -LOG2E + column(table, 0) * -LOG2E
                a, _ = rectify(neg, 1.0 - column(table, 1))
                wide_s[r, 0:LANES] = a
                return c

            per_tile(tile)

    def phase2(k):
        width = W if k == 0 else F
        at = 0 if k == 0 else DILATION
        act = act1_0 if k == 0 else act1_1

        def item(i):
            finish_norm(4 * k, 2 * k, i)
            mean, inv = tall(stat[2 * k, i, 0], R), tall(stat[2 * k, i, 1], R)
            m = mask_row(i, R, at, width)

            def tile(r, c):
                table = chan[k, r, :]
                scale = inv * column(table, 2)
                shift = column(table, 3) - mean * scale
                a = act[i, r, :].astype(F32)
                buf[i, r, at : at + width] = (
                    (a * wide(scale, width) + wide(shift, width)) * m
                ).astype(BF16)
                return c

            per_tile(tile)

        per_item(item)
        if k == 1:
            mean, inv = tall(lanes_of(stat.at[2], 0), R), tall(lanes_of(stat.at[2], 1), R)
            m = tall(edge_mask_ref[...], R)

            def tile(r, c):
                table = chan[1, r, :]
                scale = inv * column(table, 2)
                a = wide_s[r, 0:LANES]
                first_edge[r, :] = (((a - mean) * scale + column(table, 3)) * m).astype(BF16)
                return c

            per_tile(tile)

    def neighbours(f, edge, i):
        shifted_in = pltpu.roll(edge, lax.rem(127 - 32 * i + 256, 128), 1)
        before = pltpu.roll(f, 1, 1)
        lead = jnp.where(lane == 0, shifted_in, before[:, 0:LANES])
        before = jnp.concatenate([lead, before[:, LANES:]], axis=1)
        shifted_in = pltpu.roll(edge, lax.rem(110 - 32 * i + 256, 128), 1)
        after = pltpu.roll(f, F - 1, 1)
        trail = jnp.where(lane == LANES - 1, shifted_in, after[:, F - LANES :])
        after = jnp.concatenate([after[:, : F - LANES], trail], axis=1)
        return before, after

    def taps(k, i, r, edge):
        f = buf[i, r, MID].astype(F32)
        if k == 0:
            return buf[i, r, 0:F].astype(F32), f, buf[i, r, 2 * DILATION : W].astype(F32)
        before, after = neighbours(f, edge[r, :].astype(F32), i)
        return before, f, after

    def conv_coefs(table):
        return [column(table, j) * -LOG2E for j in (4, 5, 6, 7)], 1.0 - column(table, 8)

    def phase3(k):
        def item(i):
            m = mask_row(i, R)

            def tile(r, sums):
                c, rest = conv_coefs(chan[k, r, :])
                before, f, after = taps(k, i, r, first_edge)
                neg = wide(c[0], F) * before + wide(c[1], F) * f + wide(c[2], F) * after + wide(c[3], F)
                a, soft = rectify(neg, wide(rest, F))
                act2[k, i, r, :] = a.astype(BF16)
                soft2[k, i, r, :] = soft.astype(BF16)
                return masked_sums(a, m, sums)

            a, b = per_tile(tile, init=(zero8, zero8))
            send_stats(4 * k + 1, i, a, b)

        per_item(item)
        if k == 1:

            def tile(r, x):
                c, rest = conv_coefs(chan[1, r, :])
                f = first_edge[r, :].astype(F32)
                neg = c[0] * pltpu.roll(f, 1, 1) + c[1] * f + c[2] * pltpu.roll(f, LANES - 1, 1) + c[3]
                a, soft = rectify(neg, rest)
                act_edge[r, :] = a.astype(BF16)
                soft_edge[r, :] = soft.astype(BF16)
                return x

            per_tile(tile)

    def out_copy(kind, k, i, src):
        dst = (block_h, skip_h)[kind]
        row = first_item + i
        return (
            pltpu.make_async_copy(src.at[i], dst.at[row], sem_o.at[kind, k, i]),
            remote(src.at[i], dst.at[row], sem_o.at[kind, k, i], sem_or.at[kind, i], {"section": o}),
        )

    def phase4(k):
        x = x0 if k == 0 else x1
        mid = MID if k == 0 else slice(0, F)
        out = x1 if k == 0 else out1
        skip = skip0 if k == 0 else skip1

        def item(i):
            finish_norm(4 * k + 1, 2 * k + 1, i)
            mean, inv = tall(stat[2 * k + 1, i, 0], R), tall(stat[2 * k + 1, i, 1], R)
            m = mask_row(i, R)
            y = pl.ds(0, 2 * B)
            wide_s[y, 0:F] = dot(wg[k], act2[k, i])

            def project(r):
                table = col[k, r, :]
                shift = column(table, 0) - mean * inv * column(table, 1)
                return (wide_s[r, 0:F] * wide(inv, F) + wide(shift, F)) * m

            def residual(r, c):
                out[i, r, :] = (x[i, r, mid].astype(F32) + project(r)).astype(BF16)
                return c

            def skipped(j, c):
                r = rows_at(j, R)
                p = project(pl.ds(pl.multiple_of(B + j * R, R), R))
                if k == 1:
                    p += skip0[i, r, :].astype(F32)
                skip[i, r, :] = p.astype(BF16)
                return c

            per_tile(residual, B)
            lax.fori_loop(0, B // R, skipped, 0)
            for kind, src in ((0, out), (1, skip)):
                here, there = out_copy(kind, k, i, src)

                @pl.when(s == k)
                def _():
                    here.start()

                @pl.when(s != k)
                def _():
                    there.start()

        per_item(item)

    def phase5(k):
        R5 = 4 * R

        def item(i):
            mean, inv = tall(stat[2 * k + 1, i, 0], R5), tall(stat[2 * k + 1, i, 1], R5)
            wide_s[:, 0 : 2 * B] = dot(act2[k, i], dp[i], NT)
            total8 = dot(jnp.ones((8, F), BF16), dp[i], NT)
            gb[k] += total8
            total = tall(total8, R5)

            def tile(r, sums):
                table = chan[k, r, :]
                g, e = column(table, 9), column(table, 10)
                product = wide_s[r, 0 : 2 * B]
                w = wout[k, r, :].astype(F32)
                against = fold(w * product)
                plain = fold(w * total)
                normed = inv * (against - mean * plain)
                gacc[9, r, :] += normed
                gacc[10, r, :] += plain
                scale = inv * g
                shift = e - mean * scale
                gwo[k, r, :] += wide(scale, 2 * B) * product + wide(shift, 2 * B) * total
                return (sums[0] + fold_rows(g * plain), sums[1] + fold_rows(g * normed))

            a, b = per_tile(tile, rows=R5, init=(zero8, zero8))
            send_stats(4 * k + 2, i, a, b)

        per_item(item)

    def halo_copy(i, side):
        edge = pl.ds(DILATION, DILATION) if side == 0 else pl.ds(F, DILATION)
        return remote(
            buf.at[i, :, edge],
            buf.at[i, :, tail if side == 0 else head],
            sem_hs.at[side, i],
            sem_hr.at[side, i],
            {"tm": left if side == 0 else right},
        )

    def phase6(k):
        def item(i):
            finish_back(4 * k + 2, 2 * k + 1, i)
            inv = tall(stat[2 * k + 1, i, 1], R) * LOG2E
            p, q = wide(tall(back[i, 0], R), F), wide(tall(back[i, 1], R), F)
            m = mask_row(i, R)
            wide_s[:, 0:F] = dot(wout[k], dp[i])

            def tile(r, c):
                table = chan[k, r, :]
                slope = column(table, 8)
                g = inv * column(table, 9)
                d_act = wide_s[r, 0:F] * wide(g, F) + m * (p + q * act2[k, i, r, :].astype(F32))
                soft = soft2[k, i, r, :].astype(F32)
                d_conv = d_act * (wide(slope, F) + wide(1.0 - slope, F) * jnp.exp2(-soft))
                gacc[8, r, :] += fold(d_act * soft) * -LN2
                gacc[7, r, :] += fold(d_conv)
                buf[i, r, MID] = d_conv.astype(BF16)
                return c

            per_tile(tile)
            if k == 0:

                @pl.when(t > 0)
                def _():
                    halo_copy(i, 0).start()

                @pl.when(t < last)
                def _():
                    halo_copy(i, 1).start()

                @pl.when(t == 0)
                def _():
                    buf[i, :, 0:DILATION] = jnp.zeros((H, DILATION), BF16)

                @pl.when(t == last)
                def _():
                    buf[i, :, F + DILATION : W] = jnp.zeros((H, DILATION), BF16)

        per_item(item)
        if k == 1:
            wide_s[:, 0:LANES] = dot(wout[1], dp_edge[...])
            inv = tall(lanes_of(stat.at[3], 1), R) * LOG2E
            p, q = tall(lanes_of(back, 0), R), tall(lanes_of(back, 1), R)
            m = tall(edge_mask_ref[...], R)

            def tile(r, c):
                table = chan[1, r, :]
                slope = column(table, 8)
                d_act = wide_s[r, 0:LANES] * (inv * column(table, 9)) + m * (p + q * act_edge[r, :].astype(F32))
                d_conv = d_act * (slope + (1.0 - slope) * jnp.exp2(-soft_edge[r, :].astype(F32)))
                conv_edge[r, :] = d_conv.astype(BF16)
                return c

            per_tile(tile)

    def phase7(k):
        act = act1_0 if k == 0 else act1_1
        mid = MID if k == 0 else slice(0, F)

        def item(i):
            if k == 0:

                @pl.when(t > 0)
                def _():
                    halo_copy(i, 0).wait_send()
                    halo_copy(i, 1).wait_recv()

                @pl.when(t < last)
                def _():
                    halo_copy(i, 1).wait_send()
                    halo_copy(i, 0).wait_recv()

            mean, inv = tall(stat[2 * k, i, 0], R), tall(stat[2 * k, i, 1], R)
            m = mask_row(i, R)

            def tile(r, sums):
                table = chan[k, r, :]
                g = column(table, 2)
                scale = inv * g
                shift = column(table, 3) - mean * scale
                before, d, after = taps(k, i, r, conv_edge)
                u = (
                    wide(column(table, 4), F) * after
                    + wide(column(table, 5), F) * d
                    + wide(column(table, 6), F) * before
                ) * m
                a = act[i, r, mid].astype(F32)
                first = (a * wide(scale, F) + wide(shift, F)) * m
                plain = fold(u)
                normed = inv * (fold(u * a) - mean * plain)
                gacc[2, r, :] += normed
                gacc[3, r, :] += plain
                gacc[4, r, :] += fold(after * first)
                gacc[5, r, :] += fold(d * first)
                gacc[6, r, :] += fold(before * first)
                soft2[k, i, r, :] = u.astype(BF16)
                return (sums[0] + fold_rows(g * plain), sums[1] + fold_rows(g * normed))

            a, b = per_tile(tile, init=(zero8, zero8))
            send_stats(4 * k + 3, i, a, b)

        per_item(item)

    def mix_copy(i):
        row = first_item + i
        return (
            pltpu.make_async_copy(out1.at[i, own_rows], gmix_h.at[row], sem_m.at[0, i]),
            remote(out1.at[i, other_rows], gmix_h.at[row], sem_m.at[1, i], sem_mr.at[i], {"section": o}),
        )

    def phase8(k):
        act = act1_0 if k == 0 else act1_1
        x = x0 if k == 0 else x1
        mid = MID if k == 0 else slice(0, F)

        def item(i):
            finish_back(4 * k + 3, 2 * k, i)
            inv = tall(stat[2 * k, i, 1], R) * LOG2E
            p, q = wide(tall(back[i, 0], R), F), wide(tall(back[i, 1], R), F)
            m = mask_row(i, R)

            def tile(r, c):
                table = chan[k, r, :]
                slope = column(table, 1)
                g = inv * column(table, 2)
                d_act = soft2[k, i, r, :].astype(F32) * wide(g, F) + m * (p + q * act[i, r, mid].astype(F32))
                soft = soft1[k, i, r, :].astype(F32)
                d_pre = d_act * (wide(slope, F) + wide(1.0 - slope, F) * jnp.exp2(-soft))
                gacc[1, r, :] += fold(d_act * soft) * -LN2
                gacc[0, r, :] += fold(d_pre)
                dpre[r, :] = d_pre.astype(BF16)
                return c

            per_tile(tile)
            gwi[k] += dot(dpre[...], x[i, :, mid], NT)
            wide_s[0:B, 0:F] = dot(win[k], dpre[...])

            def add(r, c):
                d_input = wide_s[r, 0:F] + dp[i, r, :].astype(F32)
                if k == 1:
                    dp[i, r, :] = (d_input * m).astype(BF16)
                else:
                    out1[i, r, :] = (d_input * m).astype(BF16)
                return c

            per_tile(add, B)
            if k == 0:
                here, there = mix_copy(i)
                there.start()
                here.start()

        per_item(item)

    grads = ((gwi, rwi, gwi_h), (gwo, rwo, gwo_h), (gch, rch, gch_h), (gb, rb, gb_h))

    def grad_copy(j, k):
        own, there, _ = grads[j]
        return remote(own.at[k], there, sem_k.at[j], sem_kr.at[j], {"section": o})

    def finish_block(k):
        ones = jnp.ones((8, LANES), F32)
        gch[k] = jnp.concatenate(
            [dot(ones, gacc[j], NT, lax.Precision.HIGHEST)[0:1] for j in range(11)] + [jnp.zeros((5, H), F32)], axis=0
        )

        @pl.when(s != k)
        def _():
            for j in range(4):
                grad_copy(j, k).start()

    for j in range(len(weights)):
        local, send, recv = weight_copies(j)
        local.wait()
        recv.wait_recv()
        send.wait_send()
    main_local.wait()
    main_send.wait_send()
    main_recv.wait_recv()

    @pl.when(t > 0)
    def _():
        for core in (0, 1):
            halo_send(0, core).wait_send()
            halo_recv(1, core).wait_recv()

    @pl.when(t < last)
    def _():
        for core in (0, 1):
            halo_send(1, core).wait_send()
            halo_recv(0, core).wait_recv()

    phase1(0)
    load_out.wait()
    load_skip.wait()

    def mask_gradients(i):
        m = mask_row(i, R)

        def tile(r, c):
            dp[i, r, :] = (dp[i, r, :].astype(F32) * m).astype(BF16)
            return c

        per_tile(tile, 2 * B)

    per_item(mask_gradients)
    pack_edges(dp, 2 * B, 0)
    send_edges(0, 2 * B)
    phase2(0)
    phase3(0)
    phase4(0)
    pack_edges(x1, B, 1)
    send_edges(1, B)
    phase1(1)
    phase2(1)
    phase3(1)
    phase4(1)
    recv_edges(0, 2 * B, dp_edge)
    for k in (1, 0):
        gacc[...] = jnp.zeros(gacc.shape, F32)
        phase5(k)
        phase6(k)
        phase7(k)
        if k == 0:
            for i in range(NI):
                here, there = out_copy(0, 1, i, out1)

                @pl.when(s == 1)
                def _():
                    here.wait()

                @pl.when(s == 0)
                def _():
                    there.wait_send()

        phase8(k)
        finish_block(k)

    for k in (0, 1):

        @pl.when(s != k)
        def _():
            for j in range(4):
                grad_copy(j, k).wait_send()

        @pl.when(s == k)
        def _():
            for j in range(4):
                grad_copy(j, k).wait_recv()
                own, there, _ = grads[j]
                own[k] += there[...]
            for j in range(4):
                own, _, result = grads[j]
                pltpu.make_async_copy(own.at[k], result, sem_f.at[j]).start()
            for j in range(4):
                own, _, result = grads[j]
                pltpu.make_async_copy(own.at[k], result, sem_f.at[j]).wait()

    for i in range(NI):
        here, there = mix_copy(i)
        here.wait()
        there.wait_send()
        remote(
            out1.at[i, other_rows], gmix_h.at[o * NI + i], sem_m.at[1, i], sem_mr.at[i], {"section": o}
        ).wait_recv()
        for kind, srcs in ((0, (x1, out1)), (1, (skip0, skip1))):
            for k in (0, 1):
                here, there = out_copy(kind, k, i, srcs[k])

                if (kind, k) != (0, 1):

                    @pl.when(s == k)
                    def _():
                        here.wait()

                    @pl.when(s != k)
                    def _():
                        there.wait_send()

            dst = (block_h, skip_h)[kind]
            remote(
                srcs[0].at[i], dst.at[o * NI + i], sem_o.at[kind, 0, i], sem_or.at[kind, i], {"section": o}
            ).wait_recv()


def run(n_tm, mix, gout, gskip, masks, edge_mask, inv_n, wpre, wout, wg, win, chan, col):
    items, half, F = mix.shape
    NI = items // 2
    H, B = wpre.shape
    W = F + 2 * DILATION
    any_spec = pl.BlockSpec(memory_space=pl.ANY)
    vmem = pl.BlockSpec(memory_space=pltpu.VMEM)
    dma = pltpu.SemaphoreType.DMA
    shape = jax.ShapeDtypeStruct
    outs = (
        shape((items, B, F), BF16),
        shape((items, B, F), BF16),
        shape((items, half, F), BF16),
        shape((H, B), F32),
        shape((H, 2 * B), F32),
        shape((16, H), F32),
        shape((8, 2 * B), F32),
    )
    scratch = [
        pltpu.VMEM((NI, B, W), BF16),
        pltpu.VMEM((NI, B, F), BF16),
        pltpu.VMEM((NI, B, F), BF16),
        pltpu.VMEM((NI, B, F), BF16),
        pltpu.VMEM((NI, B, F), BF16),
        pltpu.VMEM((NI, H, W), BF16),
        pltpu.VMEM((NI, H, F), BF16),
        pltpu.VMEM((2, NI, H, F), BF16),
        pltpu.VMEM((2, NI, H, F), BF16),
        pltpu.VMEM((2, NI, H, F), BF16),
        pltpu.VMEM((NI, H, W), BF16),
        pltpu.VMEM((H, W), F32),
        pltpu.VMEM((H, F), BF16),
        pltpu.VMEM((NI, 2 * B, F), BF16),
        pltpu.VMEM((11, H, LANES), F32),
        pltpu.VMEM((2, H, B), BF16),
        pltpu.VMEM((2, H, 2 * B), BF16),
        pltpu.VMEM((2, 2 * B, H), BF16),
        pltpu.VMEM((2, B, H), BF16),
        pltpu.VMEM((2, H, LANES), F32),
        pltpu.VMEM((2, 2 * B, LANES), F32),
        pltpu.VMEM((2, H, B), F32),
        pltpu.VMEM((2, H, 2 * B), F32),
        pltpu.VMEM((2, 16, H), F32),
        pltpu.VMEM((2, 8, 2 * B), F32),
        pltpu.VMEM((H, B), F32),
        pltpu.VMEM((H, 2 * B), F32),
        pltpu.VMEM((16, H), F32),
        pltpu.VMEM((8, 2 * B), F32),
        pltpu.VMEM((4, NI, 2, 8, LANES), F32),
        pltpu.VMEM((NI, 2, 8, LANES), F32),
        pltpu.VMEM((2, NI, 8, LANES), F32),
        pltpu.VMEM((2, NI, n_tm - 1, 8, LANES), F32),
        pltpu.VMEM((2, 3, 2 * B, LANES), BF16),
        pltpu.VMEM((2, 2, 2 * B, LANES), BF16),
        pltpu.VMEM((B, LANES), BF16),
        pltpu.VMEM((2 * B, LANES), BF16),
        pltpu.VMEM((H, LANES), BF16),
        pltpu.VMEM((H, LANES), BF16),
        pltpu.VMEM((H, LANES), BF16),
        pltpu.VMEM((H, LANES), BF16),
        dma((6, 3)),
        dma((6,)),
        dma((5,)),
        dma((2,)),
        dma((2, 2)),
        dma((2, 2)),
        dma((2, NI, n_tm - 1)),
        dma((2, NI, n_tm - 1)),
        dma((2, NI)),
        dma((2, NI)),
        dma((2, 2, NI)),
        dma((2, NI)),
        dma((2, NI)),
        dma((NI,)),
        dma((4,)),
        dma((4,)),
        dma((4,)),
    ]
    return pl.pallas_call(
        functools.partial(kernel, (n_tm, NI, H, B, F)),
        out_shape=outs,
        in_specs=[any_spec] * 3 + [vmem] * 3 + [any_spec] * 6,
        out_specs=[any_spec] * len(outs),
        scratch_shapes=scratch,
        compiler_params=pltpu.CompilerParams(
            collective_id=0, has_side_effects=True, vmem_limit_bytes=63 * 1024 * 1024
        ),
        name="temporal_blocks",
    )(mix, gout, gskip, masks, edge_mask, inv_n, wpre, wout, wg, win, chan, col)


def local(sources, source_counts, valid_lengths, w_in, chan, w_out, b_out, grad_out, grad_skip):
    n_sources, per_device, half, F = sources.shape
    H, B = w_in.shape[1:]
    NI = per_device // 2
    n_tm = lax.axis_size("tm")
    s = lax.axis_index("section")
    start = lax.axis_index("tm") * F
    where = start + jnp.arange(F, dtype=jnp.int32)
    masks = (where[None, :] < valid_lengths[:, None]).astype(F32)
    chosen = (jnp.arange(n_sources, dtype=jnp.int32)[:, None] < source_counts[None, :]).astype(F32)
    mix = (jnp.sum(sources.astype(F32) * chosen[:, :, None, None], axis=0) * masks[:, None, :]).astype(BF16)
    own = lax.dynamic_slice_in_dim(valid_lengths, s * NI, NI, 0)
    wider = start - DILATION + jnp.arange(F + 2 * DILATION, dtype=jnp.int32)
    own_masks = ((wider[None, :] >= 0) & (wider[None, :] < own[:, None])).astype(F32)
    own_masks = jnp.broadcast_to(own_masks[:, None, :], (NI, 8, F + 2 * DILATION))
    lanes = jnp.arange(LANES, dtype=jnp.int32)
    within = lanes % 32
    frame = start + jnp.where(within < 16, within - 2, within - 17 + F)
    edge_mask = (
        ((within < 3) | ((within >= 16) & (within < 19))) & (frame >= 0) & (frame < jnp.repeat(own, 32)[:LANES])
    ).astype(F32)
    edge_mask = jnp.broadcast_to(edge_mask[None, :], (8, LANES))
    inv_n = jnp.broadcast_to((1.0 / (own.astype(F32) * H))[:, None, None], (NI, 8, LANES))
    table = chan[0]
    gained = (w_out[0].astype(F32) * table[9][None, :]).astype(BF16)
    col = jnp.stack(
        [
            b_out[0] + jnp.sum(w_out[0].astype(F32) * table[10][None, :], axis=1),
            jnp.sum(gained.astype(F32), axis=1),
        ],
        axis=1,
    )
    block_out, skip_out, gmix, gwi, gwo, gch, gb = run(
        n_tm,
        mix,
        grad_out,
        grad_skip,
        own_masks,
        edge_mask,
        inv_n,
        w_in[0],
        w_out[0].T,
        gained,
        w_in[0].T,
        jnp.pad(table.T, ((0, 0), (0, LANES - table.shape[0]))),
        jnp.pad(col, ((0, 0), (0, LANES - 2))),
    )
    gwi, gwo, gch, gb = lax.psum((gwi, gwo, gch[:11], gb[0]), ("tm", "item"))
    grad_sources = chosen[:, :, None, None] * gmix.astype(F32)[None]
    return (block_out[None], skip_out[None], grad_sources, gwi[None], gch[None], gwo.T[None], gb[None])


def solution(mesh):
    in_specs = (
        P(None, "item", "section", "tm"),
        P("item"),
        P("item"),
        P("section", None, None),
        P("section", None, None),
        P("section", None, None),
        P("section", None),
        P("item", None, "tm"),
        P("item", None, "tm"),
    )
    out_specs = (
        P("section", "item", None, "tm"),
        P("section", "item", None, "tm"),
        P(None, "item", "section", "tm"),
        P("section", None, None),
        P("section", None, None),
        P("section", None, None),
        P("section", None),
    )
    return jax.shard_map(local, mesh=mesh, in_specs=in_specs, out_specs=out_specs, check_vma=False)
```

time: 1200 us -> 385 us (0.32)
  other arithmetic: 356 us -> 14.1 us
  blocking collectives: 369 us -> 75.5 us
  Pallas kernels: 0 us -> 237 us
  matrix products: 148 us -> 0 us
  waiting for transfers between devices: 164 us -> 27 us
  starting transfers between devices: 82.6 us -> 0.04 us
  local copies, waits for them, and re-layouts: 53.4 us -> 17.1 us
    psum x31 -> x1, blocking collectives: 369 us -> 75.5 us  [local(): gwi, gwo, gch, gb = lax.psum((gwi, gwo, gch[:11], gb[0]), ('tm', 'item'))]
    reduce_sum x53 -> x2, other arithmetic: 287 us -> 4.7 us  [the longest x1 2.98 us: local(): jnp.sum(sources.astype(F32) * chosen[:, :, None, None], axis=0)]
    pallas_call x0 -> x1, Pallas kernels: none -> 237 us  [run(): pl.pallas_call(functools.partial(kernel, (n_tm, NI, H, B, F)), out_shape=...]
    dot_general x35 -> x0, matrix products: 148 us -> none  [the longest x10 71.2 us: block_forward(): jnp.einsum('hb,ibf->ihf', w_first, block_in, preferred_element_type=jnp.f...]
    ppermute x43 -> x0, starting transfers between devices: 82.5 us -> none  [the longest x15 38.7 us: padded(): lax.ppermute(tail, axis, [(i, (i + 1) % count) for i in range(ends)])]
    psum x1, waiting for transfers between devices: 94 us -> 27 us  [local(): gwi, gwo, gch, gb = lax.psum((gwi, gwo, gch[:11], gb[0]), ('tm', 'item'))]
    ppermute x43 -> x0, waiting for transfers between devices: 57.6 us -> none  [the longest x15 39 us: padded(): lax.ppermute(head, axis, [((i + 1) % count, i) for i in range(ends)])]
    select_n x16 -> x0, other arithmetic: 23.7 us -> none  [the longest x5 13.9 us: local(): jnp.where(is_live, lax.dynamic_update_slice_in_dim(skip_store, next_skip,...]
  transfers between devices with their start and end apart: 45 -> 1, of which waited for: 23 -> 1; matrix products, arithmetic and copies ran while one was open for 29% -> 2% of each run, Pallas kernels for 0% -> 0%
where the time goes in v1:
time: 385 us
  Pallas kernels  237 us (62%)
  blocking collectives  75.5 us (20%)
  waiting for transfers between devices  27 us (7%)
  local copies, waits for them, and re-layouts  17.1 us (4%)
  other arithmetic  14.1 us (4%)
  between operations  14.1 us (4%)
    pallas_call x1, Pallas kernels, run(): pl.pallas_call(functools.partial(kernel, (n_tm, NI, H, B, F)), out_shape=...  237 us
    psum x1, blocking collectives, local(): gwi, gwo, gch, gb = lax.psum((gwi, gwo, gch[:11], gb[0]), ('tm', 'item'))  75.5 us
    psum x1, waiting for transfers between devices, local(): gwi, gwo, gch, gb = lax.psum((gwi, gwo, gch[:11], gb[0]), ('tm', 'item'))  27 us
    unnamed x13, local copies, waits for them, and re-layouts  9.57 us
  transfers between devices with their start and end apart: 1, of which 1 were waited for; matrix products, arithmetic and copies ran while one was open for 2% of the time, Pallas kernels for 0%

profile of v1, /device:TPU:0, one launch (start us, length us, event | category | flops | bytes accessed | tf_op | source)
XLA Modules:
  0.0 384.8 jit_solution(123790107816252724)
XLA Ops:
  7.2 0.0 all-reduce.6.cloned.1.call-start
  7.3 0.7 fusion.5
  8.0 0.9 copy.32
  8.8 0.7 fusion.2
  9.5 0.7 multiply_divide_fusion
  10.2 0.1 broadcast_in_dim.21
  10.3 0.1 reshape.156
  10.4 0.7 compare_convert_fusion
  11.1 1.7 copy.31
  12.8 1.7 convert_reduce_fusion
  14.5 0.7 bitcast_add_fusion
  15.2 0.1 copy.33
  15.3 1.8 copy.35.wout_h
  17.1 0.7 pad.9.col_h
  17.8 0.7 pad.8.chan_h
  18.5 0.1 and_convert_fusion
  18.6 3.0 multiply_reduce_fusion
  21.6 1.2 multiply_convert_fusion.mix_h
  22.8 0.6 broadcast_in_dim.22.edge_mask_ref
  23.4 0.7 broadcast_in_dim.23.invn_ref
  24.1 0.7 broadcast_in_dim.20.mask_ref
  24.8 236.8 %temporal_blocks.1 = (bf16[8,128,1024]{2,1,0:T(8,128)(2,1)}, bf16[8,128,1024]{2,1,0:T(8,128)(2,1)}, bf16[8,64,1024]{2,1,0:T(8,128)(2,1)}, f32[512,128]{1,0:T(8,1...) custom-call(bf16[8,64,1024]{2,1,0:T(8,128)(2,1)} %multiply_convert_fusion.mix_h, ...), custom_call_target="tpu_custom_call" | custom-call | tf_op jit(solution)/shard_map/temporal_blocks/pallas_call | solution.py:895
  261.6 0.0 all-reduce.6.cloned.1.call-update
  261.7 0.7 slice.17
  262.4 0.8 slice_bitcast_fusion
  263.1 75.5 %all-reduce.2 = (f32[1,11,512]{2,1,0:T(8,128)S(1)}, f32[1,256]{1,0:T(1,128)}) all-reduce(f32[1,11,512]{2,1,0:T(8,128)S(1)} %slice_bitcast_fusion, f32[1,256]{1,0:T(1,128)S(1)} %slice.17), channel_id=1, replica_groups=mesh['section'=2,'tm'=4,'item'=4] {'tm','item'}, use_global_device_ids=true, to_apply=%region_4.5 | all-reduce | flops 5888 | bytes 47104 | tf_op jit(solution)/shard_map/psum | solution.py:955
  338.6 0.6 copy.36
  339.3 1.5 convert_element_type.64
  340.8 0.0 copy-start.1
  340.8 3.8 broadcast_multiply_fusion
  344.5 27.0 %all-reduce.6.cloned.1.call-done = (f32[1,512,128]{2,1,0:T(8,128)}, f32[1,256,512]{1,2,0:T(8,128)}) async-done(((f32[1,512,128]{2,1,0:T(8,128)}, f32[1,256,512]{1,2,0:T(8,128)}), (f32[1,512,128]{2,1,0:T(8,128)}, f32[1,256,512]{1,2,0:T(8,128)})) %all-reduce.6.cloned.1.call-update) | async-done | bytes 786448 | tf_op jit(solution)/shard_map/psum | solution.py:955
  371.5 2.0 copy.37
  373.5 0.0 copy-done.1
  373.5 0.0 copy-start
  373.5 1.3 copy.44
  374.9 1.0 copy-done
  375.9 0.0 copy-start.2
  375.9 1.3 copy.45
  377.2 0.0 copy-done.2
  377.2 0.7 copy.46
  (5 shorter events, 0.0 us)
Async XLA Ops:
  7.2 364.3 %all-reduce.6.cloned.1.call-start = ((), (), s32[]{:S(2)}) async-start(), calls=%async_computation | async-start | bytes 1572864 | tf_op jit(solution)/shard_map/psum | solution.py:955
  340.8 32.8 %copy-start.1 = (bf16[8,128,1024]{2,1,0:T(8,128)(2,1)S(1)}, bf16[8,128,1024]{2,1,0:T(8,128)(2,1)}, u32[]{:S(2)}) copy-start(bf16[8,128,1024]{2,1,0:T(8,128)(2,1)} %get-tuple-element.14) | copy-start | bytes 6291460
  373.5 2.3 copy-start
  375.9 1.3 copy-start.2
Sparse Core Ops, SparseCore 0:
  261.8 109.6 all-reduce.5

commit v2 on v1

--- a/solution.py
+++ b/solution.py
@@ -10,7 +10,7 @@
 
 DILATION = 128
 LANES = 128
-ROWS = 16
+ROWS = 128
 EPSILON = 1e-05
 LN2 = math.log(2.0)
 LOG2E = 1.0 / LN2

time: 385 us -> 273 us (0.71)
  Pallas kernels: 237 us -> 125 us
    pallas_call x1, Pallas kernels: 237 us -> 125 us  [run(): pl.pallas_call(functools.partial(kernel, (n_tm, NI, H, B, F)), out_shape=...]
  transfers between devices with their start and end apart: 1 -> 1, of which waited for: 1 -> 1; matrix products, arithmetic and copies ran while one was open for 2% -> 3% of each run, Pallas kernels for 0% -> 0%
where the time goes in v2:
time: 273 us
  Pallas kernels  125 us (46%)
  blocking collectives  75.6 us (28%)
  waiting for transfers between devices  27.1 us (10%)
  local copies, waits for them, and re-layouts  17.1 us (6%)
  other arithmetic  14.1 us (5%)
  between operations  14.1 us (5%)
    pallas_call x1, Pallas kernels, run(): pl.pallas_call(functools.partial(kernel, (n_tm, NI, H, B, F)), out_shape=...  125 us
    psum x1, blocking collectives, local(): gwi, gwo, gch, gb = lax.psum((gwi, gwo, gch[:11], gb[0]), ('tm', 'item'))  75.6 us
    psum x1, waiting for transfers between devices, local(): gwi, gwo, gch, gb = lax.psum((gwi, gwo, gch[:11], gb[0]), ('tm', 'item'))  27.1 us
    unnamed x13, local copies, waits for them, and re-layouts  9.57 us
  transfers between devices with their start and end apart: 1, of which 1 were waited for; matrix products, arithmetic and copies ran while one was open for 3% of the time, Pallas kernels for 0%

profile of v2, /device:TPU:0, one launch (start us, length us, event | category | flops | bytes accessed | tf_op | source)
XLA Modules:
  0.0 272.6 jit_solution(10351879184733615486)
XLA Ops:
  7.2 0.0 all-reduce.6.cloned.1.call-start
  7.3 0.7 fusion.5
  8.0 0.9 copy.32
  8.8 0.7 fusion.2
  9.5 0.7 multiply_divide_fusion
  10.2 0.1 broadcast_in_dim.21
  10.3 0.1 reshape.156
  10.4 0.7 compare_convert_fusion
  11.1 1.7 copy.31
  12.8 1.7 convert_reduce_fusion
  14.5 0.7 bitcast_add_fusion
  15.2 0.1 copy.33
  15.3 1.8 copy.35.wout_h
  17.1 0.7 pad.9.col_h
  17.8 0.7 pad.8.chan_h
  18.5 0.1 and_convert_fusion
  18.6 3.0 %multiply_reduce_fusion = f32[8,64,1024]{2,1,0:T(8,128)S(1)} fusion(bf16[3,8,64,1024]{3,2,1,0:T(8,128)(2,1)} %param.9, f32[3,8]{1,0:T(4,128)S(1)} %fusion.2), kind=kLoop, calls=%fused_computation | loop fusion | flops 4194304 | bytes 5242976 | tf_op jit(solution)/shard_map/reduce_sum | solution.py:918
  21.6 1.2 multiply_convert_fusion.mix_h
  22.8 0.6 broadcast_in_dim.22.edge_mask_ref
  23.4 0.7 broadcast_in_dim.23.invn_ref
  24.1 0.7 broadcast_in_dim.20.mask_ref
  24.8 124.5 %temporal_blocks.1 = (bf16[8,128,1024]{2,1,0:T(8,128)(2,1)}, bf16[8,128,1024]{2,1,0:T(8,128)(2,1)}, bf16[8,64,1024]{2,1,0:T(8,128)(2,1)}, f32[512,128]{1,0:T(8,1...) custom-call(bf16[8,64,1024]{2,1,0:T(8,128)(2,1)} %multiply_convert_fusion.mix_h, ...), custom_call_target="tpu_custom_call" | custom-call | tf_op jit(solution)/shard_map/temporal_blocks/pallas_call | solution.py:895
  149.3 0.0 all-reduce.6.cloned.1.call-update
  149.3 0.7 slice.17
  150.0 0.8 slice_bitcast_fusion
  150.8 75.6 %all-reduce.2 = (f32[1,11,512]{2,1,0:T(8,128)S(1)}, f32[1,256]{1,0:T(1,128)}) all-reduce(f32[1,11,512]{2,1,0:T(8,128)S(1)} %slice_bitcast_fusion, f32[1,256]{1,0:T(1,128)S(1)} %slice.17), channel_id=1, replica_groups=mesh['section'=2,'tm'=4,'item'=4] {'tm','item'}, use_global_device_ids=true, to_apply=%region_4.5 | all-reduce | flops 5888 | bytes 47104 | tf_op jit(solution)/shard_map/psum | solution.py:955
  226.4 0.6 copy.36
  227.0 1.5 convert_element_type.64
  228.5 0.0 copy-start.1
  228.5 3.8 %broadcast_multiply_fusion = f32[3,8,64,1024]{3,2,1,0:T(8,128)} fusion(f32[8,64,1024]{2,1,0:T(8,128)S(1)} %convert_element_type.64, f32[3,8]{1,0:T(4,128)S(1)} %fusion.2), kind=kLoop, calls=%fused_computation.1 | loop fusion | flops 1572864 | bytes 8388704 | tf_op jit(solution)/shard_map/mul | solution.py:956
  232.3 27.1 %all-reduce.6.cloned.1.call-done = (f32[1,512,128]{2,1,0:T(8,128)}, f32[1,256,512]{1,2,0:T(8,128)}) async-done(((f32[1,512,128]{2,1,0:T(8,128)}, f32[1,256,512]{1,2,0:T(8,128)}), (f32[1,512,128]{2,1,0:T(8,128)}, f32[1,256,512]{1,2,0:T(8,128)})) %all-reduce.6.cloned.1.call-update) | async-done | bytes 786448 | tf_op jit(solution)/shard_map/psum | solution.py:955
  259.4 2.0 copy.37
  261.4 0.0 copy-done.1
  261.4 0.0 copy-start
  261.4 1.3 copy.44
  262.7 1.0 copy-done
  263.7 0.0 copy-start.2
  263.7 1.3 copy.45
  265.1 0.0 copy-done.2
  265.1 0.7 copy.46
  (5 shorter events, 0.0 us)
Async XLA Ops:
  7.2 252.2 %all-reduce.6.cloned.1.call-start = ((), (), s32[]{:S(2)}) async-start(), calls=%async_computation | async-start | bytes 1572864 | tf_op jit(solution)/shard_map/psum | solution.py:955
  228.5 32.9 %copy-start.1 = (bf16[8,128,1024]{2,1,0:T(8,128)(2,1)S(1)}, bf16[8,128,1024]{2,1,0:T(8,128)(2,1)}, u32[]{:S(2)}) copy-start(bf16[8,128,1024]{2,1,0:T(8,128)(2,1)} %get-tuple-element.14) | copy-start | bytes 6291460
  261.4 2.3 copy-start
  263.7 1.3 copy-start.2
Sparse Core Ops, SparseCore 0:
  149.5 109.8 all-reduce.5

commit v3 on v2

v3 whole, which is shorter than its diff:
```python
import functools
import math

import jax
import jax.numpy as jnp
from jax import lax
from jax.experimental import pallas as pl
from jax.experimental.pallas import tpu as pltpu
from jax.sharding import PartitionSpec as P

DILATION = 128
LANES = 128
ROWS = 128
ROWS1 = 512
ROWS2 = 512
ROWS3 = 512
ROWS4 = 128
ROWS5 = 512
ROWS6 = 512
ROWS7 = 256
ROWS8 = 512
EPSILON = 1e-05
VMEM_LIMIT = 63 * 1024 * 1024 + 512 * 1024
LN2 = math.log(2.0)
LOG2E = 1.0 / LN2
F32 = jnp.float32
BF16 = jnp.bfloat16
MESH = pl.DeviceIdType.MESH
NT = (((1,), (1,)), ((), ()))
NN = (((1,), (0,)), ((), ()))


def dot(a, b, dims=NN, precision=None):
    return lax.dot_general(a, b, dims, precision=precision, preferred_element_type=F32)


def remote(src, dst, send, recv, device):
    return pltpu.make_async_remote_copy(
        src_ref=src, dst_ref=dst, send_sem=send, recv_sem=recv, device_id=device, device_id_type=MESH
    )


def wide(v, width):
    return jnp.concatenate([v] * (width // LANES), axis=1)


def tall(v, rows):
    return jnp.concatenate([v] * (rows // v.shape[0]), axis=0)


def fold(v):
    parts = [v[:, at : at + LANES] for at in range(0, v.shape[1], LANES)]
    while len(parts) > 1:
        parts = [a + b for a, b in zip(parts[::2], parts[1::2])] + parts[len(parts) & ~1 :]
    return parts[0]


def fold_rows(v):
    parts = [v[at : at + 8] for at in range(0, v.shape[0], 8)]
    while len(parts) > 1:
        parts = [a + b for a, b in zip(parts[::2], parts[1::2])] + parts[len(parts) & ~1 :]
    return parts[0]


def low(v):
    return v.astype(BF16)


def column(table, j):
    return jnp.broadcast_to(table[:, j : j + 1], (table.shape[0], LANES))


def rows_at(t, count):
    return pl.ds(pl.multiple_of(t * count, count), count)


def kernel(
    dims,
    sources_h, gout_h, gskip_h, w_in_ref, chan_ref, w_out_ref, b_out_ref, counts, lengths,
    block_h, skip_h, gmix_h, grad_h,
    stage, x0, x1, skips, act1_0, act1_1, soft1, act2, soft2, buf, wide_s, dp, gacc,
    wpre, wout, wg, win, chan, col,
    grad, bias_sum, came0, came1, from_item0, from_item1, from_tm0, from_tm1,
    mask_ref, edge_mask_ref, invn_ref, stat, back, st_src, st_buf,
    edge_src, edge_in, x_edge, dp_edge, first_edge, act_edge, soft_edge, conv_edge,
    sem_s, sem_w, sem_x, sem_xr, sem_g, sem_es, sem_er, sem_ss, sem_sr, sem_hs, sem_hr, sem_o, sem_or, sem_m, sem_mr,
    sem_k, sem_kr, sem_ri, sem_rir, sem_rt, sem_rtr, sem_at, sem_atr, sem_ai, sem_air, sem_f,
):
    n_tm, n_item, NI, H, B, F = dims
    R = ROWS
    W = F + 2 * DILATION
    MID = slice(DILATION, DILATION + F)
    half = B // 2
    s = lax.axis_index("section")
    t = lax.axis_index("tm")
    o = 1 - s
    left = t - 1
    right = t + 1
    last = n_tm - 1
    first_item = s * NI
    lane = lax.broadcasted_iota(jnp.int32, (R, LANES), 1)
    lane8 = lax.broadcasted_iota(jnp.int32, (8, LANES), 1)

    it = lax.axis_index("item")
    members = n_tm * n_item
    me = t * n_item + it
    n_src = sources_h.shape[0]

    def load_source(n):
        return pltpu.make_async_copy(sources_h.at[n], soft2.at[1, n], sem_s.at[n])

    for n in range(n_src):
        load_source(n).start()
    load_out = pltpu.make_async_copy(gout_h.at[pl.ds(first_item, NI)], dp.at[:, pl.ds(0, B)], sem_g.at[0])
    load_skip = pltpu.make_async_copy(gskip_h.at[pl.ds(first_item, NI)], dp.at[:, pl.ds(B, B)], sem_g.at[1])
    load_out.start()
    load_skip.start()
    edge_in[...] = jnp.zeros(edge_in.shape, BF16)

    barrier = pltpu.get_barrier_semaphore()

    def greet(d, c):
        peer = lax.rem(me + d, members)
        device = {"tm": peer // n_item, "item": lax.rem(peer, n_item)}
        pl.semaphore_signal(barrier, inc=1, device_id=device, device_id_type=MESH)
        return c

    def greet_other(d, c):
        device = {"section": o, "tm": lax.rem(t + d, n_tm)}
        pl.semaphore_signal(barrier, inc=1, device_id=device, device_id_type=MESH)
        return c

    lax.fori_loop(1, members, greet, 0)
    lax.fori_loop(0, n_tm, greet_other, 0)

    w_in = w_in_ref[...]
    w_out = w_out_ref[...].astype(F32)
    wpre[s] = w_in
    win[s] = w_in.astype(F32).T.astype(BF16)
    wout[s] = w_out.T.astype(BF16)
    gained = (w_out * chan_ref[9]).astype(BF16)
    wg[s] = gained
    wide_s[0:LANES, 0:H] = jnp.zeros((LANES, H), F32)
    for j in range(chan_ref.shape[0]):
        wide_s[j : j + 1, 0:H] = chan_ref[j]
    chan[s] = wide_s[0:LANES, 0:H].T
    bias = jnp.broadcast_to(b_out_ref[...], (LANES, 2 * B)).T
    bias += jnp.sum(w_out * chan_ref[10], axis=1, keepdims=True)
    gain = jnp.sum(gained.astype(F32), axis=1, keepdims=True)
    lane_w = lax.broadcasted_iota(jnp.int32, (2 * B, LANES), 1)
    col[s] = jnp.where(lane_w == 0, bias, gain)

    for i in range(NI):
        length = lengths[first_item + i]
        where = lax.broadcasted_iota(jnp.int32, (8, W), 1) + (t * F - DILATION)
        mask_ref[i] = jnp.where((where >= 0) & (where < length), 1.0, 0.0)
        invn_ref[i] = 1.0 / (jnp.full((8, LANES), length, jnp.int32).astype(F32) * H)
    within = lane8 % 32
    frame = t * F + jnp.where(within < 16, within - 2, within - 17 + F)
    length = jnp.full((8, LANES), lengths[first_item], jnp.int32)
    for i in range(1, NI):
        length = jnp.where(lane8 >= 32 * i, lengths[first_item + i], length)
    held = (within < 3) | ((within >= 16) & (within < 19))
    edge_mask_ref[...] = jnp.where(held & (frame >= 0) & (frame < length), 1.0, 0.0)

    for n in range(n_src):
        load_source(n).wait()

    def mix_item(i, c):
        rows = pl.ds(pl.multiple_of(i * half, half), half)
        where = lax.broadcasted_iota(jnp.int32, (8, F), 1) + t * F
        m = tall(jnp.where(where < lengths[i], 1.0, 0.0), half)
        total = jnp.zeros((half, F), F32)
        for n in range(n_src):
            total += soft2[1, n, rows, :].astype(F32) * jnp.where(n < counts[i], 1.0, 0.0)
        stage[i] = (total * m).astype(BF16)
        return c

    lax.fori_loop(0, 2 * NI, mix_item, 0)

    pl.semaphore_wait(barrier, members - 1 + n_tm)

    own_rows = pl.ds(pl.multiple_of(s * half, half), half)
    other_rows = pl.ds(pl.multiple_of(o * half, half), half)
    items_of = lambda core: pl.ds(core * NI, NI)
    centre = pl.ds(DILATION, F)
    head, tail = pl.ds(0, DILATION), pl.ds(F + DILATION, DILATION)

    main_local = pltpu.make_async_copy(stage.at[items_of(s)], x0.at[:, own_rows, centre], sem_x.at[0])
    main_send = remote(
        stage.at[items_of(o)], x0.at[:, own_rows, centre], sem_x.at[1], sem_xr.at[0], {"section": o}
    )
    main_recv = remote(
        stage.at[items_of(o)], x0.at[:, other_rows, centre], sem_x.at[1], sem_xr.at[0], {"section": o}
    )

    def halo_send(side, core):
        edge = pl.ds(0, DILATION) if side == 0 else pl.ds(F - DILATION, DILATION)
        place = tail if side == 0 else head
        return remote(
            stage.at[items_of(core), :, edge],
            x0.at[:, own_rows, place],
            sem_x.at[2 + 2 * side + core],
            sem_xr.at[1 + 2 * side + s],
            {"section": core, "tm": left if side == 0 else right},
        )

    def halo_recv(side, core):
        place = tail if side == 0 else head
        rows = pl.ds(core * half, half)
        return remote(
            x0.at[:, rows, place], x0.at[:, rows, place], sem_x.at[0], sem_xr.at[1 + 2 * side + core], {"section": o}
        )

    main_local.start()
    main_send.start()

    @pl.when(t > 0)
    def _():
        for core in (0, 1):
            halo_send(0, core).start()

    @pl.when(t < last)
    def _():
        for core in (0, 1):
            halo_send(1, core).start()

    weights = (wpre, chan, wg, col, wout, win)

    def weight_copies(j):
        ref = weights[j]
        return (
            remote(ref.at[s], ref.at[s], sem_w.at[j, 0], sem_w.at[j, 1], {"section": o}),
            remote(ref.at[o], ref.at[o], sem_w.at[j, 0], sem_w.at[j, 1], {"section": o}),
        )

    for j in range(len(weights)):
        weight_copies(j)[0].start()

    def wait_weights(*which):
        for j in which:
            send, recv = weight_copies(j)
            recv.wait_recv()
            send.wait_send()

    @pl.when(t == 0)
    def _():
        x0[:, :, 0:DILATION] = jnp.zeros((NI, B, DILATION), BF16)

    @pl.when(t == last)
    def _():
        x0[:, :, F + DILATION : W] = jnp.zeros((NI, B, DILATION), BF16)

    grad[...] = jnp.zeros(grad.shape, F32)
    bias_sum[...] = jnp.zeros(bias_sum.shape, F32)

    def stat_copy(ph, i, d, to):
        p = ph % 2
        return remote(
            st_src.at[p, i], st_buf.at[p, i, d - 1], sem_ss.at[p, i, d - 1], sem_sr.at[p, i, d - 1], {"tm": to}
        )

    def send_stats(ph, i, a, b):
        rows = [jnp.sum(a, axis=0, keepdims=True), jnp.sum(b, axis=0, keepdims=True)]
        st_src[ph % 2, i] = jnp.concatenate(rows + [jnp.zeros((6, LANES), F32)], axis=0)

        def one(d, c):
            stat_copy(ph, i, d, lax.rem(t + d, n_tm)).start()
            return c

        lax.fori_loop(1, n_tm, one, 0)

    def recv_stats(ph, i):
        def one(d, total):
            copy = stat_copy(ph, i, d, lax.rem(t + d, n_tm))
            copy.wait_send()
            copy.wait_recv()
            return total + st_buf[ph % 2, i, d - 1]

        total = lax.fori_loop(1, n_tm, one, st_src[ph % 2, i])
        sums = jnp.sum(total, axis=1, keepdims=True)
        return (
            jnp.broadcast_to(sums[0:1], (8, LANES)),
            jnp.broadcast_to(sums[1:2], (8, LANES)),
        )

    def finish_norm(ph, slot, i):
        a, b = recv_stats(ph, i)
        inv_n = invn_ref[i]
        mean = a * inv_n
        spread = jnp.maximum(b * inv_n - mean * mean, 0.0)
        stat[slot, i, 0] = mean
        stat[slot, i, 1] = lax.rsqrt(spread + EPSILON / (LN2 * LN2))

    def finish_back(ph, slot, i):
        a, b = recv_stats(ph, i)
        inv_n = invn_ref[i]
        mean, inv = stat[slot, i, 0], stat[slot, i, 1]
        q = b * inv_n * inv
        back[i, 0] = (mean * q - a * inv_n) * (inv * LOG2E)
        back[i, 1] = -q * (inv * LOG2E)

    def lanes_of(ref, j):
        out = ref[0, j]
        for i in range(1, NI):
            out = jnp.where(lane8 >= 32 * i, ref[i, j], out)
        return out

    def per_item(body):
        lax.fori_loop(0, NI, lambda i, c: (body(i), c)[1], 0)

    def per_tile(body, count=H, rows=R, init=0):
        return lax.fori_loop(0, count // rows, lambda j, c: body(rows_at(j, rows), c), init)

    def mask_row(i, rows, at=DILATION, width=F):
        return tall(mask_ref[i, :, at : at + width], rows)

    zero8 = jnp.zeros((8, LANES), F32)

    def pack_edges(src, channels, slot):
        def tile(r, c):
            to_left = to_right = own = jnp.zeros((R, LANES), F32)
            for i in range(NI):
                a = src[i, r, 0:LANES].astype(F32)
                z = src[i, r, F - LANES : F].astype(F32)
                base = 32 * i
                to_left += jnp.where(
                    (lane == base + 17) | (lane == base + 18), pltpu.roll(a, base + 17, 1), 0.0
                )
                to_right += jnp.where(
                    (lane == base) | (lane == base + 1), pltpu.roll(z, base + 2, 1), 0.0
                )
                own += jnp.where(lane == base + 2, pltpu.roll(a, base + 2, 1), 0.0)
                own += jnp.where(lane == base + 16, pltpu.roll(z, base + 17, 1), 0.0)
            edge_src[slot, 0, r, :] = to_left.astype(BF16)
            edge_src[slot, 1, r, :] = to_right.astype(BF16)
            edge_src[slot, 2, r, :] = own.astype(BF16)
            return c

        per_tile(tile, channels)

    def edge_copy(slot, side, channels):
        rows = pl.ds(0, channels)
        return remote(
            edge_src.at[slot, side, rows],
            edge_in.at[slot, side, rows],
            sem_es.at[slot, side],
            sem_er.at[slot, side],
            {"tm": left if side == 0 else right},
        )

    def send_edges(slot, channels):
        @pl.when(t > 0)
        def _():
            edge_copy(slot, 0, channels).start()

        @pl.when(t < last)
        def _():
            edge_copy(slot, 1, channels).start()

    def recv_edges(slot, channels, dst):
        @pl.when(t > 0)
        def _():
            edge_copy(slot, 0, channels).wait_send()
            edge_copy(slot, 1, channels).wait_recv()

        @pl.when(t < last)
        def _():
            edge_copy(slot, 1, channels).wait_send()
            edge_copy(slot, 0, channels).wait_recv()

        def tile(r, c):
            total = edge_src[slot, 2, r, :].astype(F32)
            for side in (0, 1):
                total += edge_in[slot, side, r, :].astype(F32)
            dst[r, :] = total.astype(BF16)
            return c

        per_tile(tile, channels)

    def rectify(neg, rest):
        soft = jnp.maximum(neg, jnp.log2(1.0 + jnp.exp2(jnp.minimum(neg, 100.0))))
        return rest * soft - neg, soft

    def masked_sums(a, m, sums):
        am = a * m
        return (sums[0] + fold_rows(fold(am)), sums[1] + fold_rows(fold(am * a)))

    def phase1(k):
        R = ROWS1
        width = W if k == 0 else F
        x = x0 if k == 0 else x1
        act = act1_0 if k == 0 else act1_1
        mid = MID if k == 0 else slice(0, F)

        def item(i):
            wide_s[:, 0:width] = dot(wpre[k], x[i])
            m = mask_row(i, R)

            def tile(r, sums):
                table = chan[k, r, :]
                bias = column(table, 0) * -LOG2E
                rest = 1.0 - column(table, 1)
                neg = wide_s[r, 0:width] * -LOG2E + wide(bias, width)
                a, soft = rectify(neg, wide(rest, width))
                act[i, r, :] = a.astype(BF16)
                soft1[k, i, r, :] = soft[:, mid].astype(BF16)
                return masked_sums(a[:, mid], m, sums)

            a, b = per_tile(tile, rows=R, init=(zero8, zero8))
            send_stats(4 * k, i, a, b)

        per_item(item)
        if k == 1:
            recv_edges(1, B, x_edge)
            wide_s[:, 0:LANES] = dot(wpre[1], x_edge[...])

            def tile(r, c):
                table = chan[1, r, :]
                neg = wide_s[r, 0:LANES] * -LOG2E + column(table, 0) * -LOG2E
                a, _ = rectify(neg, 1.0 - column(table, 1))
                wide_s[r, 0:LANES] = a
                return c

            per_tile(tile, rows=R)

    def phase2(k):
        R = ROWS2
        width = W if k == 0 else F
        at = 0 if k == 0 else DILATION
        act = act1_0 if k == 0 else act1_1

        def item(i):
            finish_norm(4 * k, 2 * k, i)
            mean, inv = tall(stat[2 * k, i, 0], R), tall(stat[2 * k, i, 1], R)
            m = mask_row(i, R, at, width)

            def tile(r, c):
                table = chan[k, r, :]
                scale = inv * column(table, 2)
                shift = column(table, 3) - mean * scale
                a = act[i, r, :].astype(F32)
                buf[i, r, at : at + width] = (
                    (a * wide(scale, width) + wide(shift, width)) * m
                ).astype(BF16)
                return c

            per_tile(tile, rows=R)

        per_item(item)
        if k == 1:
            mean, inv = tall(lanes_of(stat.at[2], 0), R), tall(lanes_of(stat.at[2], 1), R)
            m = tall(edge_mask_ref[...], R)

            def tile(r, c):
                table = chan[1, r, :]
                scale = inv * column(table, 2)
                a = wide_s[r, 0:LANES]
                first_edge[r, :] = (((a - mean) * scale + column(table, 3)) * m).astype(BF16)
                return c

            per_tile(tile, rows=R)

    def neighbours(f, edge, i):
        shifted_in = pltpu.roll(edge, lax.rem(127 - 32 * i + 256, 128), 1)
        before = pltpu.roll(f, 1, 1)
        lane = lax.broadcasted_iota(jnp.int32, edge.shape, 1)
        lead = jnp.where(lane == 0, shifted_in, before[:, 0:LANES])
        before = jnp.concatenate([lead, before[:, LANES:]], axis=1)
        shifted_in = pltpu.roll(edge, lax.rem(110 - 32 * i + 256, 128), 1)
        after = pltpu.roll(f, F - 1, 1)
        trail = jnp.where(lane == LANES - 1, shifted_in, after[:, F - LANES :])
        after = jnp.concatenate([after[:, : F - LANES], trail], axis=1)
        return before, after

    def taps(k, i, r, edge):
        f = buf[i, r, MID]
        if k == 0:
            return buf[i, r, 0:F], f, buf[i, r, 2 * DILATION : W]
        before, after = neighbours(f, edge[r, :], i)
        return before, f, after

    def conv_coefs(table):
        return [column(table, j) * -LOG2E for j in (4, 5, 6, 7)], 1.0 - column(table, 8)

    def phase3(k):
        R = ROWS3
        def item(i):
            m = mask_row(i, R)

            def tile(r, sums):
                c, rest = conv_coefs(chan[k, r, :])
                before, f, after = (v.astype(F32) for v in taps(k, i, r, first_edge))
                neg = wide(c[0], F) * before + wide(c[1], F) * f + wide(c[2], F) * after + wide(c[3], F)
                a, soft = rectify(neg, wide(rest, F))
                act2[k, i, r, :] = a.astype(BF16)
                soft2[k, i, r, :] = soft.astype(BF16)
                return masked_sums(a, m, sums)

            a, b = per_tile(tile, rows=R, init=(zero8, zero8))
            send_stats(4 * k + 1, i, a, b)

        per_item(item)
        if k == 1:

            def tile(r, x):
                c, rest = conv_coefs(chan[1, r, :])
                f = first_edge[r, :].astype(F32)
                neg = c[0] * pltpu.roll(f, 1, 1) + c[1] * f + c[2] * pltpu.roll(f, LANES - 1, 1) + c[3]
                a, soft = rectify(neg, rest)
                act_edge[r, :] = a.astype(BF16)
                soft_edge[r, :] = soft.astype(BF16)
                return x

            per_tile(tile, rows=R)

    def out_copies(kind, k, i):
        row = first_item + i
        if kind == 0 and k == 1:
            pairs = [
                (stage.at[2 * i + j], block_h.at[row, pl.ds(j * half, half)], sem_o.at[2 * j, 1, i], sem_or.at[2 * j, i])
                for j in (0, 1)
            ]
        else:
            src, dst = ((x1, block_h), (skips, skip_h))[kind]
            pairs = [(src.at[i], dst.at[row], sem_o.at[kind, k, i], sem_or.at[kind, i])]
        return [
            (pltpu.make_async_copy(a, b, sem), remote(a, b, sem, there, {"section": o})) for a, b, sem, there in pairs
        ]

    def start_out(kind, k, i):
        for here, there in out_copies(kind, k, i):
            pl.when(s == k)(lambda: here.start())
            pl.when(s != k)(lambda: there.start())

    def wait_out(kind, k, i):
        for here, there in out_copies(kind, k, i):
            pl.when(s == k)(lambda: here.wait())
            pl.when(s != k)(lambda: there.wait_send())

    def wait_came(i):
        row = o * NI + i
        skip_in = remote(skips.at[i], skip_h.at[row], sem_o.at[1, 0, i], sem_or.at[1, i], {"section": o})
        skip_in.wait_recv()

        @pl.when(s == 0)
        def _():
            remote(x1.at[i], block_h.at[row], sem_o.at[0, 0, i], sem_or.at[0, i], {"section": o}).wait_recv()

        @pl.when(s == 1)
        def _():
            for j in (0, 1):
                dst = block_h.at[row, pl.ds(j * half, half)]
                remote(stage.at[0], dst, sem_o.at[2 * j, 1, i], sem_or.at[2 * j, i], {"section": o}).wait_recv()

    def phase4(k):
        R = ROWS4
        x = x0 if k == 0 else x1
        mid = MID if k == 0 else slice(0, F)

        def item(i):
            finish_norm(4 * k + 1, 2 * k + 1, i)
            mean, inv = tall(stat[2 * k + 1, i, 0], B), tall(stat[2 * k + 1, i, 1], B)
            m = mask_row(i, B)
            y = pl.ds(0, 2 * B)
            wide_s[y, 0:F] = dot(wg[k], act2[k, i])

            def project(r):
                table = col[k, r, :]
                shift = column(table, 0) - mean * inv * column(table, 1)
                return (wide_s[r, 0:F] * wide(inv, F) + wide(shift, F)) * m

            total = (x[i, :, mid].astype(F32) + project(pl.ds(0, B))).astype(BF16)
            if k == 0:
                x1[i] = total
            else:
                stage[2 * i] = total[0:half]
                stage[2 * i + 1] = total[half:]

            p = project(pl.ds(B, B))
            if k == 1:
                wait_out(1, 0, i)
                p += skips[i].astype(F32)
            skips[i] = p.astype(BF16)
            start_out(0, k, i)
            start_out(1, k, i)

        per_item(item)

    def phase5(k):
        R = ROWS5
        R5 = ROWS5

        def item(i):
            mean, inv = tall(stat[2 * k + 1, i, 0], R5), tall(stat[2 * k + 1, i, 1], R5)
            wide_s[:, 0 : 2 * B] = dot(act2[k, i], dp[i], NT)
            total8 = dot(jnp.ones((8, F), BF16), dp[i], NT)
            bias_sum[k] += total8
            total = tall(total8, R5)

            def tile(r, sums):
                table = chan[k, r, :]
                g, e = column(table, 9), column(table, 10)
                product = wide_s[r, 0 : 2 * B]
                w = wout[k, r, :].astype(F32)
                against = fold(w * product)
                plain = fold(w * total)
                normed = inv * (against - mean * plain)
                gacc[9, r, :] += normed
                gacc[10, r, :] += plain
                scale = inv * g
                shift = e - mean * scale
                step = wide(scale, 2 * B) * product + wide(shift, 2 * B) * total
                grad[k, r, :] += step[:, :B]
                grad[k, pl.ds(H + r.start, R5), :] += step[:, B:]
                return (sums[0] + fold_rows(g * plain), sums[1] + fold_rows(g * normed))

            a, b = per_tile(tile, rows=R5, init=(zero8, zero8))
            send_stats(4 * k + 2, i, a, b)

        per_item(item)

    def halo_copy(i, side):
        edge = pl.ds(DILATION, DILATION) if side == 0 else pl.ds(F, DILATION)
        return remote(
            buf.at[i, :, edge],
            buf.at[i, :, tail if side == 0 else head],
            sem_hs.at[side, i],
            sem_hr.at[side, i],
            {"tm": left if side == 0 else right},
        )

    def phase6(k):
        R = ROWS6
        def item(i):
            finish_back(4 * k + 2, 2 * k + 1, i)
            inv = tall(stat[2 * k + 1, i, 1], R) * LOG2E
            p, q = wide(tall(back[i, 0], R), F), wide(tall(back[i, 1], R), F)
            m = mask_row(i, R)
            wide_s[:, 0:F] = dot(wout[k], dp[i])

            def tile(r, c):
                table = chan[k, r, :]
                slope = column(table, 8)
                g = inv * column(table, 9)
                d_act = low(wide_s[r, 0:F] * wide(g, F) + m * (p + q * act2[k, i, r, :].astype(F32)))
                soft = soft2[k, i, r, :]
                d_conv = d_act * (wide(low(slope), F) + wide(low(1.0 - slope), F) * jnp.exp2(-soft))
                gacc[8, r, :] += fold(d_act * soft).astype(F32) * -LN2
                gacc[7, r, :] += fold(d_conv).astype(F32)
                buf[i, r, MID] = d_conv
                return c

            per_tile(tile, rows=R)
            if k == 0:

                @pl.when(t > 0)
                def _():
                    halo_copy(i, 0).start()

                @pl.when(t < last)
                def _():
                    halo_copy(i, 1).start()

                @pl.when(t == 0)
                def _():
                    buf[i, :, 0:DILATION] = jnp.zeros((H, DILATION), BF16)

                @pl.when(t == last)
                def _():
                    buf[i, :, F + DILATION : W] = jnp.zeros((H, DILATION), BF16)

        per_item(item)
        if k == 1:
            wide_s[:, 0:LANES] = dot(wout[1], dp_edge[...])
            inv = tall(lanes_of(stat.at[3], 1), R) * LOG2E
            p, q = tall(lanes_of(back, 0), R), tall(lanes_of(back, 1), R)
            m = tall(edge_mask_ref[...], R)

            def tile(r, c):
                table = chan[1, r, :]
                slope = column(table, 8)
                d_act = wide_s[r, 0:LANES] * (inv * column(table, 9)) + m * (p + q * act_edge[r, :].astype(F32))
                d_conv = d_act * (slope + (1.0 - slope) * jnp.exp2(-soft_edge[r, :].astype(F32)))
                conv_edge[r, :] = d_conv.astype(BF16)
                return c

            per_tile(tile, rows=R)

    def phase7(k):
        R = ROWS7
        act = act1_0 if k == 0 else act1_1
        mid = MID if k == 0 else slice(0, F)

        def item(i):
            if k == 0:

                @pl.when(t > 0)
                def _():
                    halo_copy(i, 0).wait_send()
                    halo_copy(i, 1).wait_recv()

                @pl.when(t < last)
                def _():
                    halo_copy(i, 1).wait_send()
                    halo_copy(i, 0).wait_recv()

            mean, inv = tall(stat[2 * k, i, 0], R), tall(stat[2 * k, i, 1], R)
            m = low(mask_row(i, R))

            def tile(r, sums):
                table = chan[k, r, :]
                g = column(table, 2)
                scale = inv * g
                shift = column(table, 3) - mean * scale
                before, d, after = taps(k, i, r, conv_edge)
                u = (
                    wide(low(column(table, 4)), F) * after
                    + wide(low(column(table, 5)), F) * d
                    + wide(low(column(table, 6)), F) * before
                ) * m
                a = act[i, r, mid]
                first = (a * wide(low(scale), F) + wide(low(shift), F)) * m
                plain = fold(u).astype(F32)
                normed = inv * (fold(u * a).astype(F32) - mean * plain)
                gacc[2, r, :] += normed
                gacc[3, r, :] += plain
                gacc[4, r, :] += fold(after * first).astype(F32)
                gacc[5, r, :] += fold(d * first).astype(F32)
                gacc[6, r, :] += fold(before * first).astype(F32)
                soft2[k, i, r, :] = u
                return (sums[0] + fold_rows(g * plain), sums[1] + fold_rows(g * normed))

            a, b = per_tile(tile, rows=R, init=(zero8, zero8))
            send_stats(4 * k + 3, i, a, b)

        per_item(item)

    def mix_copy(i):
        row = first_item + i
        return (
            pltpu.make_async_copy(stage.at[2 * i + s], gmix_h.at[row], sem_m.at[0, i]),
            remote(stage.at[2 * i + o], gmix_h.at[row], sem_m.at[1, i], sem_mr.at[i], {"section": o}),
        )

    def phase8(k):
        R = ROWS8
        act = act1_0 if k == 0 else act1_1
        x = x0 if k == 0 else x1
        mid = MID if k == 0 else slice(0, F)

        def item(i):
            finish_back(4 * k + 3, 2 * k, i)
            inv = tall(stat[2 * k, i, 1], R) * LOG2E
            p, q = wide(tall(back[i, 0], R), F), wide(tall(back[i, 1], R), F)
            m = mask_row(i, R)

            def tile(r, c):
                table = chan[k, r, :]
                slope = column(table, 1)
                g = inv * column(table, 2)
                d_act = low(soft2[k, i, r, :].astype(F32) * wide(g, F) + m * (p + q * act[i, r, mid].astype(F32)))
                soft = soft1[k, i, r, :]
                d_pre = d_act * (wide(low(slope), F) + wide(low(1.0 - slope), F) * jnp.exp2(-soft))
                gacc[1, r, :] += fold(d_act * soft).astype(F32) * -LN2
                gacc[0, r, :] += fold(d_pre).astype(F32)
                buf[i, r, MID] = d_pre
                return c

            per_tile(tile, rows=R)
            grad[k, 2 * H : 3 * H] += dot(buf[i, :, MID], x[i, :, mid], NT)

            if k == 1:
                input_gradient(1, i)

        per_item(item)

    def input_gradient(k, i):
        wide_s[0:B, 0:F] = dot(win[k], buf[i, :, MID])
        m = mask_row(i, B)
        d_input = (wide_s[0:B, 0:F] + dp[i, 0:B, :].astype(F32)) * m
        if k == 1:
            dp[i, 0:B, :] = d_input.astype(BF16)
        else:
            stage[2 * i] = d_input[0:half].astype(BF16)
            stage[2 * i + 1] = d_input[half:].astype(BF16)
            here, there = mix_copy(i)
            there.start()
            here.start()

    rows_at_part = ((0, 2 * H), (2 * H, grad.shape[1]))
    came = (came0, came1)
    slots = ((from_item0, from_tm0), (from_item1, from_tm1))

    def sizes(part):
        big, chunk = slots[part][0].shape[1], slots[part][1].shape[1]
        return big, chunk, big // chunk

    def item_peer(d):
        return lax.rem(it + d, n_item)

    def tm_peer(d):
        return lax.rem(t + d, n_tm)

    def each(count, body):
        lax.fori_loop(1, count, lambda d, c: (body(d), c)[1], 0)

    def at_part(part, k, start, rows):
        return grad.at[k, pl.ds(rows_at_part[part][0] + start, rows)]

    def to_owner(part, k):
        a, b = rows_at_part[part]
        return remote(grad.at[k, pl.ds(a, b - a)], came[part], sem_k.at[part], sem_kr.at[part], {"section": o})

    def item_scatter(part, k, d):
        big = sizes(part)[0]
        src = at_part(part, k, item_peer(d) * big, big)
        return remote(
            src, slots[part][0].at[d - 1], sem_ri.at[part, d - 1], sem_rir.at[part, d - 1], {"item": item_peer(d)}
        )

    def tm_scatter(part, k, d):
        big, chunk, owners = sizes(part)
        src = at_part(part, k, it * big + lax.rem(tm_peer(d), owners) * chunk, chunk)
        return remote(
            src, slots[part][1].at[d - 1], sem_rt.at[part, d - 1], sem_rtr.at[part, d - 1], {"tm": tm_peer(d)}
        )

    def tm_gather(part, d, member):
        big, chunk, owners = sizes(part)
        rows = came[part].at[pl.ds(it * big + lax.rem(member, owners) * chunk, chunk)]
        return remote(rows, rows, sem_at.at[part, d - 1], sem_atr.at[part, d - 1], {"tm": tm_peer(d)})

    def item_gather(part, d, member):
        big = sizes(part)[0]
        rows = came[part].at[pl.ds(member * big, big)]
        return remote(rows, rows, sem_ai.at[part, d - 1], sem_air.at[part, d - 1], {"item": item_peer(d)})

    def sum_1(part, k):
        pl.when(s != k)(lambda: to_owner(part, k).start())

    def sum_2(part, k):
        pl.when(s != k)(lambda: to_owner(part, k).wait_send())

        @pl.when(s == k)
        def _():
            a, b = rows_at_part[part]
            to_owner(part, k).wait_recv()
            grad[k, a:b] += came[part][...]
            each(n_item, lambda d: item_scatter(part, k, d).start())

    def sum_3(part, k):
        big, chunk, owners = sizes(part)

        @pl.when(s == k)
        def _():
            each(n_item, lambda d: item_scatter(part, k, d).wait())
            mine = pl.ds(pl.multiple_of(rows_at_part[part][0] + it * big, 8), big)
            grad[k, mine] = lax.fori_loop(0, n_item - 1, lambda j, x: x + slots[part][0][j], grad[k, mine])
            each(n_tm, lambda d: pl.when(tm_peer(d) < owners)(lambda: tm_scatter(part, k, d).start()))

    def sum_4(part, k):
        big, chunk, owners = sizes(part)

        @pl.when(s == k)
        def _():
            def wait(d):
                pl.when(tm_peer(d) < owners)(lambda: tm_scatter(part, k, d).wait_send())
                pl.when(t < owners)(lambda: tm_scatter(part, k, d).wait_recv())

            each(n_tm, wait)

            @pl.when(t < owners)
            def _():
                start = it * big + t * chunk
                own = grad[k, pl.ds(pl.multiple_of(rows_at_part[part][0] + start, 8), chunk)]
                total = lax.fori_loop(0, n_tm - 1, lambda j, x: x + slots[part][1][j], own)
                came[part][pl.ds(pl.multiple_of(start, 8), chunk)] = total
                each(n_tm, lambda d: tm_gather(part, d, t).start())

    def sum_5(part, k):
        _, _, owners = sizes(part)

        @pl.when(s == k)
        def _():
            def wait(d):
                source = lax.rem(t - d + n_tm, n_tm)
                pl.when(t < owners)(lambda: tm_gather(part, d, t).wait_send())
                pl.when(source < owners)(lambda: tm_gather(part, d, source).wait_recv())

            each(n_tm, wait)
            each(n_item, lambda d: item_gather(part, d, it).start())

    def sum_6(part, k):
        @pl.when(s == k)
        def _():
            def wait(d):
                item_gather(part, d, it).wait_send()
                item_gather(part, d, lax.rem(it - d + n_item, n_item)).wait_recv()

            each(n_item, wait)

    def finish_block(k):
        group = H // 4
        lanes = lax.broadcasted_iota(jnp.int32, (group, LANES), 1)
        bias = jnp.broadcast_to(bias_sum[k, 0:1, :], (LANES, 2 * B)).T
        packed = jnp.zeros((group, LANES), F32)
        for g in range(4):
            for j in range(11):
                total = jnp.sum(gacc[j, g * group : (g + 1) * group, :], axis=1, keepdims=True)
                packed = jnp.where(lanes == 32 * g + j, total, packed)
            if (g + 1) * group <= 2 * B:
                packed = jnp.where(lanes == 32 * g + 11, bias[g * group : (g + 1) * group], packed)
        grad[k, 3 * H : 3 * H + group] = packed

    def mask_gradients(i):
        m = mask_row(i, R)

        def tile(r, c):
            dp[i, r, :] = (dp[i, r, :].astype(F32) * m).astype(BF16)
            return c

        per_tile(tile, 2 * B)

    wait_weights(0, 1)
    main_local.wait()
    main_send.wait_send()
    main_recv.wait_recv()

    @pl.when(t > 0)
    def _():
        for core in (0, 1):
            halo_send(0, core).wait_send()
            halo_recv(1, core).wait_recv()

    @pl.when(t < last)
    def _():
        for core in (0, 1):
            halo_send(1, core).wait_send()
            halo_recv(0, core).wait_recv()

    phase1(0)
    load_out.wait()
    load_skip.wait()

    per_item(mask_gradients)
    pack_edges(dp, 2 * B, 0)
    send_edges(0, 2 * B)
    phase2(0)
    phase3(0)
    wait_weights(2, 3)
    phase4(0)
    pack_edges(x1, B, 1)
    send_edges(1, B)
    phase1(1)
    phase2(1)
    phase3(1)
    phase4(1)
    recv_edges(0, 2 * B, dp_edge)
    wait_weights(4)
    gacc[...] = jnp.zeros(gacc.shape, F32)
    phase5(1)
    sum_1(0, 1)
    phase6(1)
    sum_2(0, 1)
    phase7(1)
    sum_3(0, 1)
    wait_weights(5)
    phase8(1)
    finish_block(1)
    sum_1(1, 1)
    sum_4(0, 1)
    gacc[...] = jnp.zeros(gacc.shape, F32)
    phase5(0)
    sum_1(0, 0)
    sum_2(1, 1)
    sum_5(0, 1)
    phase6(0)
    sum_2(0, 0)
    sum_3(1, 1)
    phase7(0)
    sum_3(0, 0)
    sum_4(1, 1)
    for i in range(NI):
        wait_out(0, 1, i)
    phase8(0)
    finish_block(0)
    sum_1(1, 0)
    sum_4(0, 0)
    sum_5(1, 1)
    per_item(lambda i: input_gradient(0, i))
    sum_2(1, 0)
    sum_5(0, 0)
    sum_3(1, 0)
    sum_4(1, 0)
    sum_5(1, 0)
    sum_6(0, 1)
    sum_6(1, 1)
    sum_6(0, 0)
    sum_6(1, 0)
    results = [
        pltpu.make_async_copy(came[part], grad_h.at[pl.ds(a, b - a)], sem_f.at[part])
        for part, (a, b) in enumerate(rows_at_part)
    ]
    for copy in results:
        copy.start()
    for copy in results:
        copy.wait()

    for i in range(NI):
        here, there = mix_copy(i)
        here.wait()
        there.wait_send()
        remote(
            stage.at[2 * i], gmix_h.at[o * NI + i], sem_m.at[1, i], sem_mr.at[i], {"section": o}
        ).wait_recv()
        wait_out(0, 0, i)
        wait_out(1, 1, i)
        wait_came(i)


def chunk_of(rows, members):
    chunk = -(-rows // members)
    chunk = -(-chunk // 8) * 8
    while rows % chunk:
        chunk += 8
    return chunk


def run(n_tm, n_item, sources, gout, gskip, w_in, chan, w_out, b_out, counts, lengths):
    n_src, flat, F = sources.shape
    items, B, _ = gout.shape
    NI = items // 2
    H = w_in.shape[0]
    W = F + 2 * DILATION
    half = B // 2
    rows0, rows1 = 2 * H, H + H // 4
    quarter0, quarter1 = rows0 // n_item, rows1 // n_item
    smem = pl.BlockSpec(memory_space=pltpu.SMEM)
    any_spec = pl.BlockSpec(memory_space=pl.ANY)
    vmem = pl.BlockSpec(memory_space=pltpu.VMEM)
    dma = pltpu.SemaphoreType.DMA
    shape = jax.ShapeDtypeStruct
    outs = (
        shape((items, B, F), BF16),
        shape((items, B, F), BF16),
        shape((items, half, F), BF16),
        shape((rows0 + rows1, LANES), F32),
    )
    scratch = [
        pltpu.VMEM((items, half, F), BF16),
        pltpu.VMEM((NI, B, W), BF16),
        pltpu.VMEM((NI, B, F), BF16),
        pltpu.VMEM((NI, B, F), BF16),
        pltpu.VMEM((NI, H, W), BF16),
        pltpu.VMEM((NI, H, F), BF16),
        pltpu.VMEM((2, NI, H, F), BF16),
        pltpu.VMEM((2, NI, H, F), BF16),
        pltpu.VMEM((2, NI, H, F), BF16),
        pltpu.VMEM((NI, H, W), BF16),
        pltpu.VMEM((H, W), F32),
        pltpu.VMEM((NI, 2 * B, F), BF16),
        pltpu.VMEM((11, H, LANES), F32),
        pltpu.VMEM((2, H, B), BF16),
        pltpu.VMEM((2, H, 2 * B), BF16),
        pltpu.VMEM((2, 2 * B, H), BF16),
        pltpu.VMEM((2, B, H), BF16),
        pltpu.VMEM((2, H, LANES), F32),
        pltpu.VMEM((2, 2 * B, LANES), F32),
        pltpu.VMEM((2, rows0 + rows1, LANES), F32),
        pltpu.VMEM((2, 8, 2 * B), F32),
        pltpu.VMEM((rows0, LANES), F32),
        pltpu.VMEM((rows1, LANES), F32),
        pltpu.VMEM((n_item - 1, quarter0, LANES), F32),
        pltpu.VMEM((n_item - 1, quarter1, LANES), F32),
        pltpu.VMEM((n_tm - 1, chunk_of(quarter0, n_tm), LANES), F32),
        pltpu.VMEM((n_tm - 1, chunk_of(quarter1, n_tm), LANES), F32),
        pltpu.VMEM((NI, 8, W), F32),
        pltpu.VMEM((8, LANES), F32),
        pltpu.VMEM((NI, 8, LANES), F32),
        pltpu.VMEM((4, NI, 2, 8, LANES), F32),
        pltpu.VMEM((NI, 2, 8, LANES), F32),
        pltpu.VMEM((2, NI, 8, LANES), F32),
        pltpu.VMEM((2, NI, n_tm - 1, 8, LANES), F32),
        pltpu.VMEM((2, 3, 2 * B, LANES), BF16),
        pltpu.VMEM((2, 2, 2 * B, LANES), BF16),
        pltpu.VMEM((B, LANES), BF16),
        pltpu.VMEM((2 * B, LANES), BF16),
        pltpu.VMEM((H, LANES), BF16),
        pltpu.VMEM((H, LANES), BF16),
        pltpu.VMEM((H, LANES), BF16),
        pltpu.VMEM((H, LANES), BF16),
        dma((n_src,)),
        dma((6, 2)),
        dma((6,)),
        dma((5,)),
        dma((2,)),
        dma((2, 2)),
        dma((2, 2)),
        dma((2, NI, n_tm - 1)),
        dma((2, NI, n_tm - 1)),
        dma((2, NI)),
        dma((2, NI)),
        dma((3, 2, NI)),
        dma((3, NI)),
        dma((2, NI)),
        dma((NI,)),
        dma((2,)),
        dma((2,)),
        dma((2, n_item - 1)),
        dma((2, n_item - 1)),
        dma((2, n_tm - 1)),
        dma((2, n_tm - 1)),
        dma((2, n_tm - 1)),
        dma((2, n_tm - 1)),
        dma((2, n_item - 1)),
        dma((2, n_item - 1)),
        dma((2,)),
    ]
    return pl.pallas_call(
        functools.partial(kernel, (n_tm, n_item, NI, H, B, F)),
        out_shape=outs,
        in_specs=[any_spec] * 3 + [vmem] * 4 + [smem] * 2,
        out_specs=[any_spec] * len(outs),
        scratch_shapes=scratch,
        compiler_params=pltpu.CompilerParams(
            collective_id=0, has_side_effects=True, vmem_limit_bytes=VMEM_LIMIT
        ),
        name="temporal_blocks",
    )(sources, gout, gskip, w_in, chan, w_out, b_out, counts, lengths)


def close_kernel(
    block_in, skip_in, gmix_in, grad_in, counts,
    block_h, skip_h, sources_h, w_in_out, chan_out, w_out_out, b_out_out,
    held, mixed, full, nothing, sem_a, sem_b, sem_g, sem_s,
):
    items = gmix_in.shape[0]
    H = w_in_out.shape[0]
    B = w_in_out.shape[1]
    n_src = sources_h.shape[0]
    plain = [(j, i) for i in range(items) for j in (0, 1)]

    def fetch(j, i):
        return pltpu.make_async_copy((block_in, skip_in)[j].at[i], held.at[j, i], sem_a.at[j, i])

    def store(j, i):
        return pltpu.make_async_copy(held.at[j, i], (block_h, skip_h)[j].at[i], sem_b.at[j, i])

    loads = [pltpu.make_async_copy(gmix_in.at[i], mixed.at[i], sem_g.at[i]) for i in range(items)]
    for copy in loads:
        copy.start()
    for j, i in plain:
        fetch(j, i).start()
    nothing[...] = jnp.zeros(nothing.shape, F32)
    for i in range(items):
        loads[i].wait()
        full[i] = mixed[i].astype(F32)
        for n in range(n_src):

            @pl.when(n < counts[i])
            def _():
                pltpu.make_async_copy(full.at[i], sources_h.at[n, i], sem_s.at[n, i]).start()

            @pl.when(n >= counts[i])
            def _():
                pltpu.make_async_copy(nothing, sources_h.at[n, i], sem_s.at[n, i]).start()

    for j, i in plain:
        fetch(j, i).wait()
        store(j, i).start()
    w_out_out[0:B, :] = grad_in[0:H, :].T
    w_out_out[B : 2 * B, :] = grad_in[H : 2 * H, :].T
    w_in_out[...] = grad_in[2 * H : 3 * H, :]
    rows = grad_in[3 * H : 3 * H + H // 4, :].T
    for j in range(chan_out.shape[0]):
        chan_out[j] = jnp.concatenate([rows[32 * g + j : 32 * g + j + 1] for g in range(4)], axis=1)
    b_out_out[...] = jnp.concatenate([rows[32 * g + 11 : 32 * g + 12] for g in range(2 * B * 4 // H)], axis=1)
    for j, i in plain:
        store(j, i).wait()
    for i in range(items):
        for n in range(n_src):
            pltpu.make_async_copy(full.at[i], sources_h.at[n, i], sem_s.at[n, i]).wait()


def close(n_src, n_rows, block, skip, gmix, grad, counts):
    items, half, F = gmix.shape
    B = 2 * half
    H = (grad.shape[0] * 4) // 13
    any_spec = pl.BlockSpec(memory_space=pl.ANY)
    vmem = pl.BlockSpec(memory_space=pltpu.VMEM)
    dma = pltpu.SemaphoreType.DMA
    shape = jax.ShapeDtypeStruct
    return pl.pallas_call(
        close_kernel,
        out_shape=(
            shape(block.shape, BF16),
            shape(skip.shape, BF16),
            shape((n_src, items, half, F), F32),
            shape((H, B), F32),
            shape((n_rows, 1, H), F32),
            shape((2 * B, H), F32),
            shape((1, 2 * B), F32),
        ),
        in_specs=[any_spec] * 3 + [vmem, pl.BlockSpec(memory_space=pltpu.SMEM)],
        out_specs=[any_spec] * 3 + [vmem] * 4,
        scratch_shapes=[
            pltpu.VMEM((2, items, B, F), BF16),
            pltpu.VMEM((items, half, F), BF16),
            pltpu.VMEM((items, half, F), F32),
            pltpu.VMEM((half, F), F32),
            dma((2, items)),
            dma((2, items)),
            dma((items,)),
            dma((n_src, items)),
        ],
        compiler_params=pltpu.CompilerParams(vmem_limit_bytes=VMEM_LIMIT),
        name="lay_out",
    )(block, skip, gmix, grad, counts)


def local(sources, source_counts, valid_lengths, w_in, chan, w_out, b_out, grad_out, grad_skip):
    n_sources, per_device, half, F = sources.shape
    block_out, skip_out, gmix, grad = run(
        lax.axis_size("tm"),
        lax.axis_size("item"),
        sources.reshape(n_sources, per_device * half, F),
        grad_out,
        grad_skip,
        w_in[0],
        chan.transpose(1, 0, 2),
        w_out[0],
        b_out,
        source_counts,
        valid_lengths,
    )
    block_out, skip_out, grad_sources, grad_w_in, grad_chan, grad_w_out, grad_b_out = close(
        n_sources, chan.shape[1], block_out, skip_out, gmix, grad, source_counts
    )
    return (
        block_out[None],
        skip_out[None],
        grad_sources,
        grad_w_in[None],
        grad_chan.transpose(1, 0, 2),
        grad_w_out[None],
        grad_b_out,
    )


def solution(mesh):
    in_specs = (
        P(None, "item", "section", "tm"),
        P("item"),
        P("item"),
        P("section", None, None),
        P("section", None, None),
        P("section", None, None),
        P("section", None),
        P("item", None, "tm"),
        P("item", None, "tm"),
    )
    out_specs = (
        P("section", "item", None, "tm"),
        P("section", "item", None, "tm"),
        P(None, "item", "section", "tm"),
        P("section", None, None),
        P("section", None, None),
        P("section", None, None),
        P("section", None),
    )
    return jax.shard_map(local, mesh=mesh, in_specs=in_specs, out_specs=out_specs, check_vma=False)
```

time: 273 us -> 135 us (0.49)
  blocking collectives: 75.6 us -> 0 us
  waiting for transfers between devices: 27.1 us -> 0 us
  local copies, waits for them, and re-layouts: 17.1 us -> 0 us
  other arithmetic: 14.1 us -> 0 us
  between operations: 14.1 us -> 0.8 us
  Pallas kernels: 125 us -> 135 us
    psum x1 -> x0, blocking collectives: 75.6 us -> none  [local(): gwi, gwo, gch, gb = lax.psum((gwi, gwo, gch[:11], gb[0]), ('tm', 'item'))]
    psum x1 -> x0, waiting for transfers between devices: 27.1 us -> none  [local(): gwi, gwo, gch, gb = lax.psum((gwi, gwo, gch[:11], gb[0]), ('tm', 'item'))]
    pallas_call x1 -> x2, Pallas kernels: 125 us -> 135 us  [the longest x1 126 us: run(): pl.pallas_call(functools.partial(kernel, (n_tm, n_item, NI, H, B, F)), ou...]
    unnamed x13 -> x0, local copies, waits for them, and re-layouts: 9.57 us -> none
    reduce_sum x2 -> x0, other arithmetic: 4.7 us -> none  [the longest x1 2.98 us: local(): jnp.sum(sources.astype(F32) * chosen[:, :, None, None], axis=0)]
    convert_element_type x6 -> x0, other arithmetic: 4.2 us -> none  [the longest x1 1.47 us: local(): grad_sources = chosen[:, :, None, None] * gmix.astype(F32)[None]]
    mul x1 -> x0, other arithmetic: 3.76 us -> none  [local(): grad_sources = chosen[:, :, None, None] * gmix.astype(F32)[None]]
    broadcast_in_dim x5 -> x0, local copies, waits for them, and re-layouts: 2.76 us -> none  [the longest x1 0.76 us: local(): gch[None]]
  transfers between devices with their start and end apart: 1 -> 0, of which waited for: 1 -> 0; matrix products, arithmetic and copies ran while one was open for 3% -> 0% of each run, Pallas kernels for 0% -> 0%
where the time goes in v3:
time: 135 us
  Pallas kernels  135 us (100%)
    pallas_call x1, Pallas kernels, run(): pl.pallas_call(functools.partial(kernel, (n_tm, n_item, NI, H, B, F)), ou...  126 us
    pallas_call x1, Pallas kernels, close(): pl.pallas_call(close_kernel, out_shape=(shape(block.shape, BF16), shape(s...  8.1 us

profile of v3, /device:TPU:0, one launch (start us, length us, event | category | flops | bytes accessed | tf_op | source)
XLA Modules:
  0.0 135.3 jit_solution(8194233184994459160)
XLA Ops:
  0.6 126.4 %temporal_blocks.1 = (bf16[8,128,1024]{2,1,0:T(8,128)(2,1)}, bf16[8,128,1024]{2,1,0:T(8,128)(2,1)}, bf16[8,64,1024]{2,1,0:T(8,128)(2,1)}, f32[1664,128]{1,0:T(8,128)}) custom-call(bf16[3,512,1024]{2,1,0:T(8,128)(2,1)} %bitcast.9, bf16[8,128,1024]{2,1,0:T(8,128)(2,1)} %gout_h.1, bf16[8,128,1024]{2,1,0:T(8,128)(2,1)} %gskip_h.1, bf16[512,128]{1,0:T(8,128)(2,1)} %bitcast.11, ...), custom_call_target="tpu_custom_call" | custom-call | tf_op jit(solution)/shard_map/temporal_blocks/pallas_call | solution.py:1120
  127.0 8.1 %lay_out.1 = (bf16[8,128,1024]{2,1,0:T(8,128)(2,1)}, bf16[8,128,1024]{2,1,0:T(8,128)(2,1)}, f32[3,8,64,1024]{3,2,1,0:T(8,128)}, f32[512,128]{1,0:T(8,128)}, f32[...) custom-call(bf16[8,128,1024]{2,1,0:T(8,128)(2,1)} %get-tuple-element.18.block_in, ...), custom_call_target="tpu_custom_call" | custom-call | tf_op jit(solution)/shard_map/lay_out/pallas_call | solution.py:1194

commit v4 on v3

--- a/solution.py
+++ b/solution.py
@@ -13,11 +13,11 @@
 ROWS = 128
 ROWS1 = 512
 ROWS2 = 512
-ROWS3 = 512
+ROWS3 = 256
 ROWS4 = 128
 ROWS5 = 512
 ROWS6 = 512
-ROWS7 = 256
+ROWS7 = 128
 ROWS8 = 512
 EPSILON = 1e-05
 VMEM_LIMIT = 63 * 1024 * 1024 + 512 * 1024
@@ -80,11 +80,11 @@
     block_h, skip_h, gmix_h, grad_h,
     stage, x0, x1, skips, act1_0, act1_1, soft1, act2, soft2, buf, wide_s, dp, gacc,
     wpre, wout, wg, win, chan, col,
-    grad, bias_sum, came0, came1, from_item0, from_item1, from_tm0, from_tm1,
+    low_grad, low_total, to_owner_slots, grad, bias_sum, came0, came1, from_item0, from_item1, from_tm0, from_tm1,
     mask_ref, edge_mask_ref, invn_ref, stat, back, st_src, st_buf,
     edge_src, edge_in, x_edge, dp_edge, first_edge, act_edge, soft_edge, conv_edge,
     sem_s, sem_w, sem_x, sem_xr, sem_g, sem_es, sem_er, sem_ss, sem_sr, sem_hs, sem_hr, sem_o, sem_or, sem_m, sem_mr,
-    sem_k, sem_kr, sem_ri, sem_rir, sem_rt, sem_rtr, sem_at, sem_atr, sem_ai, sem_air, sem_f,
+    sem_ls, sem_lr, sem_gs, sem_gr, sem_k, sem_kr, sem_ri, sem_rir, sem_rt, sem_rtr, sem_at, sem_atr, sem_ai, sem_air, sem_f,
 ):
     n_tm, n_item, NI, H, B, F = dims
     R = ROWS
@@ -123,15 +123,11 @@
         peer = lax.rem(me + d, members)
         device = {"tm": peer // n_item, "item": lax.rem(peer, n_item)}
         pl.semaphore_signal(barrier, inc=1, device_id=device, device_id_type=MESH)
+        pl.semaphore_signal(barrier, inc=1, device_id={"section": o} | device, device_id_type=MESH)
         return c
 
-    def greet_other(d, c):
-        device = {"section": o, "tm": lax.rem(t + d, n_tm)}
-        pl.semaphore_signal(barrier, inc=1, device_id=device, device_id_type=MESH)
-        return c
-
+    pl.semaphore_signal(barrier, inc=1, device_id={"section": o}, device_id_type=MESH)
     lax.fori_loop(1, members, greet, 0)
-    lax.fori_loop(0, n_tm, greet_other, 0)
 
     w_in = w_in_ref[...]
     w_out = w_out_ref[...].astype(F32)
@@ -178,7 +174,7 @@
 
     lax.fori_loop(0, 2 * NI, mix_item, 0)
 
-    pl.semaphore_wait(barrier, members - 1 + n_tm)
+    pl.semaphore_wait(barrier, 2 * members - 1)
 
     own_rows = pl.ds(pl.multiple_of(s * half, half), half)
     other_rows = pl.ds(pl.multiple_of(o * half, half), half)
@@ -316,6 +312,7 @@
         return tall(mask_ref[i, :, at : at + width], rows)
 
     zero8 = jnp.zeros((8, LANES), F32)
+    zero8f = jnp.zeros((8, F), F32)
 
     def pack_edges(src, channels, slot):
         def tile(r, c):
@@ -382,9 +379,12 @@
         soft = jnp.maximum(neg, jnp.log2(1.0 + jnp.exp2(jnp.minimum(neg, 100.0))))
         return rest * soft - neg, soft
 
-    def masked_sums(a, m, sums):
-        am = a * m
-        return (sums[0] + fold_rows(fold(am)), sums[1] + fold_rows(fold(am * a)))
+    def add_sums(a, sums):
+        return (sums[0] + fold_rows(a), sums[1] + fold_rows(a * a))
+
+    def send_sums(ph, i, sums):
+        m = mask_ref[i, :, MID]
+        send_stats(ph, i, fold(sums[0] * m), fold(sums[1] * m))
 
     def phase1(k):
         R = ROWS1
@@ -394,35 +394,34 @@
         mid = MID if k == 0 else slice(0, F)
 
         def item(i):
-            wide_s[:, 0:width] = dot(wpre[k], x[i])
-            m = mask_row(i, R)
 
             def tile(r, sums):
                 table = chan[k, r, :]
                 bias = column(table, 0) * -LOG2E
                 rest = 1.0 - column(table, 1)
-                neg = wide_s[r, 0:width] * -LOG2E + wide(bias, width)
+                neg = dot(wpre[k, r, :], x[i]) * -LOG2E + wide(bias, width)
                 a, soft = rectify(neg, wide(rest, width))
                 act[i, r, :] = a.astype(BF16)
                 soft1[k, i, r, :] = soft[:, mid].astype(BF16)
-                return masked_sums(a[:, mid], m, sums)
-
-            a, b = per_tile(tile, rows=R, init=(zero8, zero8))
-            send_stats(4 * k, i, a, b)
-
-        per_item(item)
-        if k == 1:
-            recv_edges(1, B, x_edge)
-            wide_s[:, 0:LANES] = dot(wpre[1], x_edge[...])
-
-            def tile(r, c):
-                table = chan[1, r, :]
-                neg = wide_s[r, 0:LANES] * -LOG2E + column(table, 0) * -LOG2E
-                a, _ = rectify(neg, 1.0 - column(table, 1))
-                wide_s[r, 0:LANES] = a
-                return c
-
-            per_tile(tile, rows=R)
+                return add_sums(a[:, mid], sums)
+
+            send_sums(4 * k, i, per_tile(tile, rows=R, init=(zero8f, zero8f)))
+
+        return item
+
+    def edge1():
+        R = ROWS1
+        recv_edges(1, B, x_edge)
+        wide_s[:, 0:LANES] = dot(wpre[1], x_edge[...])
+
+        def tile(r, c):
+            table = chan[1, r, :]
+            neg = wide_s[r, 0:LANES] * -LOG2E + column(table, 0) * -LOG2E
+            a, _ = rectify(neg, 1.0 - column(table, 1))
+            wide_s[r, 0:LANES] = a
+            return c
+
+        per_tile(tile, rows=R)
 
     def phase2(k):
         R = ROWS2
@@ -447,19 +446,21 @@
 
             per_tile(tile, rows=R)
 
-        per_item(item)
-        if k == 1:
-            mean, inv = tall(lanes_of(stat.at[2], 0), R), tall(lanes_of(stat.at[2], 1), R)
-            m = tall(edge_mask_ref[...], R)
-
-            def tile(r, c):
-                table = chan[1, r, :]
-                scale = inv * column(table, 2)
-                a = wide_s[r, 0:LANES]
-                first_edge[r, :] = (((a - mean) * scale + column(table, 3)) * m).astype(BF16)
-                return c
-
-            per_tile(tile, rows=R)
+        return item
+
+    def edge2():
+        R = ROWS2
+        mean, inv = tall(lanes_of(stat.at[2], 0), R), tall(lanes_of(stat.at[2], 1), R)
+        m = tall(edge_mask_ref[...], R)
+
+        def tile(r, c):
+            table = chan[1, r, :]
+            scale = inv * column(table, 2)
+            a = wide_s[r, 0:LANES]
+            first_edge[r, :] = (((a - mean) * scale + column(table, 3)) * m).astype(BF16)
+            return c
+
+        per_tile(tile, rows=R)
 
     def neighbours(f, edge, i):
         shifted_in = pltpu.roll(edge, lax.rem(127 - 32 * i + 256, 128), 1)
@@ -486,7 +487,6 @@
     def phase3(k):
         R = ROWS3
         def item(i):
-            m = mask_row(i, R)
 
             def tile(r, sums):
                 c, rest = conv_coefs(chan[k, r, :])
@@ -495,63 +495,49 @@
                 a, soft = rectify(neg, wide(rest, F))
                 act2[k, i, r, :] = a.astype(BF16)
                 soft2[k, i, r, :] = soft.astype(BF16)
-                return masked_sums(a, m, sums)
-
-            a, b = per_tile(tile, rows=R, init=(zero8, zero8))
-            send_stats(4 * k + 1, i, a, b)
-
-        per_item(item)
-        if k == 1:
-
-            def tile(r, x):
-                c, rest = conv_coefs(chan[1, r, :])
-                f = first_edge[r, :].astype(F32)
-                neg = c[0] * pltpu.roll(f, 1, 1) + c[1] * f + c[2] * pltpu.roll(f, LANES - 1, 1) + c[3]
-                a, soft = rectify(neg, rest)
-                act_edge[r, :] = a.astype(BF16)
-                soft_edge[r, :] = soft.astype(BF16)
-                return x
-
-            per_tile(tile, rows=R)
-
-    def out_copies(kind, k, i):
+                return add_sums(a, sums)
+
+            send_sums(4 * k + 1, i, per_tile(tile, rows=R, init=(zero8f, zero8f)))
+
+        return item
+
+    def edge3():
+        R = ROWS3
+        def tile(r, x):
+            c, rest = conv_coefs(chan[1, r, :])
+            f = first_edge[r, :].astype(F32)
+            neg = c[0] * pltpu.roll(f, 1, 1) + c[1] * f + c[2] * pltpu.roll(f, LANES - 1, 1) + c[3]
+            a, soft = rectify(neg, rest)
+            act_edge[r, :] = a.astype(BF16)
+            soft_edge[r, :] = soft.astype(BF16)
+            return x
+
+        per_tile(tile, rows=R)
+
+    def out_copy(kind, k, i):
         row = first_item + i
-        if kind == 0 and k == 1:
-            pairs = [
-                (stage.at[2 * i + j], block_h.at[row, pl.ds(j * half, half)], sem_o.at[2 * j, 1, i], sem_or.at[2 * j, i])
-                for j in (0, 1)
-            ]
-        else:
-            src, dst = ((x1, block_h), (skips, skip_h))[kind]
-            pairs = [(src.at[i], dst.at[row], sem_o.at[kind, k, i], sem_or.at[kind, i])]
-        return [
-            (pltpu.make_async_copy(a, b, sem), remote(a, b, sem, there, {"section": o})) for a, b, sem, there in pairs
-        ]
+        src, dst = (((x1, x0)[k], block_h), (skips, skip_h))[kind]
+        src = src.at[i, :, centre] if (kind, k) == (0, 1) else src.at[i]
+        return (
+            pltpu.make_async_copy(src, dst.at[row], sem_o.at[kind, k, i]),
+            remote(src, dst.at[row], sem_o.at[kind, k, i], sem_or.at[kind, i], {"section": o}),
+        )
 
     def start_out(kind, k, i):
-        for here, there in out_copies(kind, k, i):
-            pl.when(s == k)(lambda: here.start())
-            pl.when(s != k)(lambda: there.start())
+        here, there = out_copy(kind, k, i)
+        pl.when(s == k)(lambda: here.start())
+        pl.when(s != k)(lambda: there.start())
 
     def wait_out(kind, k, i):
-        for here, there in out_copies(kind, k, i):
-            pl.when(s == k)(lambda: here.wait())
-            pl.when(s != k)(lambda: there.wait_send())
-
-    def wait_came(i):
-        row = o * NI + i
-        skip_in = remote(skips.at[i], skip_h.at[row], sem_o.at[1, 0, i], sem_or.at[1, i], {"section": o})
-        skip_in.wait_recv()
-
-        @pl.when(s == 0)
-        def _():
-            remote(x1.at[i], block_h.at[row], sem_o.at[0, 0, i], sem_or.at[0, i], {"section": o}).wait_recv()
-
-        @pl.when(s == 1)
-        def _():
-            for j in (0, 1):
-                dst = block_h.at[row, pl.ds(j * half, half)]
-                remote(stage.at[0], dst, sem_o.at[2 * j, 1, i], sem_or.at[2 * j, i], {"section": o}).wait_recv()
+        here, there = out_copy(kind, k, i)
+        pl.when(s == k)(lambda: here.wait())
+        pl.when(s != k)(lambda: there.wait_send())
+
+    def wait_came(kind, i):
+        src, dst = ((x1, block_h), (skips, skip_h))[kind]
+        remote(
+            src.at[i], dst.at[o * NI + i], sem_o.at[kind, 0, i], sem_or.at[kind, i], {"section": o}
+        ).wait_recv()
 
     def phase4(k):
         R = ROWS4
@@ -559,7 +545,8 @@
         mid = MID if k == 0 else slice(0, F)
 
         def item(i):
-            finish_norm(4 * k + 1, 2 * k + 1, i)
+            if k == 0:
+                finish_norm(1, 1, i)
             mean, inv = tall(stat[2 * k + 1, i, 0], B), tall(stat[2 * k + 1, i, 1], B)
             m = mask_row(i, B)
             y = pl.ds(0, 2 * B)
@@ -574,9 +561,7 @@
             if k == 0:
                 x1[i] = total
             else:
-                stage[2 * i] = total[0:half]
-                stage[2 * i + 1] = total[half:]
-
+                x0[i, :, MID] = total
             p = project(pl.ds(B, B))
             if k == 1:
                 wait_out(1, 0, i)
@@ -585,13 +570,15 @@
             start_out(0, k, i)
             start_out(1, k, i)
 
-        per_item(item)
+        return item
 
     def phase5(k):
         R = ROWS5
         R5 = ROWS5
 
         def item(i):
+            if k == 1:
+                finish_norm(5, 3, i)
             mean, inv = tall(stat[2 * k + 1, i, 0], R5), tall(stat[2 * k + 1, i, 1], R5)
             wide_s[:, 0 : 2 * B] = dot(act2[k, i], dp[i], NT)
             total8 = dot(jnp.ones((8, F), BF16), dp[i], NT)
@@ -618,7 +605,7 @@
             a, b = per_tile(tile, rows=R5, init=(zero8, zero8))
             send_stats(4 * k + 2, i, a, b)
 
-        per_item(item)
+        return item
 
     def halo_copy(i, side):
         edge = pl.ds(DILATION, DILATION) if side == 0 else pl.ds(F, DILATION)
@@ -637,13 +624,12 @@
             inv = tall(stat[2 * k + 1, i, 1], R) * LOG2E
             p, q = wide(tall(back[i, 0], R), F), wide(tall(back[i, 1], R), F)
             m = mask_row(i, R)
-            wide_s[:, 0:F] = dot(wout[k], dp[i])
 
             def tile(r, c):
                 table = chan[k, r, :]
                 slope = column(table, 8)
                 g = inv * column(table, 9)
-                d_act = low(wide_s[r, 0:F] * wide(g, F) + m * (p + q * act2[k, i, r, :].astype(F32)))
+                d_act = low(dot(wout[k, r, :], dp[i]) * wide(g, F) + m * (p + q * act2[k, i, r, :].astype(F32)))
                 soft = soft2[k, i, r, :]
                 d_conv = d_act * (wide(low(slope), F) + wide(low(1.0 - slope), F) * jnp.exp2(-soft))
                 gacc[8, r, :] += fold(d_act * soft).astype(F32) * -LN2
@@ -670,22 +656,24 @@
                 def _():
                     buf[i, :, F + DILATION : W] = jnp.zeros((H, DILATION), BF16)
 
-        per_item(item)
-        if k == 1:
-            wide_s[:, 0:LANES] = dot(wout[1], dp_edge[...])
-            inv = tall(lanes_of(stat.at[3], 1), R) * LOG2E
-            p, q = tall(lanes_of(back, 0), R), tall(lanes_of(back, 1), R)
-            m = tall(edge_mask_ref[...], R)
-
-            def tile(r, c):
-                table = chan[1, r, :]
-                slope = column(table, 8)
-                d_act = wide_s[r, 0:LANES] * (inv * column(table, 9)) + m * (p + q * act_edge[r, :].astype(F32))
-                d_conv = d_act * (slope + (1.0 - slope) * jnp.exp2(-soft_edge[r, :].astype(F32)))
-                conv_edge[r, :] = d_conv.astype(BF16)
-                return c
-
-            per_tile(tile, rows=R)
+        return item
+
+    def edge6():
+        R = ROWS6
+        wide_s[:, 0:LANES] = dot(wout[1], dp_edge[...])
+        inv = tall(lanes_of(stat.at[3], 1), R) * LOG2E
+        p, q = tall(lanes_of(back, 0), R), tall(lanes_of(back, 1), R)
+        m = tall(edge_mask_ref[...], R)
+
+        def tile(r, c):
+            table = chan[1, r, :]
+            slope = column(table, 8)
+            d_act = wide_s[r, 0:LANES] * (inv * column(table, 9)) + m * (p + q * act_edge[r, :].astype(F32))
+            d_conv = d_act * (slope + (1.0 - slope) * jnp.exp2(-soft_edge[r, :].astype(F32)))
+            conv_edge[r, :] = d_conv.astype(BF16)
+            return c
+
+        per_tile(tile, rows=R)
 
     def phase7(k):
         R = ROWS7
@@ -734,7 +722,7 @@
             a, b = per_tile(tile, rows=R, init=(zero8, zero8))
             send_stats(4 * k + 3, i, a, b)
 
-        per_item(item)
+        return item
 
     def mix_copy(i):
         row = first_item + i
@@ -765,15 +753,15 @@
                 gacc[1, r, :] += fold(d_act * soft).astype(F32) * -LN2
                 gacc[0, r, :] += fold(d_pre).astype(F32)
                 buf[i, r, MID] = d_pre
+                grad[k, pl.ds(2 * H + r.start, R), :] += dot(d_pre, x[i, :, mid], NT)
                 return c
 
             per_tile(tile, rows=R)
-            grad[k, 2 * H : 3 * H] += dot(buf[i, :, MID], x[i, :, mid], NT)
 
             if k == 1:
                 input_gradient(1, i)
 
-        per_item(item)
+        return item
 
     def input_gradient(k, i):
         wide_s[0:B, 0:F] = dot(win[k], buf[i, :, MID])
@@ -900,6 +888,84 @@
 
             each(n_item, wait)
 
+    last_rows = grad.shape[1] - 2 * H
+    last_chunk = to_owner_slots.shape[2]
+    last_owners = low_grad.shape[0] // last_chunk
+    first_core = jnp.int32(0)
+
+    def member_at(d):
+        peer = lax.rem(me + d, members)
+        return peer, {"section": first_core, "tm": peer // n_item, "item": lax.rem(peer, n_item)}
+
+    def chunk_rows(member):
+        return pl.ds(pl.multiple_of(lax.rem(member, last_owners) * last_chunk, 16), last_chunk)
+
+    def last_scatter(core, d):
+        peer, device = member_at(d)
+        return remote(
+            low_grad.at[chunk_rows(peer)], to_owner_slots.at[core, d], sem_ls.at[d], sem_lr.at[core, d], device
+        )
+
+    def last_gather(d, member):
+        rows = low_total.at[chunk_rows(member)]
+        return remote(rows, rows, sem_gs.at[d], sem_gr.at[d], member_at(d)[1])
+
+    def others(body, start=1):
+        lax.fori_loop(start, members, lambda d, c: (body(d), c)[1], 0)
+
+    def last_1():
+        low_grad[0:last_rows] = low(grad[0, 2 * H :])
+        if low_grad.shape[0] > last_rows:
+            low_grad[last_rows:] = jnp.zeros((low_grad.shape[0] - last_rows, LANES), BF16)
+
+        def send(core):
+            def one(d):
+                pl.when(member_at(d)[0] < last_owners)(lambda: last_scatter(core, d).start())
+
+            others(one, 1 - core)
+
+        pl.when(s == 0)(lambda: send(0))
+        pl.when(s == 1)(lambda: send(1))
+
+    def last_2():
+        def sent(core):
+            def one(d):
+                pl.when(member_at(d)[0] < last_owners)(lambda: last_scatter(core, d).wait_send())
+
+            others(one, 1 - core)
+
+        pl.when(s == 1)(lambda: sent(1))
+
+        @pl.when(s == 0)
+        def _():
+            sent(0)
+
+            @pl.when(me < last_owners)
+            def _():
+                others(lambda d: last_scatter(0, d).wait_recv())
+                others(lambda d: last_scatter(1, d).wait_recv(), 0)
+                mine = chunk_rows(me)
+                total = low_grad[mine].astype(F32) + to_owner_slots[1, 0].astype(F32)
+                total = lax.fori_loop(
+                    1,
+                    members,
+                    lambda d, x: x + (to_owner_slots[0, d].astype(F32) + to_owner_slots[1, d].astype(F32)),
+                    total,
+                )
+                low_total[mine] = low(total)
+                others(lambda d: last_gather(d, me).start())
+
+    def last_3():
+        @pl.when(s == 0)
+        def _():
+            def wait(d):
+                source = lax.rem(me - d + members, members)
+                pl.when(me < last_owners)(lambda: last_gather(d, me).wait_send())
+                pl.when(source < last_owners)(lambda: last_gather(d, source).wait_recv())
+
+            others(wait)
+            came1[...] = low_total[0:last_rows].astype(F32)
+
     def finish_block(k):
         group = H // 4
         lanes = lax.broadcasted_iota(jnp.int32, (group, LANES), 1)
@@ -939,65 +1005,74 @@
             halo_send(1, core).wait_send()
             halo_recv(0, core).wait_recv()
 
-    phase1(0)
+    def steps(count, *bodies):
+        def step(j, c):
+            for first, body in bodies:
+                pl.when((j >= first) & (j < first + NI))(functools.partial(body, j - first))
+            return c
+
+        lax.fori_loop(0, count, step, 0)
+
+    def send_x1_edges(i):
+        @pl.when(i == NI - 1)
+        def _():
+            pack_edges(x1, B, 1)
+            send_edges(1, B)
+
+    per_item(phase1(0))
+    p2, p3 = phase2(0), phase3(0)
+    per_item(lambda i: (p2(i), p3(i)))
+    wait_weights(2, 3)
+    steps(NI + 2, (0, phase4(0)), (0, send_x1_edges), (2, phase1(1)))
+    edge1()
     load_out.wait()
     load_skip.wait()
-
     per_item(mask_gradients)
     pack_edges(dp, 2 * B, 0)
     send_edges(0, 2 * B)
-    phase2(0)
-    phase3(0)
-    wait_weights(2, 3)
-    phase4(0)
-    pack_edges(x1, B, 1)
-    send_edges(1, B)
-    phase1(1)
-    phase2(1)
-    phase3(1)
-    phase4(1)
+    per_item(phase2(1))
+    edge2()
+    per_item(phase3(1))
+    edge3()
     recv_edges(0, 2 * B, dp_edge)
     wait_weights(4)
     gacc[...] = jnp.zeros(gacc.shape, F32)
-    phase5(1)
+    per_item(phase5(1))
     sum_1(0, 1)
-    phase6(1)
+    per_item(phase6(1))
+    edge6()
     sum_2(0, 1)
-    phase7(1)
+    wait_weights(5)
+    per_item(phase7(1))
+    per_item(phase8(1))
     sum_3(0, 1)
-    wait_weights(5)
-    phase8(1)
     finish_block(1)
     sum_1(1, 1)
+    gacc[...] = jnp.zeros(gacc.shape, F32)
+    per_item(phase5(0))
+    sum_1(0, 0)
     sum_4(0, 1)
-    gacc[...] = jnp.zeros(gacc.shape, F32)
-    phase5(0)
-    sum_1(0, 0)
     sum_2(1, 1)
+    per_item(phase6(0))
     sum_5(0, 1)
-    phase6(0)
     sum_2(0, 0)
     sum_3(1, 1)
-    phase7(0)
+    per_item(phase7(0))
+    per_item(phase8(0))
+    finish_block(0)
+    last_1()
     sum_3(0, 0)
     sum_4(1, 1)
-    for i in range(NI):
-        wait_out(0, 1, i)
-    phase8(0)
-    finish_block(0)
-    sum_1(1, 0)
+    per_item(phase4(1))
     sum_4(0, 0)
     sum_5(1, 1)
     per_item(lambda i: input_gradient(0, i))
-    sum_2(1, 0)
+    last_2()
     sum_5(0, 0)
-    sum_3(1, 0)
-    sum_4(1, 0)
-    sum_5(1, 0)
     sum_6(0, 1)
     sum_6(1, 1)
+    last_3()
     sum_6(0, 0)
-    sum_6(1, 0)
     results = [
         pltpu.make_async_copy(came[part], grad_h.at[pl.ds(a, b - a)], sem_f.at[part])
         for part, (a, b) in enumerate(rows_at_part)
@@ -1014,9 +1089,10 @@
         remote(
             stage.at[2 * i], gmix_h.at[o * NI + i], sem_m.at[1, i], sem_mr.at[i], {"section": o}
         ).wait_recv()
-        wait_out(0, 0, i)
-        wait_out(1, 1, i)
-        wait_came(i)
+        for kind, k in ((0, 0), (0, 1), (1, 1)):
+            wait_out(kind, k, i)
+        wait_came(0, i)
+        wait_came(1, i)
 
 
 def chunk_of(rows, members):
@@ -1036,6 +1112,9 @@
     half = B // 2
     rows0, rows1 = 2 * H, H + H // 4
     quarter0, quarter1 = rows0 // n_item, rows1 // n_item
+    members = n_tm * n_item
+    low_chunk = -(-rows1 // (16 * members)) * 16
+    low_owners = -(-rows1 // low_chunk)
     smem = pl.BlockSpec(memory_space=pltpu.SMEM)
     any_spec = pl.BlockSpec(memory_space=pl.ANY)
     vmem = pl.BlockSpec(memory_space=pltpu.VMEM)
@@ -1067,6 +1146,9 @@
         pltpu.VMEM((2, B, H), BF16),
         pltpu.VMEM((2, H, LANES), F32),
         pltpu.VMEM((2, 2 * B, LANES), F32),
+        pltpu.VMEM((low_chunk * low_owners, LANES), BF16),
+        pltpu.VMEM((low_chunk * low_owners, LANES), BF16),
+        pltpu.VMEM((2, members, low_chunk, LANES), BF16),
         pltpu.VMEM((2, rows0 + rows1, LANES), F32),
         pltpu.VMEM((2, 8, 2 * B), F32),
         pltpu.VMEM((rows0, LANES), F32),
@@ -1101,10 +1183,14 @@
         dma((2, NI, n_tm - 1)),
         dma((2, NI)),
         dma((2, NI)),
-        dma((3, 2, NI)),
-        dma((3, NI)),
+        dma((2, 2, NI)),
+        dma((2, NI)),
         dma((2, NI)),
         dma((NI,)),
+        dma((members,)),
+        dma((2, members)),
+        dma((members,)),
+        dma((members,)),
         dma((2,)),
         dma((2,)),
         dma((2, n_item - 1)),
@@ -1132,12 +1218,11 @@
 
 def close_kernel(
     block_in, skip_in, gmix_in, grad_in, counts,
-    block_h, skip_h, sources_h, w_in_out, chan_out, w_out_out, b_out_out,
-    held, mixed, full, nothing, sem_a, sem_b, sem_g, sem_s,
+    block_h, skip_h, sources_h, w_in_h, chan_h, w_out_h, b_out_h,
+    held, mixed, full, nothing, sums, w_out, chan, bias, sem_a, sem_b, sem_g, sem_s, sem_w,
 ):
     items = gmix_in.shape[0]
-    H = w_in_out.shape[0]
-    B = w_in_out.shape[1]
+    H, B = w_in_h.shape
     n_src = sources_h.shape[0]
     plain = [(j, i) for i in range(items) for j in (0, 1)]
 
@@ -1148,8 +1233,10 @@
         return pltpu.make_async_copy(held.at[j, i], (block_h, skip_h)[j].at[i], sem_b.at[j, i])
 
     loads = [pltpu.make_async_copy(gmix_in.at[i], mixed.at[i], sem_g.at[i]) for i in range(items)]
+    load_sums = pltpu.make_async_copy(grad_in, sums, sem_w.at[0])
     for copy in loads:
         copy.start()
+    load_sums.start()
     for j, i in plain:
         fetch(j, i).start()
     nothing[...] = jnp.zeros(nothing.shape, F32)
@@ -1166,16 +1253,27 @@
             def _():
                 pltpu.make_async_copy(nothing, sources_h.at[n, i], sem_s.at[n, i]).start()
 
+    load_sums.wait()
+    store_w_in = pltpu.make_async_copy(sums.at[pl.ds(2 * H, H)], w_in_h, sem_w.at[1])
+    store_w_in.start()
     for j, i in plain:
         fetch(j, i).wait()
         store(j, i).start()
-    w_out_out[0:B, :] = grad_in[0:H, :].T
-    w_out_out[B : 2 * B, :] = grad_in[H : 2 * H, :].T
-    w_in_out[...] = grad_in[2 * H : 3 * H, :]
-    rows = grad_in[3 * H : 3 * H + H // 4, :].T
-    for j in range(chan_out.shape[0]):
-        chan_out[j] = jnp.concatenate([rows[32 * g + j : 32 * g + j + 1] for g in range(4)], axis=1)
-    b_out_out[...] = jnp.concatenate([rows[32 * g + 11 : 32 * g + 12] for g in range(2 * B * 4 // H)], axis=1)
+    w_out[0:B, :] = sums[0:H, :].T
+    w_out[B : 2 * B, :] = sums[H : 2 * H, :].T
+    rows = sums[3 * H : 3 * H + H // 4, :].T
+    for j in range(chan.shape[0]):
+        chan[j] = jnp.concatenate([rows[32 * g + j : 32 * g + j + 1] for g in range(4)], axis=1)
+    bias[...] = jnp.concatenate([rows[32 * g + 11 : 32 * g + 12] for g in range(2 * B * 4 // H)], axis=1)
+    late = [
+        pltpu.make_async_copy(src, dst, sem_w.at[2 + j])
+        for j, (src, dst) in enumerate(((w_out, w_out_h), (chan, chan_h), (bias, b_out_h)))
+    ]
+    for copy in late:
+        copy.start()
+    for copy in late:
+        copy.wait()
+    store_w_in.wait()
     for j, i in plain:
         store(j, i).wait()
     for i in range(items):
@@ -1188,7 +1286,6 @@
     B = 2 * half
     H = (grad.shape[0] * 4) // 13
     any_spec = pl.BlockSpec(memory_space=pl.ANY)
-    vmem = pl.BlockSpec(memory_space=pltpu.VMEM)
     dma = pltpu.SemaphoreType.DMA
     shape = jax.ShapeDtypeStruct
     return pl.pallas_call(
@@ -1202,17 +1299,22 @@
             shape((2 * B, H), F32),
             shape((1, 2 * B), F32),
         ),
-        in_specs=[any_spec] * 3 + [vmem, pl.BlockSpec(memory_space=pltpu.SMEM)],
-        out_specs=[any_spec] * 3 + [vmem] * 4,
+        in_specs=[any_spec] * 4 + [pl.BlockSpec(memory_space=pltpu.SMEM)],
+        out_specs=[any_spec] * 7,
         scratch_shapes=[
             pltpu.VMEM((2, items, B, F), BF16),
             pltpu.VMEM((items, half, F), BF16),
             pltpu.VMEM((items, half, F), F32),
             pltpu.VMEM((half, F), F32),
+            pltpu.VMEM(grad.shape, F32),
+            pltpu.VMEM((2 * B, H), F32),
+            pltpu.VMEM((n_rows, 1, H), F32),
+            pltpu.VMEM((1, 2 * B), F32),
             dma((2, items)),
             dma((2, items)),
             dma((items,)),
             dma((n_src, items)),
+            dma((5,)),
         ],
         compiler_params=pltpu.CompilerParams(vmem_limit_bytes=VMEM_LIMIT),
         name="lay_out",

time: 135 us -> 124 us (0.919)
  Pallas kernels: 135 us -> 123 us
    pallas_call x1, Pallas kernels: 126 us -> 116 us  [run(): pl.pallas_call(functools.partial(kernel, (n_tm, n_item, NI, H, B, F)), ou...]
where the time goes in v4:
time: 124 us
  Pallas kernels  123 us (99%)
    pallas_call x1, Pallas kernels, run(): pl.pallas_call(functools.partial(kernel, (n_tm, n_item, NI, H, B, F)), ou...  116 us
    pallas_call x1, Pallas kernels, close(): pl.pallas_call(close_kernel, out_shape=(shape(block.shape, BF16), shape(s...  7.03 us

profile of v4, /device:TPU:0, one launch (start us, length us, event | category | flops | bytes accessed | tf_op | source)
XLA Modules:
  0.0 123.5 jit_solution(16181635551870412311)
XLA Ops:
  0.6 115.7 %temporal_blocks.1 = (bf16[8,128,1024]{2,1,0:T(8,128)(2,1)}, bf16[8,128,1024]{2,1,0:T(8,128)(2,1)}, bf16[8,64,1024]{2,1,0:T(8,128)(2,1)}, f32[1664,128]{1,0:T(8,128)}) custom-call(bf16[3,512,1024]{2,1,0:T(8,128)(2,1)} %bitcast.9, bf16[8,128,1024]{2,1,0:T(8,128)(2,1)} %gout_h.1, bf16[8,128,1024]{2,1,0:T(8,128)(2,1)} %gskip_h.1, bf16[512,128]{1,0:T(8,128)(2,1)} %bitcast.11, ...), custom_call_target="tpu_custom_call" | custom-call | tf_op jit(solution)/shard_map/temporal_blocks/pallas_call | solution.py:1206
  116.3 7.0 %lay_out.1 = (bf16[8,128,1024]{2,1,0:T(8,128)(2,1)}, bf16[8,128,1024]{2,1,0:T(8,128)(2,1)}, f32[3,8,64,1024]{3,2,1,0:T(8,128)}, f32[512,128]{1,0:T(8,128)}, f32[...) custom-call(bf16[8,128,1024]{2,1,0:T(8,128)(2,1)} %get-tuple-element.18.block_in, ...), custom_call_target="tpu_custom_call" | custom-call | tf_op jit(solution)/shard_map/lay_out/pallas_call | solution.py:1291

commit v5 on v4

--- a/solution.py
+++ b/solution.py
@@ -17,7 +17,8 @@
 ROWS4 = 128
 ROWS5 = 512
 ROWS6 = 512
-ROWS7 = 128
+ROWS7 = 256
+ROWS7_ENDS = 512
 ROWS8 = 512
 EPSILON = 1e-05
 VMEM_LIMIT = 63 * 1024 * 1024 + 512 * 1024
@@ -76,13 +77,13 @@
 
 def kernel(
     dims,
-    sources_h, gout_h, gskip_h, w_in_ref, chan_ref, w_out_ref, b_out_ref, counts, lengths,
+    sources_h, gout_h, gskip_h, w_in_h, chan_h, w_out_h, b_out_h, counts, lengths,
     block_h, skip_h, gmix_h, grad_h,
     stage, x0, x1, skips, act1_0, act1_1, soft1, act2, soft2, buf, wide_s, dp, gacc,
     wpre, wout, wg, win, chan, col,
     low_grad, low_total, to_owner_slots, grad, bias_sum, came0, came1, from_item0, from_item1, from_tm0, from_tm1,
-    mask_ref, edge_mask_ref, invn_ref, stat, back, st_src, st_buf,
-    edge_src, edge_in, x_edge, dp_edge, first_edge, act_edge, soft_edge, conv_edge,
+    mask_ref, edge_mask_ref, invn_ref, inner_sums, stat, back, st_src, st_buf,
+    shifts, w_in_ref, chan_ref, w_out_ref, b_out_ref, edge_src, edge_in, x_edge, dp_edge, first_edge, act_edge, soft_edge, conv_edge,
     sem_s, sem_w, sem_x, sem_xr, sem_g, sem_es, sem_er, sem_ss, sem_sr, sem_hs, sem_hr, sem_o, sem_or, sem_m, sem_mr,
     sem_ls, sem_lr, sem_gs, sem_gr, sem_k, sem_kr, sem_ri, sem_rir, sem_rt, sem_rtr, sem_at, sem_atr, sem_ai, sem_air, sem_f,
 ):
@@ -109,13 +110,21 @@
     def load_source(n):
         return pltpu.make_async_copy(sources_h.at[n], soft2.at[1, n], sem_s.at[n])
 
+    small = [
+        pltpu.make_async_copy(src, dst, sem_s.at[n_src + j])
+        for j, (src, dst) in enumerate(
+            ((w_in_h, w_in_ref), (chan_h, chan_ref), (w_out_h, w_out_ref), (b_out_h, b_out_ref))
+        )
+    ]
+    for copy in small:
+        copy.start()
     for n in range(n_src):
         load_source(n).start()
-    load_out = pltpu.make_async_copy(gout_h.at[pl.ds(first_item, NI)], dp.at[:, pl.ds(0, B)], sem_g.at[0])
-    load_skip = pltpu.make_async_copy(gskip_h.at[pl.ds(first_item, NI)], dp.at[:, pl.ds(B, B)], sem_g.at[1])
-    load_out.start()
-    load_skip.start()
     edge_in[...] = jnp.zeros(edge_in.shape, BF16)
+    row = lax.broadcasted_iota(jnp.int32, (2 * LANES, 2 * LANES), 0)
+    to = lax.broadcasted_iota(jnp.int32, (2 * LANES, 2 * LANES), 1)
+    step = jnp.where(to < LANES, LANES - 1, 1 - LANES)
+    shifts[...] = low(jnp.where(row - to == step, 1.0, 0.0))
 
     barrier = pltpu.get_barrier_semaphore()
 
@@ -128,6 +137,8 @@
 
     pl.semaphore_signal(barrier, inc=1, device_id={"section": o}, device_id_type=MESH)
     lax.fori_loop(1, members, greet, 0)
+    for copy in small:
+        copy.wait()
 
     w_in = w_in_ref[...]
     w_out = w_out_ref[...].astype(F32)
@@ -172,8 +183,7 @@
         stage[i] = (total * m).astype(BF16)
         return c
 
-    lax.fori_loop(0, 2 * NI, mix_item, 0)
-
+    lax.fori_loop(o * NI, o * NI + NI, mix_item, 0)
     pl.semaphore_wait(barrier, 2 * members - 1)
 
     own_rows = pl.ds(pl.multiple_of(s * half, half), half)
@@ -208,18 +218,19 @@
             x0.at[:, rows, place], x0.at[:, rows, place], sem_x.at[0], sem_xr.at[1 + 2 * side + core], {"section": o}
         )
 
+    def send_halos(core):
+        pl.when(t > 0)(lambda: halo_send(0, core).start())
+        pl.when(t < last)(lambda: halo_send(1, core).start())
+
+    main_send.start()
+    send_halos(o)
+    lax.fori_loop(s * NI, s * NI + NI, mix_item, 0)
     main_local.start()
-    main_send.start()
-
-    @pl.when(t > 0)
-    def _():
-        for core in (0, 1):
-            halo_send(0, core).start()
-
-    @pl.when(t < last)
-    def _():
-        for core in (0, 1):
-            halo_send(1, core).start()
+    send_halos(s)
+    load_out = pltpu.make_async_copy(gout_h.at[pl.ds(first_item, NI)], dp.at[:, pl.ds(0, B)], sem_g.at[0])
+    load_skip = pltpu.make_async_copy(gskip_h.at[pl.ds(first_item, NI)], dp.at[:, pl.ds(B, B)], sem_g.at[1])
+    load_out.start()
+    load_skip.start()
 
     weights = (wpre, chan, wg, col, wout, win)
 
@@ -462,23 +473,27 @@
 
         per_tile(tile, rows=R)
 
-    def neighbours(f, edge, i):
-        shifted_in = pltpu.roll(edge, lax.rem(127 - 32 * i + 256, 128), 1)
-        before = pltpu.roll(f, 1, 1)
-        lane = lax.broadcasted_iota(jnp.int32, edge.shape, 1)
-        lead = jnp.where(lane == 0, shifted_in, before[:, 0:LANES])
-        before = jnp.concatenate([lead, before[:, LANES:]], axis=1)
-        shifted_in = pltpu.roll(edge, lax.rem(110 - 32 * i + 256, 128), 1)
-        after = pltpu.roll(f, F - 1, 1)
-        trail = jnp.where(lane == LANES - 1, shifted_in, after[:, F - LANES :])
-        after = jnp.concatenate([after[:, : F - LANES], trail], axis=1)
-        return before, after
-
-    def taps(k, i, r, edge):
+    def place_halos(edge):
+        def item(i):
+            wide_edge = edge[...].astype(F32)
+            buf[i, :, 0:DILATION] = low(pltpu.roll(wide_edge, lax.rem(254 - 32 * i, 128), 1))
+            buf[i, :, F + DILATION : W] = low(pltpu.roll(wide_edge, lax.rem(239 - 32 * i, 128), 1))
+
+        per_item(item)
+
+    def shifted(i, r):
+        before, after = [], []
+        for j in range(F // LANES + 1):
+            v = dot(buf[i, r, j * LANES : (j + 2) * LANES], shifts[...])
+            before.append(v[:, :LANES])
+            after.append(v[:, LANES:])
+        return jnp.concatenate(before[:-1], axis=1), jnp.concatenate(after[1:], axis=1)
+
+    def taps(k, i, r):
         f = buf[i, r, MID]
         if k == 0:
             return buf[i, r, 0:F], f, buf[i, r, 2 * DILATION : W]
-        before, after = neighbours(f, edge[r, :], i)
+        before, after = shifted(i, r)
         return before, f, after
 
     def conv_coefs(table):
@@ -490,7 +505,7 @@
 
             def tile(r, sums):
                 c, rest = conv_coefs(chan[k, r, :])
-                before, f, after = (v.astype(F32) for v in taps(k, i, r, first_edge))
+                before, f, after = (v.astype(F32) for v in taps(k, i, r))
                 neg = wide(c[0], F) * before + wide(c[1], F) * f + wide(c[2], F) * after + wide(c[3], F)
                 a, soft = rectify(neg, wide(rest, F))
                 act2[k, i, r, :] = a.astype(BF16)
@@ -516,7 +531,7 @@
 
     def out_copy(kind, k, i):
         row = first_item + i
-        src, dst = (((x1, x0)[k], block_h), (skips, skip_h))[kind]
+        src, dst = (((x1, x0)[k], block_h), ((skips, x1)[k], skip_h))[kind]
         src = src.at[i, :, centre] if (kind, k) == (0, 1) else src.at[i]
         return (
             pltpu.make_async_copy(src, dst.at[row], sem_o.at[kind, k, i]),
@@ -539,38 +554,31 @@
             src.at[i], dst.at[o * NI + i], sem_o.at[kind, 0, i], sem_or.at[kind, i], {"section": o}
         ).wait_recv()
 
+    def projected(k, i, first, rows):
+        mean, inv = tall(stat[2 * k + 1, i, 0], rows), tall(stat[2 * k + 1, i, 1], rows)
+        r = slice(first, first + rows)
+        table = col[k, r, :]
+        shift = column(table, 0) - mean * inv * column(table, 1)
+        y = dot(wg[k, r, :], act2[k, i])
+        return (y * wide(inv, F) + wide(shift, F)) * mask_row(i, rows)
+
     def phase4(k):
-        R = ROWS4
-        x = x0 if k == 0 else x1
-        mid = MID if k == 0 else slice(0, F)
-
         def item(i):
-            if k == 0:
-                finish_norm(1, 1, i)
-            mean, inv = tall(stat[2 * k + 1, i, 0], B), tall(stat[2 * k + 1, i, 1], B)
-            m = mask_row(i, B)
-            y = pl.ds(0, 2 * B)
-            wide_s[y, 0:F] = dot(wg[k], act2[k, i])
-
-            def project(r):
-                table = col[k, r, :]
-                shift = column(table, 0) - mean * inv * column(table, 1)
-                return (wide_s[r, 0:F] * wide(inv, F) + wide(shift, F)) * m
-
-            total = (x[i, :, mid].astype(F32) + project(pl.ds(0, B))).astype(BF16)
-            if k == 0:
-                x1[i] = total
-            else:
-                x0[i, :, MID] = total
-            p = project(pl.ds(B, B))
-            if k == 1:
-                wait_out(1, 0, i)
-                p += skips[i].astype(F32)
-            skips[i] = p.astype(BF16)
-            start_out(0, k, i)
-            start_out(1, k, i)
+            finish_norm(1, 1, i)
+            x1[i] = low(x0[i, :, MID].astype(F32) + projected(0, i, 0, B))
+            start_out(0, 0, i)
 
         return item
+
+    def outputs(i):
+        skips[i] = low(projected(0, i, B, B))
+        start_out(1, 0, i)
+        both = projected(1, i, 0, 2 * B)
+        x0[i, :, MID] = low(x1[i].astype(F32) + both[:B])
+        start_out(0, 1, i)
+        wait_out(0, 0, i)
+        x1[i] = low(skips[i].astype(F32) + both[B:])
+        start_out(1, 1, i)
 
     def phase5(k):
         R = ROWS5
@@ -580,8 +588,9 @@
             if k == 1:
                 finish_norm(5, 3, i)
             mean, inv = tall(stat[2 * k + 1, i, 0], R5), tall(stat[2 * k + 1, i, 1], R5)
-            wide_s[:, 0 : 2 * B] = dot(act2[k, i], dp[i], NT)
-            total8 = dot(jnp.ones((8, F), BF16), dp[i], NT)
+            both = dot(jnp.concatenate([act2[k, i], jnp.ones((16, F), BF16)], axis=0), dp[i], NT)
+            wide_s[:, 0 : 2 * B] = both[:H]
+            total8 = both[H : H + 8]
             bias_sum[k] += total8
             total = tall(total8, R5)
 
@@ -675,54 +684,93 @@
 
         per_tile(tile, rows=R)
 
+    def first_back(k, i, r, rows, before, d, after, a, m, sums, store):
+        table = chan[k, r, :]
+        g = column(table, 2)
+        mean, inv = tall(stat[2 * k, i, 0], rows), tall(stat[2 * k, i, 1], rows)
+        scale = inv * g
+        shift = column(table, 3) - mean * scale
+        spread = lambda v: wide(low(v), a.shape[1])
+        u = (
+            spread(column(table, 4)) * after + spread(column(table, 5)) * d + spread(column(table, 6)) * before
+        ) * m
+        first = (a * spread(scale) + spread(shift)) * m
+        plain = fold(u).astype(F32)
+        normed = inv * (fold(u * a).astype(F32) - mean * plain)
+        gacc[2, r, :] += normed
+        gacc[3, r, :] += plain
+        gacc[4, r, :] += fold(after * first).astype(F32)
+        gacc[5, r, :] += fold(d * first).astype(F32)
+        gacc[6, r, :] += fold(before * first).astype(F32)
+        store(u)
+        return (sums[0] + fold_rows(g * plain), sums[1] + fold_rows(g * normed))
+
     def phase7(k):
         R = ROWS7
-        act = act1_0 if k == 0 else act1_1
-        mid = MID if k == 0 else slice(0, F)
 
         def item(i):
-            if k == 0:
-
-                @pl.when(t > 0)
-                def _():
-                    halo_copy(i, 0).wait_send()
-                    halo_copy(i, 1).wait_recv()
-
-                @pl.when(t < last)
-                def _():
-                    halo_copy(i, 1).wait_send()
-                    halo_copy(i, 0).wait_recv()
-
-            mean, inv = tall(stat[2 * k, i, 0], R), tall(stat[2 * k, i, 1], R)
             m = low(mask_row(i, R))
 
             def tile(r, sums):
-                table = chan[k, r, :]
-                g = column(table, 2)
-                scale = inv * g
-                shift = column(table, 3) - mean * scale
-                before, d, after = taps(k, i, r, conv_edge)
-                u = (
-                    wide(low(column(table, 4)), F) * after
-                    + wide(low(column(table, 5)), F) * d
-                    + wide(low(column(table, 6)), F) * before
-                ) * m
-                a = act[i, r, mid]
-                first = (a * wide(low(scale), F) + wide(low(shift), F)) * m
-                plain = fold(u).astype(F32)
-                normed = inv * (fold(u * a).astype(F32) - mean * plain)
-                gacc[2, r, :] += normed
-                gacc[3, r, :] += plain
-                gacc[4, r, :] += fold(after * first).astype(F32)
-                gacc[5, r, :] += fold(d * first).astype(F32)
-                gacc[6, r, :] += fold(before * first).astype(F32)
-                soft2[k, i, r, :] = u
-                return (sums[0] + fold_rows(g * plain), sums[1] + fold_rows(g * normed))
+                before, d, after = (low(v) for v in taps(1, i, r))
+
+                def store(u):
+                    soft2[1, i, r, :] = u
+
+                return first_back(1, i, r, R, before, d, after, act1_1[i, r, :], m, sums, store)
 
             a, b = per_tile(tile, rows=R, init=(zero8, zero8))
-            send_stats(4 * k + 3, i, a, b)
-
-        return item
+            send_stats(7, i, a, b)
+
+        def inner(i):
+            lanes = slice(2 * DILATION, F)
+            m = low(tall(mask_ref[i, :, lanes], R))
+
+            def tile(r, sums):
+                def store(u):
+                    soft2[0, i, r, DILATION : F - DILATION] = u
+
+                return first_back(
+                    0, i, r, R,
+                    buf[i, r, DILATION : F - DILATION], buf[i, r, lanes], buf[i, r, 3 * DILATION : F + DILATION],
+                    act1_0[i, r, lanes], m, sums, store,
+                )
+
+            a, b = per_tile(tile, rows=R, init=(zero8, zero8))
+            inner_sums[i, 0] = a
+            inner_sums[i, 1] = b
+
+        return item if k == 1 else inner
+
+    def phase7_ends(i):
+        R = ROWS7_ENDS
+
+        @pl.when(t > 0)
+        def _():
+            halo_copy(i, 0).wait_send()
+            halo_copy(i, 1).wait_recv()
+
+        @pl.when(t < last)
+        def _():
+            halo_copy(i, 1).wait_send()
+            halo_copy(i, 0).wait_recv()
+
+        def ends(v, at):
+            return jnp.concatenate([v(at, at + DILATION), v(at + F - DILATION, at + F)], axis=1)
+
+        m = low(tall(ends(lambda x, y: mask_ref[i, :, x:y], DILATION), R))
+
+        def tile(r, sums):
+            def store(u):
+                soft2[0, i, r, 0:DILATION] = u[:, :DILATION]
+                soft2[0, i, r, F - DILATION : F] = u[:, DILATION:]
+
+            before, d, after = (ends(lambda x, y: buf[i, r, x:y], at) for at in (0, DILATION, 2 * DILATION))
+            a = ends(lambda x, y: act1_0[i, r, x:y], DILATION)
+            return first_back(0, i, r, R, before, d, after, a, m, sums, store)
+
+        a, b = per_tile(tile, rows=R, init=(inner_sums[i, 0], inner_sums[i, 1]))
+        send_stats(3, i, a, b)
 
     def mix_copy(i):
         row = first_item + i
@@ -966,18 +1014,26 @@
             others(wait)
             came1[...] = low_total[0:last_rows].astype(F32)
 
-    def finish_block(k):
-        group = H // 4
+    group = H // 4
+
+    def pack_rows(packed, which):
+        lanes = lax.broadcasted_iota(jnp.int32, (group, LANES), 1)
+        for g in range(4):
+            for j in which:
+                total = jnp.sum(gacc[j, g * group : (g + 1) * group, :], axis=1, keepdims=True)
+                packed = jnp.where(lanes == 32 * g + j, total, packed)
+        return packed
+
+    def finish_early(k):
         lanes = lax.broadcasted_iota(jnp.int32, (group, LANES), 1)
         bias = jnp.broadcast_to(bias_sum[k, 0:1, :], (LANES, 2 * B)).T
         packed = jnp.zeros((group, LANES), F32)
-        for g in range(4):
-            for j in range(11):
-                total = jnp.sum(gacc[j, g * group : (g + 1) * group, :], axis=1, keepdims=True)
-                packed = jnp.where(lanes == 32 * g + j, total, packed)
-            if (g + 1) * group <= 2 * B:
-                packed = jnp.where(lanes == 32 * g + 11, bias[g * group : (g + 1) * group], packed)
-        grad[k, 3 * H : 3 * H + group] = packed
+        for g in range(2 * B // group):
+            packed = jnp.where(lanes == 32 * g + 11, bias[g * group : (g + 1) * group], packed)
+        grad[k, 3 * H : 3 * H + group] = pack_rows(packed, range(2, 11))
+
+    def finish_block(k):
+        grad[k, 3 * H : 3 * H + group] = pack_rows(grad[k, 3 * H : 3 * H + group], (0, 1))
 
     def mask_gradients(i):
         m = mask_row(i, R)
@@ -1012,6 +1068,9 @@
             return c
 
         lax.fori_loop(0, count, step, 0)
+
+    def at_item(j, body, *args):
+        return lambda i: pl.when(i == j)(lambda: body(*args))
 
     def send_x1_edges(i):
         @pl.when(i == NI - 1)
@@ -1032,6 +1091,7 @@
     send_edges(0, 2 * B)
     per_item(phase2(1))
     edge2()
+    place_halos(first_edge)
     per_item(phase3(1))
     edge3()
     recv_edges(0, 2 * B, dp_edge)
@@ -1041,9 +1101,11 @@
     sum_1(0, 1)
     per_item(phase6(1))
     edge6()
+    place_halos(conv_edge)
     sum_2(0, 1)
     wait_weights(5)
     per_item(phase7(1))
+    finish_early(1)
     per_item(phase8(1))
     sum_3(0, 1)
     finish_block(1)
@@ -1053,32 +1115,30 @@
     sum_1(0, 0)
     sum_4(0, 1)
     sum_2(1, 1)
-    per_item(phase6(0))
+    steps(NI, (0, at_item(2, sum_2, 0, 0)), (0, phase6(0)))
     sum_5(0, 1)
-    sum_2(0, 0)
     sum_3(1, 1)
-    per_item(phase7(0))
-    per_item(phase8(0))
+    steps(NI, (0, at_item(2, sum_3, 0, 0)), (0, phase7(0)))
+    per_item(phase7_ends)
+    sum_4(1, 1)
+    finish_early(0)
+    steps(NI, (0, at_item(1, sum_4, 0, 0)), (0, phase8(0)))
     finish_block(0)
     last_1()
-    sum_3(0, 0)
-    sum_4(1, 1)
-    per_item(phase4(1))
-    sum_4(0, 0)
+    sum_5(0, 0)
     sum_5(1, 1)
-    per_item(lambda i: input_gradient(0, i))
-    last_2()
-    sum_5(0, 0)
+    steps(NI, (0, at_item(3, last_2)), (0, outputs))
+    sum_6(0, 0)
     sum_6(0, 1)
     sum_6(1, 1)
-    last_3()
-    sum_6(0, 0)
     results = [
         pltpu.make_async_copy(came[part], grad_h.at[pl.ds(a, b - a)], sem_f.at[part])
         for part, (a, b) in enumerate(rows_at_part)
     ]
-    for copy in results:
-        copy.start()
+    results[0].start()
+    per_item(lambda i: input_gradient(0, i))
+    last_3()
+    results[1].start()
     for copy in results:
         copy.wait()
 
@@ -1089,7 +1149,7 @@
         remote(
             stage.at[2 * i], gmix_h.at[o * NI + i], sem_m.at[1, i], sem_mr.at[i], {"section": o}
         ).wait_recv()
-        for kind, k in ((0, 0), (0, 1), (1, 1)):
+        for kind, k in ((1, 0), (0, 1), (1, 1)):
             wait_out(kind, k, i)
         wait_came(0, i)
         wait_came(1, i)
@@ -1117,7 +1177,6 @@
     low_owners = -(-rows1 // low_chunk)
     smem = pl.BlockSpec(memory_space=pltpu.SMEM)
     any_spec = pl.BlockSpec(memory_space=pl.ANY)
-    vmem = pl.BlockSpec(memory_space=pltpu.VMEM)
     dma = pltpu.SemaphoreType.DMA
     shape = jax.ShapeDtypeStruct
     outs = (
@@ -1160,10 +1219,16 @@
         pltpu.VMEM((NI, 8, W), F32),
         pltpu.VMEM((8, LANES), F32),
         pltpu.VMEM((NI, 8, LANES), F32),
+        pltpu.VMEM((NI, 2, 8, LANES), F32),
         pltpu.VMEM((4, NI, 2, 8, LANES), F32),
         pltpu.VMEM((NI, 2, 8, LANES), F32),
         pltpu.VMEM((2, NI, 8, LANES), F32),
         pltpu.VMEM((2, NI, n_tm - 1, 8, LANES), F32),
+        pltpu.VMEM((2 * LANES, 2 * LANES), BF16),
+        pltpu.VMEM(w_in.shape, BF16),
+        pltpu.VMEM(chan.shape, F32),
+        pltpu.VMEM(w_out.shape, BF16),
+        pltpu.VMEM(b_out.shape, F32),
         pltpu.VMEM((2, 3, 2 * B, LANES), BF16),
         pltpu.VMEM((2, 2, 2 * B, LANES), BF16),
         pltpu.VMEM((B, LANES), BF16),
@@ -1172,7 +1237,7 @@
         pltpu.VMEM((H, LANES), BF16),
         pltpu.VMEM((H, LANES), BF16),
         pltpu.VMEM((H, LANES), BF16),
-        dma((n_src,)),
+        dma((n_src + 4,)),
         dma((6, 2)),
         dma((6,)),
         dma((5,)),
@@ -1206,7 +1271,7 @@
     return pl.pallas_call(
         functools.partial(kernel, (n_tm, n_item, NI, H, B, F)),
         out_shape=outs,
-        in_specs=[any_spec] * 3 + [vmem] * 4 + [smem] * 2,
+        in_specs=[any_spec] * 7 + [smem] * 2,
         out_specs=[any_spec] * len(outs),
         scratch_shapes=scratch,
         compiler_params=pltpu.CompilerParams(

time: 124 us -> 118 us (0.952)
  Pallas kernels: 123 us -> 117 us
    pallas_call x1, Pallas kernels: 116 us -> 110 us  [run(): pl.pallas_call(functools.partial(kernel, (n_tm, n_item, NI, H, B, F)), ou...]
where the time goes in v5:
time: 118 us
  Pallas kernels  117 us (99%)
    pallas_call x1, Pallas kernels, run(): pl.pallas_call(functools.partial(kernel, (n_tm, n_item, NI, H, B, F)), ou...  110 us
    pallas_call x1, Pallas kernels, close(): pl.pallas_call(close_kernel, out_shape=(shape(block.shape, BF16), shape(s...  7.03 us

profile of v5, /device:TPU:0, one launch (start us, length us, event | category | flops | bytes accessed | tf_op | source)
XLA Modules:
  0.0 118.0 jit_solution(4251259419276016535)
XLA Ops:
  0.6 110.1 %temporal_blocks.1 = (bf16[8,128,1024]{2,1,0:T(8,128)(2,1)}, bf16[8,128,1024]{2,1,0:T(8,128)(2,1)}, bf16[8,64,1024]{2,1,0:T(8,128)(2,1)}, f32[1664,128]{1,0:T(8,128)}) custom-call(bf16[3,512,1024]{2,1,0:T(8,128)(2,1)} %bitcast.9, bf16[8,128,1024]{2,1,0:T(8,128)(2,1)} %gout_h.1, bf16[8,128,1024]{2,1,0:T(8,128)(2,1)} %gskip_h.1, bf16[512,128]{1,0:T(8,128)(2,1)} %bitcast.11, ...), custom_call_target="tpu_custom_call" | custom-call | tf_op jit(solution)/shard_map/temporal_blocks/pallas_call | solution.py:1271
  110.8 7.0 %lay_out.1 = (bf16[8,128,1024]{2,1,0:T(8,128)(2,1)}, bf16[8,128,1024]{2,1,0:T(8,128)(2,1)}, f32[3,8,64,1024]{3,2,1,0:T(8,128)}, f32[512,128]{1,0:T(8,128)}, f32[...) custom-call(bf16[8,128,1024]{2,1,0:T(8,128)(2,1)} %get-tuple-element.18.block_in, ...), custom_call_target="tpu_custom_call" | custom-call | tf_op jit(solution)/shard_map/lay_out/pallas_call | solution.py:1356

commit v6 on v5

--- a/solution.py
+++ b/solution.py
@@ -56,8 +56,8 @@
     return parts[0]
 
 
-def fold_rows(v):
-    parts = [v[at : at + 8] for at in range(0, v.shape[0], 8)]
+def fold_rows(v, count=8):
+    parts = [v[at : at + count] for at in range(0, v.shape[0], count)]
     while len(parts) > 1:
         parts = [a + b for a, b in zip(parts[::2], parts[1::2])] + parts[len(parts) & ~1 :]
     return parts[0]
@@ -140,22 +140,103 @@
     for copy in small:
         copy.wait()
 
-    w_in = w_in_ref[...]
-    w_out = w_out_ref[...].astype(F32)
-    wpre[s] = w_in
-    win[s] = w_in.astype(F32).T.astype(BF16)
-    wout[s] = w_out.T.astype(BF16)
-    gained = (w_out * chan_ref[9]).astype(BF16)
-    wg[s] = gained
+    wpre[s] = w_in_ref[...]
     wide_s[0:LANES, 0:H] = jnp.zeros((LANES, H), F32)
     for j in range(chan_ref.shape[0]):
         wide_s[j : j + 1, 0:H] = chan_ref[j]
     chan[s] = wide_s[0:LANES, 0:H].T
+    weights = (wpre, chan, wg, col, wout, win)
+
+    def weight_copies(j):
+        ref = weights[j]
+        return (
+            remote(ref.at[s], ref.at[s], sem_w.at[j, 0], sem_w.at[j, 1], {"section": o}),
+            remote(ref.at[o], ref.at[o], sem_w.at[j, 0], sem_w.at[j, 1], {"section": o}),
+        )
+
+    def wait_weights(*which):
+        for j in which:
+            send, recv = weight_copies(j)
+            recv.wait_recv()
+            send.wait_send()
+
+    pl.semaphore_wait(barrier, 2 * members - 1)
+    for j in (0, 1):
+        weight_copies(j)[0].start()
+
+    for n in range(n_src):
+        load_source(n).wait()
+
+    def mix_item(i, c):
+        rows = pl.ds(pl.multiple_of(i * half, half), half)
+        where = lax.broadcasted_iota(jnp.int32, (8, F), 1) + t * F
+        m = tall(jnp.where(where < lengths[i], 1.0, 0.0), half)
+        total = jnp.zeros((half, F), F32)
+        for n in range(n_src):
+            total += soft2[1, n, rows, :].astype(F32) * jnp.where(n < counts[i], 1.0, 0.0)
+        stage[i] = (total * m).astype(BF16)
+        return c
+
+    lax.fori_loop(o * NI, o * NI + NI, mix_item, 0)
+
+    own_rows = pl.ds(pl.multiple_of(s * half, half), half)
+    other_rows = pl.ds(pl.multiple_of(o * half, half), half)
+    items_of = lambda core: pl.ds(core * NI, NI)
+    centre = pl.ds(DILATION, F)
+    head, tail = pl.ds(0, DILATION), pl.ds(F + DILATION, DILATION)
+
+    main_local = pltpu.make_async_copy(stage.at[items_of(s)], x0.at[:, own_rows, centre], sem_x.at[0])
+    main_send = remote(
+        stage.at[items_of(o)], x0.at[:, own_rows, centre], sem_x.at[1], sem_xr.at[0], {"section": o}
+    )
+    main_recv = remote(
+        stage.at[items_of(o)], x0.at[:, other_rows, centre], sem_x.at[1], sem_xr.at[0], {"section": o}
+    )
+
+    def halo_send(side, core):
+        edge = pl.ds(0, DILATION) if side == 0 else pl.ds(F - DILATION, DILATION)
+        place = tail if side == 0 else head
+        return remote(
+            stage.at[items_of(core), :, edge],
+            x0.at[:, own_rows, place],
+            sem_x.at[2 + 2 * side + core],
+            sem_xr.at[1 + 2 * side + s],
+            {"section": core, "tm": left if side == 0 else right},
+        )
+
+    def halo_recv(side, core):
+        place = tail if side == 0 else head
+        rows = pl.ds(core * half, half)
+        return remote(
+            x0.at[:, rows, place], x0.at[:, rows, place], sem_x.at[0], sem_xr.at[1 + 2 * side + core], {"section": o}
+        )
+
+    def send_halos(core):
+        pl.when(t > 0)(lambda: halo_send(0, core).start())
+        pl.when(t < last)(lambda: halo_send(1, core).start())
+
+    main_send.start()
+    send_halos(o)
+    lax.fori_loop(s * NI, s * NI + NI, mix_item, 0)
+    main_local.start()
+    send_halos(s)
+    load_out = pltpu.make_async_copy(gout_h.at[pl.ds(first_item, NI)], dp.at[:, pl.ds(0, B)], sem_g.at[0])
+    load_skip = pltpu.make_async_copy(gskip_h.at[pl.ds(first_item, NI)], dp.at[:, pl.ds(B, B)], sem_g.at[1])
+    load_out.start()
+    load_skip.start()
+
+    w_out = w_out_ref[...].astype(F32)
+    win[s] = w_in_ref[...].astype(F32).T.astype(BF16)
+    wout[s] = w_out.T.astype(BF16)
+    gained = (w_out * chan_ref[9]).astype(BF16)
+    wg[s] = gained
     bias = jnp.broadcast_to(b_out_ref[...], (LANES, 2 * B)).T
     bias += jnp.sum(w_out * chan_ref[10], axis=1, keepdims=True)
     gain = jnp.sum(gained.astype(F32), axis=1, keepdims=True)
     lane_w = lax.broadcasted_iota(jnp.int32, (2 * B, LANES), 1)
     col[s] = jnp.where(lane_w == 0, bias, gain)
+    for j in range(2, len(weights)):
+        weight_copies(j)[0].start()
 
     for i in range(NI):
         length = lengths[first_item + i]
@@ -170,86 +251,6 @@
     held = (within < 3) | ((within >= 16) & (within < 19))
     edge_mask_ref[...] = jnp.where(held & (frame >= 0) & (frame < length), 1.0, 0.0)
 
-    for n in range(n_src):
-        load_source(n).wait()
-
-    def mix_item(i, c):
-        rows = pl.ds(pl.multiple_of(i * half, half), half)
-        where = lax.broadcasted_iota(jnp.int32, (8, F), 1) + t * F
-        m = tall(jnp.where(where < lengths[i], 1.0, 0.0), half)
-        total = jnp.zeros((half, F), F32)
-        for n in range(n_src):
-            total += soft2[1, n, rows, :].astype(F32) * jnp.where(n < counts[i], 1.0, 0.0)
-        stage[i] = (total * m).astype(BF16)
-        return c
-
-    lax.fori_loop(o * NI, o * NI + NI, mix_item, 0)
-    pl.semaphore_wait(barrier, 2 * members - 1)
-
-    own_rows = pl.ds(pl.multiple_of(s * half, half), half)
-    other_rows = pl.ds(pl.multiple_of(o * half, half), half)
-    items_of = lambda core: pl.ds(core * NI, NI)
-    centre = pl.ds(DILATION, F)
-    head, tail = pl.ds(0, DILATION), pl.ds(F + DILATION, DILATION)
-
-    main_local = pltpu.make_async_copy(stage.at[items_of(s)], x0.at[:, own_rows, centre], sem_x.at[0])
-    main_send = remote(
-        stage.at[items_of(o)], x0.at[:, own_rows, centre], sem_x.at[1], sem_xr.at[0], {"section": o}
-    )
-    main_recv = remote(
-        stage.at[items_of(o)], x0.at[:, other_rows, centre], sem_x.at[1], sem_xr.at[0], {"section": o}
-    )
-
-    def halo_send(side, core):
-        edge = pl.ds(0, DILATION) if side == 0 else pl.ds(F - DILATION, DILATION)
-        place = tail if side == 0 else head
-        return remote(
-            stage.at[items_of(core), :, edge],
-            x0.at[:, own_rows, place],
-            sem_x.at[2 + 2 * side + core],
-            sem_xr.at[1 + 2 * side + s],
-            {"section": core, "tm": left if side == 0 else right},
-        )
-
-    def halo_recv(side, core):
-        place = tail if side == 0 else head
-        rows = pl.ds(core * half, half)
-        return remote(
-            x0.at[:, rows, place], x0.at[:, rows, place], sem_x.at[0], sem_xr.at[1 + 2 * side + core], {"section": o}
-        )
-
-    def send_halos(core):
-        pl.when(t > 0)(lambda: halo_send(0, core).start())
-        pl.when(t < last)(lambda: halo_send(1, core).start())
-
-    main_send.start()
-    send_halos(o)
-    lax.fori_loop(s * NI, s * NI + NI, mix_item, 0)
-    main_local.start()
-    send_halos(s)
-    load_out = pltpu.make_async_copy(gout_h.at[pl.ds(first_item, NI)], dp.at[:, pl.ds(0, B)], sem_g.at[0])
-    load_skip = pltpu.make_async_copy(gskip_h.at[pl.ds(first_item, NI)], dp.at[:, pl.ds(B, B)], sem_g.at[1])
-    load_out.start()
-    load_skip.start()
-
-    weights = (wpre, chan, wg, col, wout, win)
-
-    def weight_copies(j):
-        ref = weights[j]
-        return (
-            remote(ref.at[s], ref.at[s], sem_w.at[j, 0], sem_w.at[j, 1], {"section": o}),
-            remote(ref.at[o], ref.at[o], sem_w.at[j, 0], sem_w.at[j, 1], {"section": o}),
-        )
-
-    for j in range(len(weights)):
-        weight_copies(j)[0].start()
-
-    def wait_weights(*which):
-        for j in which:
-            send, recv = weight_copies(j)
-            recv.wait_recv()
-            send.wait_send()
-
     @pl.when(t == 0)
     def _():
         x0[:, :, 0:DILATION] = jnp.zeros((NI, B, DILATION), BF16)
@@ -260,6 +261,13 @@
 
     grad[...] = jnp.zeros(grad.shape, F32)
     bias_sum[...] = jnp.zeros(bias_sum.shape, F32)
+
+    def each(count, body, first=1):
+        if count <= 8:
+            for d in range(first, count):
+                body(d)
+        else:
+            lax.fori_loop(first, count, lambda d, c: (body(d), c)[1], 0)
 
     def stat_copy(ph, i, d, to):
         p = ph % 2
@@ -271,11 +279,7 @@
         rows = [jnp.sum(a, axis=0, keepdims=True), jnp.sum(b, axis=0, keepdims=True)]
         st_src[ph % 2, i] = jnp.concatenate(rows + [jnp.zeros((6, LANES), F32)], axis=0)
 
-        def one(d, c):
-            stat_copy(ph, i, d, lax.rem(t + d, n_tm)).start()
-            return c
-
-        lax.fori_loop(1, n_tm, one, 0)
+        each(n_tm, lambda d: stat_copy(ph, i, d, lax.rem(t + d, n_tm)).start())
 
     def recv_stats(ph, i):
         def one(d, total):
@@ -284,7 +288,12 @@
             copy.wait_recv()
             return total + st_buf[ph % 2, i, d - 1]
 
-        total = lax.fori_loop(1, n_tm, one, st_src[ph % 2, i])
+        total = st_src[ph % 2, i]
+        if n_tm <= 8:
+            for d in range(1, n_tm):
+                total = one(d, total)
+        else:
+            total = lax.fori_loop(1, n_tm, one, total)
         sums = jnp.sum(total, axis=1, keepdims=True)
         return (
             jnp.broadcast_to(sums[0:1], (8, LANES)),
@@ -306,6 +315,10 @@
         q = b * inv_n * inv
         back[i, 0] = (mean * q - a * inv_n) * (inv * LOG2E)
         back[i, 1] = -q * (inv * LOG2E)
+
+    def correction(i, rows):
+        m = mask_ref[i, :, MID]
+        return [tall(m * wide(back[i, j], F), rows) for j in (0, 1)]
 
     def lanes_of(ref, j):
         out = ref[0, j]
@@ -391,7 +404,7 @@
         return rest * soft - neg, soft
 
     def add_sums(a, sums):
-        return (sums[0] + fold_rows(a), sums[1] + fold_rows(a * a))
+        return tuple(x + fold_rows(fold_rows(v, 16).astype(F32)) for x, v in zip(sums, (a, a * a)))
 
     def send_sums(ph, i, sums):
         m = mask_ref[i, :, MID]
@@ -412,7 +425,8 @@
                 rest = 1.0 - column(table, 1)
                 neg = dot(wpre[k, r, :], x[i]) * -LOG2E + wide(bias, width)
                 a, soft = rectify(neg, wide(rest, width))
-                act[i, r, :] = a.astype(BF16)
+                a = low(a)
+                act[i, r, :] = a
                 soft1[k, i, r, :] = soft[:, mid].astype(BF16)
                 return add_sums(a[:, mid], sums)
 
@@ -443,16 +457,14 @@
         def item(i):
             finish_norm(4 * k, 2 * k, i)
             mean, inv = tall(stat[2 * k, i, 0], R), tall(stat[2 * k, i, 1], R)
-            m = mask_row(i, R, at, width)
+            m = low(mask_row(i, R, at, width))
 
             def tile(r, c):
                 table = chan[k, r, :]
                 scale = inv * column(table, 2)
                 shift = column(table, 3) - mean * scale
                 a = act[i, r, :].astype(F32)
-                buf[i, r, at : at + width] = (
-                    (a * wide(scale, width) + wide(shift, width)) * m
-                ).astype(BF16)
+                buf[i, r, at : at + width] = low(a * wide(scale, width) + wide(shift, width)) * m
                 return c
 
             per_tile(tile, rows=R)
@@ -474,12 +486,9 @@
         per_tile(tile, rows=R)
 
     def place_halos(edge):
-        def item(i):
-            wide_edge = edge[...].astype(F32)
-            buf[i, :, 0:DILATION] = low(pltpu.roll(wide_edge, lax.rem(254 - 32 * i, 128), 1))
-            buf[i, :, F + DILATION : W] = low(pltpu.roll(wide_edge, lax.rem(239 - 32 * i, 128), 1))
-
-        per_item(item)
+        for i in range(NI):
+            buf[i, :, 0:DILATION] = pltpu.roll(edge[...], (254 - 32 * i) % 128, 1)
+            buf[i, :, F + DILATION : W] = pltpu.roll(edge[...], (239 - 32 * i) % 128, 1)
 
     def shifted(i, r):
         before, after = [], []
@@ -508,7 +517,8 @@
                 before, f, after = (v.astype(F32) for v in taps(k, i, r))
                 neg = wide(c[0], F) * before + wide(c[1], F) * f + wide(c[2], F) * after + wide(c[3], F)
                 a, soft = rectify(neg, wide(rest, F))
-                act2[k, i, r, :] = a.astype(BF16)
+                a = low(a)
+                act2[k, i, r, :] = a
                 soft2[k, i, r, :] = soft.astype(BF16)
                 return add_sums(a, sums)
 
@@ -631,14 +641,13 @@
         def item(i):
             finish_back(4 * k + 2, 2 * k + 1, i)
             inv = tall(stat[2 * k + 1, i, 1], R) * LOG2E
-            p, q = wide(tall(back[i, 0], R), F), wide(tall(back[i, 1], R), F)
-            m = mask_row(i, R)
+            p, q = correction(i, R)
 
             def tile(r, c):
                 table = chan[k, r, :]
                 slope = column(table, 8)
                 g = inv * column(table, 9)
-                d_act = low(dot(wout[k, r, :], dp[i]) * wide(g, F) + m * (p + q * act2[k, i, r, :].astype(F32)))
+                d_act = low(dot(wout[k, r, :], dp[i]) * wide(g, F) + (p + q * act2[k, i, r, :].astype(F32)))
                 soft = soft2[k, i, r, :]
                 d_conv = d_act * (wide(low(slope), F) + wide(low(1.0 - slope), F) * jnp.exp2(-soft))
                 gacc[8, r, :] += fold(d_act * soft).astype(F32) * -LN2
@@ -788,14 +797,13 @@
         def item(i):
             finish_back(4 * k + 3, 2 * k, i)
             inv = tall(stat[2 * k, i, 1], R) * LOG2E
-            p, q = wide(tall(back[i, 0], R), F), wide(tall(back[i, 1], R), F)
-            m = mask_row(i, R)
+            p, q = correction(i, R)
 
             def tile(r, c):
                 table = chan[k, r, :]
                 slope = column(table, 1)
                 g = inv * column(table, 2)
-                d_act = low(soft2[k, i, r, :].astype(F32) * wide(g, F) + m * (p + q * act[i, r, mid].astype(F32)))
+                d_act = low(soft2[k, i, r, :].astype(F32) * wide(g, F) + (p + q * act[i, r, mid].astype(F32)))
                 soft = soft1[k, i, r, :]
                 d_pre = d_act * (wide(low(slope), F) + wide(low(1.0 - slope), F) * jnp.exp2(-soft))
                 gacc[1, r, :] += fold(d_act * soft).astype(F32) * -LN2
@@ -812,9 +820,8 @@
         return item
 
     def input_gradient(k, i):
-        wide_s[0:B, 0:F] = dot(win[k], buf[i, :, MID])
         m = mask_row(i, B)
-        d_input = (wide_s[0:B, 0:F] + dp[i, 0:B, :].astype(F32)) * m
+        d_input = (dot(win[k], buf[i, :, MID]) + dp[i, 0:B, :].astype(F32)) * m
         if k == 1:
             dp[i, 0:B, :] = d_input.astype(BF16)
         else:
@@ -837,9 +844,6 @@
 
     def tm_peer(d):
         return lax.rem(t + d, n_tm)
-
-    def each(count, body):
-        lax.fori_loop(1, count, lambda d, c: (body(d), c)[1], 0)
 
     def at_part(part, k, start, rows):
         return grad.at[k, pl.ds(rows_at_part[part][0] + start, rows)]
@@ -1196,7 +1200,7 @@
         pltpu.VMEM((2, NI, H, F), BF16),
         pltpu.VMEM((2, NI, H, F), BF16),
         pltpu.VMEM((NI, H, W), BF16),
-        pltpu.VMEM((H, W), F32),
+        pltpu.VMEM((H, H), F32),
         pltpu.VMEM((NI, 2 * B, F), BF16),
         pltpu.VMEM((11, H, LANES), F32),
         pltpu.VMEM((2, H, B), BF16),
@@ -1289,15 +1293,19 @@
     items = gmix_in.shape[0]
     H, B = w_in_h.shape
     n_src = sources_h.shape[0]
-    plain = [(j, i) for i in range(items) for j in (0, 1)]
+    part = items // 2
+    plain = [(j, i) for i in (0, 1) for j in (0, 1)]
+
+    def some(i):
+        return pl.ds(i * part, part)
 
     def fetch(j, i):
-        return pltpu.make_async_copy((block_in, skip_in)[j].at[i], held.at[j, i], sem_a.at[j, i])
+        return pltpu.make_async_copy((block_in, skip_in)[j].at[some(i)], held.at[j, some(i)], sem_a.at[j, i])
 
     def store(j, i):
-        return pltpu.make_async_copy(held.at[j, i], (block_h, skip_h)[j].at[i], sem_b.at[j, i])
-
-    loads = [pltpu.make_async_copy(gmix_in.at[i], mixed.at[i], sem_g.at[i]) for i in range(items)]
+        return pltpu.make_async_copy(held.at[j, some(i)], (block_h, skip_h)[j].at[some(i)], sem_b.at[j, i])
+
+    loads = [pltpu.make_async_copy(gmix_in.at[some(i)], mixed.at[some(i)], sem_g.at[i]) for i in (0, 1)]
     load_sums = pltpu.make_async_copy(grad_in, sums, sem_w.at[0])
     for copy in loads:
         copy.start()
@@ -1306,7 +1314,8 @@
         fetch(j, i).start()
     nothing[...] = jnp.zeros(nothing.shape, F32)
     for i in range(items):
-        loads[i].wait()
+        if i % part == 0:
+            loads[i // part].wait()
         full[i] = mixed[i].astype(F32)
         for n in range(n_src):
 
@@ -1375,9 +1384,9 @@
             pltpu.VMEM((2 * B, H), F32),
             pltpu.VMEM((n_rows, 1, H), F32),
             pltpu.VMEM((1, 2 * B), F32),
-            dma((2, items)),
-            dma((2, items)),
-            dma((items,)),
+            dma((2, 2)),
+            dma((2, 2)),
+            dma((2,)),
             dma((n_src, items)),
             dma((5,)),
         ],

time: 118 us -> 116 us (0.983)
  Pallas kernels: 117 us -> 115 us
    pallas_call x1, Pallas kernels: 110 us -> 108 us  [run(): pl.pallas_call(functools.partial(kernel, (n_tm, n_item, NI, H, B, F)), ou...]
where the time goes in v6:
time: 116 us
  Pallas kernels  115 us (99%)
    pallas_call x1, Pallas kernels, run(): pl.pallas_call(functools.partial(kernel, (n_tm, n_item, NI, H, B, F)), ou...  108 us
    pallas_call x1, Pallas kernels, close(): pl.pallas_call(close_kernel, out_shape=(shape(block.shape, BF16), shape(s...  6.89 us

profile of v6, /device:TPU:0, one launch (start us, length us, event | category | flops | bytes accessed | tf_op | source)
XLA Modules:
  0.0 115.6 jit_solution(14483221411555956597)
XLA Ops:
  0.6 107.9 %temporal_blocks.1 = (bf16[8,128,1024]{2,1,0:T(8,128)(2,1)}, bf16[8,128,1024]{2,1,0:T(8,128)(2,1)}, bf16[8,64,1024]{2,1,0:T(8,128)(2,1)}, f32[1664,128]{1,0:T(8,128)}) custom-call(bf16[3,512,1024]{2,1,0:T(8,128)(2,1)} %bitcast.9, bf16[8,128,1024]{2,1,0:T(8,128)(2,1)} %gout_h.1, bf16[8,128,1024]{2,1,0:T(8,128)(2,1)} %gskip_h.1, bf16[512,128]{1,0:T(8,128)(2,1)} %bitcast.11, ...), custom_call_target="tpu_custom_call" | custom-call | tf_op jit(solution)/shard_map/temporal_blocks/pallas_call | solution.py:1275
  108.5 6.9 %lay_out.1 = (bf16[8,128,1024]{2,1,0:T(8,128)(2,1)}, bf16[8,128,1024]{2,1,0:T(8,128)(2,1)}, f32[3,8,64,1024]{3,2,1,0:T(8,128)}, f32[512,128]{1,0:T(8,128)}, f32[...) custom-call(bf16[8,128,1024]{2,1,0:T(8,128)(2,1)} %get-tuple-element.18.block_in, ...), custom_call_target="tpu_custom_call" | custom-call | tf_op jit(solution)/shard_map/lay_out/pallas_call | solution.py:1365

commit v7 on v6

--- a/solution.py
+++ b/solution.py
@@ -13,11 +13,11 @@
 ROWS = 128
 ROWS1 = 512
 ROWS2 = 512
-ROWS3 = 256
+ROWS3 = 512
 ROWS4 = 128
 ROWS5 = 512
 ROWS6 = 512
-ROWS7 = 256
+ROWS7 = 512
 ROWS7_ENDS = 512
 ROWS8 = 512
 EPSILON = 1e-05
@@ -1086,13 +1086,14 @@
     p2, p3 = phase2(0), phase3(0)
     per_item(lambda i: (p2(i), p3(i)))
     wait_weights(2, 3)
-    steps(NI + 2, (0, phase4(0)), (0, send_x1_edges), (2, phase1(1)))
-    edge1()
+    steps(NI + 1, (0, phase4(0)), (0, send_x1_edges), (1, phase1(1)))
     load_out.wait()
     load_skip.wait()
     per_item(mask_gradients)
     pack_edges(dp, 2 * B, 0)
     send_edges(0, 2 * B)
+    edge1()
+    gacc[...] = jnp.zeros(gacc.shape, F32)
     per_item(phase2(1))
     edge2()
     place_halos(first_edge)
@@ -1100,7 +1101,6 @@
     edge3()
     recv_edges(0, 2 * B, dp_edge)
     wait_weights(4)
-    gacc[...] = jnp.zeros(gacc.shape, F32)
     per_item(phase5(1))
     sum_1(0, 1)
     per_item(phase6(1))
@@ -1132,15 +1132,15 @@
     sum_5(0, 0)
     sum_5(1, 1)
     steps(NI, (0, at_item(3, last_2)), (0, outputs))
-    sum_6(0, 0)
     sum_6(0, 1)
     sum_6(1, 1)
     results = [
         pltpu.make_async_copy(came[part], grad_h.at[pl.ds(a, b - a)], sem_f.at[part])
         for part, (a, b) in enumerate(rows_at_part)
     ]
+    per_item(lambda i: input_gradient(0, i))
+    sum_6(0, 0)
     results[0].start()
-    per_item(lambda i: input_gradient(0, i))
     last_3()
     results[1].start()
     for copy in results:

time: 116 us -> 114 us (0.983)
  Pallas kernels: 115 us -> 113 us
    pallas_call x1, Pallas kernels: 108 us -> 106 us  [run(): pl.pallas_call(functools.partial(kernel, (n_tm, n_item, NI, H, B, F)), ou...]
where the time goes in v7:
time: 114 us
  Pallas kernels  113 us (99%)
    pallas_call x1, Pallas kernels, run(): pl.pallas_call(functools.partial(kernel, (n_tm, n_item, NI, H, B, F)), ou...  106 us
    pallas_call x1, Pallas kernels, close(): pl.pallas_call(close_kernel, out_shape=(shape(block.shape, BF16), shape(s...  6.89 us

profile of v7, /device:TPU:0, one launch (start us, length us, event | category | flops | bytes accessed | tf_op | source)
XLA Modules:
  0.0 114.0 jit_solution(3472811268701171816)
XLA Ops:
  0.6 106.3 %temporal_blocks.1 = (bf16[8,128,1024]{2,1,0:T(8,128)(2,1)}, bf16[8,128,1024]{2,1,0:T(8,128)(2,1)}, bf16[8,64,1024]{2,1,0:T(8,128)(2,1)}, f32[1664,128]{1,0:T(8,128)}) custom-call(bf16[3,512,1024]{2,1,0:T(8,128)(2,1)} %bitcast.9, bf16[8,128,1024]{2,1,0:T(8,128)(2,1)} %gout_h.1, bf16[8,128,1024]{2,1,0:T(8,128)(2,1)} %gskip_h.1, bf16[512,128]{1,0:T(8,128)(2,1)} %bitcast.11, ...), custom_call_target="tpu_custom_call" | custom-call | tf_op jit(solution)/shard_map/temporal_blocks/pallas_call | solution.py:1275
  107.0 6.9 %lay_out.1 = (bf16[8,128,1024]{2,1,0:T(8,128)(2,1)}, bf16[8,128,1024]{2,1,0:T(8,128)(2,1)}, f32[3,8,64,1024]{3,2,1,0:T(8,128)}, f32[512,128]{1,0:T(8,128)}, f32[...) custom-call(bf16[8,128,1024]{2,1,0:T(8,128)(2,1)} %get-tuple-element.18.block_in, ...), custom_call_target="tpu_custom_call" | custom-call | tf_op jit(solution)/shard_map/lay_out/pallas_call | solution.py:1365

commit v8 on v7

--- a/solution.py
+++ b/solution.py
@@ -963,7 +963,11 @@
         return remote(rows, rows, sem_gs.at[d], sem_gr.at[d], member_at(d)[1])
 
     def others(body, start=1):
-        lax.fori_loop(start, members, lambda d, c: (body(d), c)[1], 0)
+        if members <= 16:
+            for d in range(start, members):
+                body(d)
+        else:
+            lax.fori_loop(start, members, lambda d, c: (body(d), c)[1], 0)
 
     def last_1():
         low_grad[0:last_rows] = low(grad[0, 2 * H :])

time: 114 us -> 114 us (level)
  no operation moved by 1% of the time
where the time goes in v8:
time: 114 us; the launch traced here: 113 us
  Pallas kernels  113 us (99%)
    pallas_call x1, Pallas kernels, run(): pl.pallas_call(functools.partial(kernel, (n_tm, n_item, NI, H, B, F)), ou...  106 us
    pallas_call x1, Pallas kernels, close(): pl.pallas_call(close_kernel, out_shape=(shape(block.shape, BF16), shape(s...  6.89 us

profile of v8, /device:TPU:0, one launch (start us, length us, event | category | flops | bytes accessed | tf_op | source)
XLA Modules:
  0.0 113.5 jit_solution(7137030997515471059)
XLA Ops:
  0.6 105.8 %temporal_blocks.1 = (bf16[8,128,1024]{2,1,0:T(8,128)(2,1)}, bf16[8,128,1024]{2,1,0:T(8,128)(2,1)}, bf16[8,64,1024]{2,1,0:T(8,128)(2,1)}, f32[1664,128]{1,0:T(8,128)}) custom-call(bf16[3,512,1024]{2,1,0:T(8,128)(2,1)} %bitcast.9, bf16[8,128,1024]{2,1,0:T(8,128)(2,1)} %gout_h.1, bf16[8,128,1024]{2,1,0:T(8,128)(2,1)} %gskip_h.1, bf16[512,128]{1,0:T(8,128)(2,1)} %bitcast.11, ...), custom_call_target="tpu_custom_call" | custom-call | tf_op jit(solution)/shard_map/temporal_blocks/pallas_call | solution.py:1279
  106.4 6.9 %lay_out.1 = (bf16[8,128,1024]{2,1,0:T(8,128)(2,1)}, bf16[8,128,1024]{2,1,0:T(8,128)(2,1)}, f32[3,8,64,1024]{3,2,1,0:T(8,128)}, f32[512,128]{1,0:T(8,128)}, f32[...) custom-call(bf16[8,128,1024]{2,1,0:T(8,128)(2,1)} %get-tuple-element.18.block_in, ...), custom_call_target="tpu_custom_call" | custom-call | tf_op jit(solution)/shard_map/lay_out/pallas_call | solution.py:1369
